TPU v7x, 32 devices: a whole 2x2x4 slice. The times are simulated.
32 devices in a mesh: grp: 2 (over x), cell: 16 (over z, y, core).
Axes of the slice: x: 2, y: 2, z: 4, core: 2. Of those that a mesh axis runs over, the one named last changes fastest.
Arguments:
- features: float32 [8192, 256], P(('grp', 'cell')), parts along dimension 0, may hold values from -6 to 6
- counts: int32 [32], P(('grp', 'cell')), parts along dimension 0, may hold values from 1 to 256, 3072 in all
- cotangent: float32 [2, 8192], P(None, ('grp', 'cell')), parts along dimension 1, may hold values from -6 to 6
- weight_in: float32 [2, 256, 512], replicated, may hold values from -0.375 to 0.375
- weight_temp: float32 [2, 32], replicated, may hold values from -1 to 1
- weight_slice: float32 [2, 32, 64], replicated, may hold values from -1 to 1
- weight_qkv: float32 [2, 32, 96], replicated, may hold values from -1 to 1
- weight_out: float32 [2, 256, 256], replicated, may hold values from -0.375 to 0.375
- expansion_matrix: float32 [2, 256, 1024], replicated, may hold values from -0.375 to 0.375
- weight_down: float32 [2, 1024, 256], replicated, may hold values from -0.1875 to 0.1875
- weight_head: float32 [256, 2], replicated, may hold values from -0.375 to 0.375
Outputs:
- prediction: float32 [2, 8192], P(None, ('grp', 'cell')), parts along dimension 1
- grad_in: float32 [4, 256, 512], P('grp'), parts along dimension 0
- grad_temp: float32 [4, 32], P('grp'), parts along dimension 0
- grad_slice: float32 [4, 32, 64], P('grp'), parts along dimension 0
- grad_qkv: float32 [4, 32, 96], P('grp'), parts along dimension 0
- grad_out: float32 [4, 256, 256], P('grp'), parts along dimension 0
- grad_up: float32 [4, 256, 1024], P('grp'), parts along dimension 0
- grad_down: float32 [4, 1024, 256], P('grp'), parts along dimension 0
- grad_head: float32 [512, 2], P('grp'), parts along dimension 0
There are 2 independent parts, one for each index of `grp`. A program takes and returns all parts, laid end to end along the dimension named above; an argument that names none is the same for every part. Nothing has to cross between parts.
Inputs may be any that keep to these rules, and one draw needn't show every extreme that they name: counts[b] is the number of live cell slots of device block b; they sum to 3072, and the largest is 256.
All inputs are finite; a program needn't handle non-finite values.
Results may differ from a plain program's by a relative error of at most 0.0003.
Values sent between devices are 32-bit elements; how exact they have to be, the bound alone decides.
No kernel may reach another device: no remote copies, remote signals or barrier semaphores. Data moves between devices by JAX's collectives and lax.ppermute only.
A program may use at most 128 MiB of HBM per device.

v0:
```python
from functools import partial

import jax
import jax.numpy as jnp
from jax import lax
from jax.sharding import PartitionSpec as P

H = 8
L = 2


strict_reference_switch = lax.Precision.HIGHEST
epsilon = 1e-05


def matmul(left, right):
    return jnp.dot(
        left, right, precision=strict_reference_switch, preferred_element_type=jnp.float32
    )


def normalize(field):
    average = jnp.mean(field, axis=-1, keepdims=True)
    centered = field - average
    variance = jnp.mean(centered * centered, axis=-1, keepdims=True)
    return centered * lax.rsqrt(variance + 1e-05)


def front(field, w_in, w_temp, w_slice, mask):
    element_total_number, model_width = field.shape
    projected = matmul(normalize(field), w_in)
    x_mid = projected[:, :model_width].reshape(element_total_number, H, -1)
    features = projected[:, model_width:].reshape(element_total_number, H, -1)
    temper = 0.5 + jax.nn.softplus(
        jnp.einsum("nhd,d->nh", x_mid, w_temp, precision=strict_reference_switch)
    )
    logits = (
        jnp.einsum("nhd,dm->nhm", x_mid, w_slice, precision=strict_reference_switch)
        / temper[:, :, None]
    )
    exponent = jnp.exp(logits)
    normalized_assignment_probabilities = (
        exponent / jnp.sum(exponent, axis=-1, keepdims=True) * mask[:, None, None]
    )
    numerator = jnp.einsum(
        "wes,wek->esk",
        normalized_assignment_probabilities,
        features,
        precision=strict_reference_switch,
    )
    denom = jnp.sum(normalized_assignment_probabilities, axis=0)
    return (normalized_assignment_probabilities, numerator, denom)


def middle(token_states, query_key_value_weight):
    head_width = token_states.shape[-1]
    query_key_value = jnp.einsum(
        "kwz,za->kwa", token_states, query_key_value_weight, precision=strict_reference_switch
    )
    query_rows = query_key_value[:, :, :head_width]
    key_portion = query_key_value[:, :, head_width : 2 * head_width]
    value_portion = query_key_value[:, :, 2 * head_width :]
    attention_scores = jnp.einsum(
        "gus,gvs->guv", query_rows, key_portion, precision=strict_reference_switch
    ) / jnp.sqrt(jnp.float32(head_width))
    exponent = jnp.exp(attention_scores)
    attention_map = exponent / jnp.sum(exponent, axis=-1, keepdims=True)
    return jnp.einsum(
        "juz,jzq->juq", attention_map, value_portion, precision=strict_reference_switch
    )


def rear(field, normalized_assignment_probabilities, blended_points, w_out, w_up, w_down):
    element_total_number = field.shape[0]
    restored_point_features = jnp.einsum(
        "wel,elu->weu",
        normalized_assignment_probabilities,
        blended_points,
        precision=strict_reference_switch,
    ).reshape(element_total_number, -1)
    first = field + matmul(restored_point_features, w_out)
    hidden = jax.nn.gelu(matmul(normalize(first), w_up), approximate=True)
    return first + matmul(hidden, w_down)


def readout(field, w_head):
    return matmul(normalize(field), w_head).T


def shards(
    features,
    counts,
    cotangent,
    weight_in,
    weight_temp,
    weight_slice,
    weight_qkv,
    weight_out,
    expansion_matrix,
    weight_down,
    weight_head,
):
    element_total_number = features.shape[0]
    mask = (jnp.arange(element_total_number, dtype=jnp.int32) < counts[0]).astype(jnp.float32)
    front_masked = partial(front, mask=mask)
    field = features
    saved = []
    for layer in range(L):
        front_out, front_back = jax.vjp(
            front_masked, field, weight_in[layer], weight_temp[layer], weight_slice[layer]
        )
        normalized_assignment_probabilities, numerator, denom = front_out
        numer_all, denom_all = lax.psum((numerator, denom), "cell")
        token_states = numer_all / (denom_all[:, :, None] + epsilon)
        blended_points, middle_back = jax.vjp(middle, token_states, weight_qkv[layer])
        field, rear_back = jax.vjp(
            rear,
            field,
            normalized_assignment_probabilities,
            blended_points,
            weight_out[layer],
            expansion_matrix[layer],
            weight_down[layer],
        )
        saved.append((front_back, middle_back, rear_back, token_states, denom_all))
    prediction, head_back = jax.vjp(readout, field, weight_head)
    grad_field, head_local = head_back(cotangent * mask[None, :])
    head_total = head_local
    per_layer = []
    for layer in range(L - 1, -1, -1):
        front_back, middle_back, rear_back, token_states, denom_all = saved[layer]
        d_field, d_weights, d_mixed, g_out, g_up, g_down = rear_back(grad_field)
        d_mixed = lax.psum(d_mixed, "cell")
        d_tokens, g_qkv = middle_back(d_mixed)
        inverse = 1.0 / (denom_all + epsilon)
        d_numer = d_tokens * inverse[:, :, None]
        d_denom = -jnp.sum(d_tokens * token_states, axis=-1) * inverse
        leading_half_grad, g_in, g_temp, g_slice = front_back((d_weights, d_numer, d_denom))
        grad_field = d_field + leading_half_grad
        head_part = head_local if layer == L - 1 else jnp.zeros((1,), jnp.float32)
        summed = lax.psum((g_in, g_temp, g_slice, g_out, g_up, g_down, head_part), "cell")
        if layer == L - 1:
            head_total = summed[6]
        per_layer.append((summed[0], summed[1], summed[2], g_qkv, summed[3], summed[4], summed[5]))
    per_layer = per_layer[::-1]
    stacked = [jnp.stack([entry[slot] for entry in per_layer], axis=0) for slot in range(7)]
    grad_in, grad_temp, grad_slice = (stacked[0], stacked[1], stacked[2])
    grad_out, grad_up, grad_down = (stacked[4], stacked[5], stacked[6])
    grad_qkv = stacked[3]
    return (
        prediction,
        grad_in,
        grad_temp,
        grad_slice,
        grad_qkv,
        grad_out,
        grad_up,
        grad_down,
        head_total,
    )


def solution(mesh):
    placed = (
        P(("grp", "cell"), None),
        P(("grp", "cell")),
        P(None, ("grp", "cell")),
        P(),
        P(),
        P(),
        P(),
        P(),
        P(),
        P(),
        P(),
    )
    return jax.shard_map(
        shards,
        mesh=mesh,
        in_specs=placed,
        out_specs=(
            P(None, ("grp", "cell")),
            P("grp", None, None),
            P("grp", None),
            P("grp", None, None),
            P("grp", None, None),
            P("grp", None, None),
            P("grp", None, None),
            P("grp", None, None),
            P("grp", None),
        ),
        check_vma=False,
    )
```

profile of v0, /device:TPU:0, one launch (start us, length us, event | category | flops | bytes accessed | tf_op | source)
XLA Modules:
  0.0 624.2 jit_solution(11749956084133502471)
XLA Ops:
  10.7 1.8 fusion.50
  12.9 1.8 fusion.192
  20.1 35.1 %psum.134 = f32[8,64]{1,0:T(8,128)S(1)} all-reduce(f32[8,64]{1,0:T(8,128)S(1)} %get-tuple-element.42), channel_id=1, replica_groups=mesh['grp'=2,'cell'=16] {'cell'}, use_global_device_ids=true, to_apply=%region_5.0 | all-reduce | flops 512 | bytes 4096 | tf_op jit(solution)/shard_map/psum | solution.py:113
  55.9 52.5 %all-reduce.18.cloned.1.call-done = f32[8,64,32]{1,2,0:T(8,128)} async-done(((f32[8,64,32]{1,2,0:T(8,128)}), f32[8,64,32]{1,2,0:T(8,128)}) %all-reduce.18.cloned.1.call-update) | async-done | bytes 65552 | tf_op jit(solution)/shard_map/psum | solution.py:113
  108.4 1.5 fusion.150
  114.2 2.1 fusion.232
  118.5 2.5 fusion.190
  123.2 1.4 fusion.222
  126.3 31.7 %psum.136 = f32[8,64]{1,0:T(8,128)S(1)} all-reduce(f32[8,64]{1,0:T(8,128)S(1)} %get-tuple-element.40), channel_id=1, replica_groups=mesh['grp'=2,'cell'=16] {'cell'}, use_global_device_ids=true, to_apply=%region_14.0 | all-reduce | flops 512 | bytes 4096 | tf_op jit(solution)/shard_map/psum | solution.py:113
  159.8 83.8 %all-reduce.20.cloned.1.call-done = f32[8,64,32]{1,2,0:T(8,128)} async-done(((f32[8,64,32]{1,2,0:T(8,128)}), f32[8,64,32]{1,2,0:T(8,128)}) %all-reduce.20.cloned.1.call-update) | async-done | bytes 65552 | tf_op jit(solution)/shard_map/psum | solution.py:113
  243.6 1.5 fusion.144
  247.5 1.8 fusion.234
  250.5 2.1 fusion.235
  253.2 2.4 fusion.19
  255.6 2.9 convolution_bitcast_fusion
  259.6 2.2 convolution_bitcast_fusion.2
  264.9 87.5 %all-reduce.22.cloned.1.call-done = f32[8,64,32]{1,2,0:T(8,128)} async-done(((f32[8,64,32]{1,2,0:T(8,128)}), f32[8,64,32]{1,2,0:T(8,128)}) %all-reduce.22.cloned.1.call-update) | async-done | bytes 65552 | tf_op jit(solution)/shard_map/psum | solution.py:133
  352.4 1.6 multiply_reduce_fusion.7
  354.0 1.7 fusion.68
  363.3 2.4 fusion.13
  365.8 3.0 convolution_bitcast_fusion.1
  369.9 2.2 convolution_bitcast_fusion.3
  375.1 2.1 convolution_bitcast_fusion.4
  377.2 86.5 %all-reduce.24.cloned.1.call-done = f32[8,64,32]{1,2,0:T(8,128)} async-done(((f32[8,64,32]{1,2,0:T(8,128)}), f32[8,64,32]{1,2,0:T(8,128)}) %all-reduce.24.cloned.1.call-update) | async-done | bytes 65552 | tf_op jit(solution)/shard_map/psum | solution.py:133
  463.7 1.4 multiply_reduce_fusion.4
  470.2 1.9 convolution_bitcast_fusion.5
  476.3 62.5 %all-reduce.10 = (f32[1,32]{1,0:T(1,128)S(1)}, f32[1,32]{1,0:T(1,128)S(1)}, f32[1,32,64]{2,1,0:T(8,128)S(1)}, f32[1,32,64]{2,1,0:T(8,128)S(1)}, f32[256,2]{0,1:T(2,128)}) all-reduce(f32[1,32]{1,0:T(1,128)S(1)} %convolution_bitcast_fusion.17, ...), channel_id=1, replica_groups=mesh['grp'=2,'cell'=16] {'cell'}, use_global_device_ids=true, to_apply=%region_41.43 | all-reduce | flops 4672 | bytes 37376 | tf_op jit(solution)/shard_map/psum | solution.py:141
  541.1 68.4 %all-reduce.26.cloned.1.call-done = (f32[1,256,512]{2,1,0:T(8,128)}, f32[1,256,512]{2,1,0:T(8,128)}, f32[1,256,256]{2,1,0:T(8,128)}, f32[1,256,256]{2,1,0:T(8,12...) async-done(((f32[1,256,512]{2,1,0:T(8,128)}, f32[1,256,512]{2,1,0:T(8,128)}, ...) | async-done | bytes 5767184 | tf_op jit(solution)/shard_map/psum | solution.py:141
  609.5 2.4 pad_maximum_fusion.2
  611.9 1.9 pad_maximum_fusion.3
  613.7 1.5 pad_maximum_fusion
  616.0 1.5 pad_maximum_fusion.1
  (349 shorter events, 52.0 us)
Async XLA Ops:
  7.2 245.4 %copy-start = (f32[256,2]{0,1:T(2,128)S(1)}, f32[256,2]{0,1:T(2,128)}, u32[]{:S(2)}) copy-start(f32[256,2]{0,1:T(2,128)} %param.22) | copy-start | bytes 6148
  7.2 5.7 copy-start.84
  7.2 101.2 %all-reduce.18.cloned.1.call-start = ((), (), s32[]{:S(2)}) async-start(), calls=%async_computation | async-start | bytes 262144 | tf_op jit(solution)/shard_map/psum | solution.py:113
  7.9 8.5 %copy-start.64 = (f32[256]{0:T(256)}, f32[256]{0:T(256)S(1)}, u32[]{:S(2)}) copy-start(f32[256]{0:T(256)S(1)} %compare_convert_fusion) | copy-start | bytes 3076
  16.4 94.2 %copy-start.43 = (f32[256,8]{0,1:T(8,128)}, f32[256,8]{0,1:T(8,128)S(1)}, u32[]{:S(2)}) copy-start(f32[256,8]{0,1:T(8,128)S(1)} %get-tuple-element.62) | copy-start | bytes 24580
  16.4 39.4 %copy-start.4 = (f32[256,256]{1,0:T(8,128)S(1)}, f32[256,256]{1,0:T(8,128)}, u32[]{:S(2)}) copy-start(f32[256,256]{1,0:T(8,128)} %param.12) | copy-start | bytes 786436
  16.4 92.0 %copy-start.102 = (f32[2,32,96]{2,1,0:T(8,128)S(1)}, f32[2,32,96]{2,1,0:T(8,128)}, u32[]{:S(2)}) copy-start(f32[2,32,96]{2,1,0:T(8,128)} %param.18) | copy-start | bytes 73732
  18.6 225.0 %all-reduce.20.cloned.1.call-start = ((), (), s32[]{:S(2)}) async-start(), calls=%async_computation.1 | async-start | bytes 262144 | tf_op jit(solution)/shard_map/psum | solution.py:113
  55.2 57.1 %copy-start.52 = (f32[8,64]{1,0:T(8,128)}, f32[8,64]{1,0:T(8,128)S(1)}, u32[]{:S(2)}) copy-start(f32[8,64]{1,0:T(8,128)S(1)} %psum.134) | copy-start | bytes 6148
  55.2 53.2 %copy-start.89 = (f32[8,64]{1,0:T(8,128)}, f32[8,64]{1,0:T(8,128)S(1)}, u32[]{:S(2)}) copy-start(f32[8,64]{1,0:T(8,128)S(1)} %broadcast_add_fusion.1) | copy-start | bytes 6148
  118.3 39.7 %copy-start.24 = (f32[256,256]{0,1:T(8,128)}, f32[256,256]{0,1:T(8,128)S(1)}, u32[]{:S(2)}) copy-start(f32[256,256]{0,1:T(8,128)S(1)} %copy.63) | copy-start | bytes 786436
  118.4 6.2 copy-start.11
  121.9 121.7 %copy-start.103 = (f32[2,32,96]{2,1,0:T(8,128)S(1)}, f32[2,32,96]{2,1,0:T(8,128)}, u32[]{:S(2)}) copy-start(f32[2,32,96]{2,1,0:T(8,128)} %param.18) | copy-start | bytes 73732
  123.2 121.9 %copy-start.40 = (f32[256,8]{0,1:T(8,128)}, f32[256,8]{0,1:T(8,128)S(1)}, u32[]{:S(2)}) copy-start(f32[256,8]{0,1:T(8,128)S(1)} %get-tuple-element.53) | copy-start | bytes 24580
  124.7 121.7 %copy-start.45 = (f32[256,8]{0,1:T(8,128)}, f32[256,8]{0,1:T(8,128)S(1)}, u32[]{:S(2)}) copy-start(f32[256,8]{0,1:T(8,128)S(1)} %get-tuple-element.70) | copy-start | bytes 24580
  159.3 193.1 %all-reduce.22.cloned.1.call-start = ((), (), s32[]{:S(2)}) async-start(), calls=%async_computation.2 | async-start | bytes 262144 | tf_op jit(solution)/shard_map/psum | solution.py:133
  159.8 86.6 %copy-start.91 = (f32[8,64]{1,0:T(8,128)}, f32[8,64]{1,0:T(8,128)S(1)}, u32[]{:S(2)}) copy-start(f32[8,64]{1,0:T(8,128)S(1)} %broadcast_add_fusion) | copy-start | bytes 6148
  263.7 200.0 %all-reduce.24.cloned.1.call-start = ((), (), s32[]{:S(2)}) async-start(), calls=%async_computation.3 | async-start | bytes 262144 | tf_op jit(solution)/shard_map/psum | solution.py:133
  264.9 90.9 %copy-start.8 = (f32[8,64,96]{2,1,0:T(8,128)S(1)}, f32[8,64,96]{2,1,0:T(8,128)}, u32[]{:S(2)}) copy-start(f32[8,64,96]{2,1,0:T(8,128)} %copy-done.7) | copy-start | bytes 589828
  352.4 4.7 copy-start.39
  352.4 6.1 copy-start.92
  352.4 6.1 copy-start.100
  352.4 6.1 copy-start.104
  354.0 4.8 copy-start.55
  354.0 4.9 copy-start.37
  372.2 91.5 %copy-start.19 = (f32[8,64,64]{1,2,0:T(8,128)S(1)}, f32[8,64,64]{1,2,0:T(8,128)}, u32[]{:S(2)}) copy-start(f32[8,64,64]{1,2,0:T(8,128)} %copy-done.18) | copy-start | bytes 393220
  372.2 91.5 %copy-start.76 = (f32[8,64]{1,0:T(8,128)S(1)}, f32[8,64]{1,0:T(8,128)}, u32[]{:S(2)}) copy-start(f32[8,64]{1,0:T(8,128)} %multiply_divide_fusion.4) | copy-start | bytes 6148
  373.4 91.8 %copy-start.75 = (f32[8,64]{1,0:T(8,128)S(1)}, f32[8,64]{1,0:T(8,128)}, u32[]{:S(2)}) copy-start(f32[8,64]{1,0:T(8,128)} %copy-done.74) | copy-start | bytes 6148
  375.0 234.4 %all-reduce.26.cloned.1.call-start = ((), (), s32[]{:S(2)}) async-start(), calls=%async_computation.4 | async-start | bytes 11534336 | tf_op jit(solution)/shard_map/psum | solution.py:141
  377.2 89.8 %copy-start.90 = (f32[8,64]{1,0:T(8,128)S(1)}, f32[8,64]{1,0:T(8,128)}, u32[]{:S(2)}) copy-start(f32[8,64]{1,0:T(8,128)} %copy-done.89) | copy-start | bytes 6148
  377.2 89.9 %copy-start.99 = (f32[8,64,32]{1,2,0:T(8,128)S(1)}, f32[8,64,32]{1,2,0:T(8,128)}, u32[]{:S(2)}) copy-start(f32[8,64,32]{1,2,0:T(8,128)} %all-reduce.18.cloned.1.call-done) | copy-start | bytes 196612
  377.2 89.9 %copy-start.105 = (f32[2,32,96]{2,1,0:T(8,128)S(1)}, f32[2,32,96]{2,1,0:T(8,128)}, u32[]{:S(2)}) copy-start(f32[2,32,96]{2,1,0:T(8,128)} %param.18) | copy-start | bytes 73732
  (88 other events, 206.8 us)
Sparse Core Ops, SparseCore 0:
  18.7 89.6 all-reduce.17
  159.4 84.1 all-reduce.19
  263.8 88.5 all-reduce.21
  375.2 88.5 all-reduce.23
  472.4 137.0 all-reduce.25
where the time goes:
time: 629 us; the launch traced here: 624 us
  waiting for transfers between devices  379 us (60%)
  blocking collectives  129 us (21%)
  matrix products  72.4 us (12%)
  other arithmetic  17.9 us (3%)
  between operations  16.6 us (3%)
  local copies, waits for them, and re-layouts  8.68 us (1%)
    psum x2, waiting for transfers between devices, shards(): d_mixed = lax.psum(d_mixed, 'cell')  174 us
    psum x2, waiting for transfers between devices, shards(): numer_all, denom_all = lax.psum((numerator, denom), 'cell')  136 us
    psum x1, waiting for transfers between devices, shards(): lax.psum((g_in, g_temp, g_slice, g_out, g_up, g_down, head_part), 'cell')  68.4 us
    psum x2, blocking collectives, shards(): numer_all, denom_all = lax.psum((numerator, denom), 'cell')  66.8 us
    psum x1, blocking collectives, shards(): lax.psum((g_in, g_temp, g_slice, g_out, g_up, g_down, head_part), 'cell')  62.5 us
    dot_general x26, matrix products, matmul(): jnp.dot(left, right, precision=strict_reference_switch, preferred_element...  37.7 us
  transfers between devices with their start and end apart: 5, of which 5 were waited for; matrix products, arithmetic and copies ran while one was open for 2% of the time, Pallas kernels for 0%

commit v1 on v0

v1 whole, which is shorter than its diff:
```python
from functools import partial

import jax
import jax.numpy as jnp
from jax import lax
from jax.experimental import pallas as pl
from jax.experimental.pallas import tpu as pltpu
from jax.sharding import PartitionSpec as P

H = 8
L = 2
F32 = jnp.float32
BF16 = jnp.bfloat16
EPS = 1e-05


def split(a):
    if isinstance(a, tuple):
        return a
    hi = a.astype(BF16)
    return hi, (a - hi.astype(F32)).astype(BF16)


def exact(a):
    return (a.astype(BF16),)


def raw(a, b, ca, cb):
    return lax.dot_general(a, b, (((ca,), (cb,)), ((), ())), preferred_element_type=F32)


def product(a, b, ca, cb):
    a, b = split(a), split(b)
    out = raw(a[0], b[0], ca, cb)
    if len(b) > 1:
        out = out + raw(a[0], b[1], ca, cb)
    if len(a) > 1:
        out = out + raw(a[1], b[0], ca, cb)
    return out


def nn(a, b):
    return product(a, b, 1, 0)


def nt(a, b):
    return product(a, b, 1, 1)


def tn(a, b):
    return product(a, b, 0, 0)


def same_head(rows, row_head, cols, col_head):
    r = lax.broadcasted_iota(jnp.int32, (rows, cols), 0) // row_head
    c = lax.broadcasted_iota(jnp.int32, (rows, cols), 1) // col_head
    return r == c


def ones_block(rows, row_head, cols, col_head):
    return exact(same_head(rows, row_head, cols, col_head).astype(F32))


def expand(small, col_head):
    r, cols = small.shape
    tiled = jnp.concatenate([small] * H, axis=0)
    return jnp.where(same_head(H * r, r, cols, col_head), tiled, 0.0)


def fold(dense, col_head):
    rows, cols = dense.shape
    r = rows // H
    head = lax.broadcasted_iota(jnp.int32, (r, cols), 1) // col_head
    out = jnp.where(head == 0, dense[:r], 0.0)
    for h in range(1, H):
        out = jnp.where(head == h, dense[h * r : (h + 1) * r], out)
    return out


def tile_lanes(a, times):
    return jnp.concatenate([a] * times, axis=1)


def norm(field):
    centered = field - jnp.mean(field, axis=-1, keepdims=True)
    rstd = lax.rsqrt(jnp.mean(centered * centered, axis=-1, keepdims=True) + EPS)
    return centered * rstd, rstd


def norm_back(dy, y, rstd):
    return rstd * (
        dy - jnp.mean(dy, axis=-1, keepdims=True) - y * jnp.mean(dy * y, axis=-1, keepdims=True)
    )


def softplus(t):
    return jnp.maximum(t, 0.0) + jnp.log(1.0 + jnp.exp(-jnp.abs(t)))


def front(field, w_in, w_temp, w_slice, live):
    n, width = field.shape
    dh, m = w_slice.shape
    hm = H * m
    nf, rstd = norm(field)
    proj = nn(nf, w_in)
    x, v = proj[:, :width], proj[:, width:]
    wt = tile_lanes(w_temp, H)
    xt = split(x * wt)
    t_wide = nn(xt, ones_block(width, dh, hm, m))
    t_slim = nn(xt, ones_block(width, dh, width, dh))
    r = 1.0 / (0.5 + softplus(t_wide))
    rs = jax.nn.sigmoid(t_slim) / (0.5 + softplus(t_slim))
    logits = nn(x, expand(tile_lanes(w_slice, H), m)) * r
    e = jnp.exp(logits)
    z = nn(e, ones_block(hm, m, hm, m))
    rows = lax.broadcasted_iota(jnp.int32, (n, hm), 0)
    s = jnp.where(rows < live, e / z, 0.0)
    numer = fold(tn(v, s), m)
    denom = jnp.sum(s, axis=0, keepdims=True)
    packed = jnp.concatenate([numer, jnp.broadcast_to(denom, (8, hm))], axis=0)
    return packed, s, proj, nf, rstd, logits, r, rs


def tokens_of(packed, dh):
    inv = 1.0 / (packed[dh : dh + 1] + EPS)
    return packed[:dh] * inv, inv


def middle(packed, w_qkv):
    dh = w_qkv.shape[0]
    tok, inv = tokens_of(packed, dh)
    qkv = tn(w_qkv, tok)
    q, k, v = qkv[:dh], qkv[dh : 2 * dh], qkv[2 * dh :]
    hm = tok.shape[1]
    m = hm // H
    pair = 2 * m
    own = same_head(pair, m, pair, m)
    scale = 1.0 / float(dh) ** 0.5
    maps, mixed = [], []
    for g in range(H // 2):
        lanes = slice(g * pair, (g + 1) * pair)
        e = jnp.where(own, jnp.exp(tn(k[:, lanes], q[:, lanes]) * scale), 0.0)
        a = e / jnp.sum(e, axis=0, keepdims=True)
        maps.append(a)
        mixed.append(nn(v[:, lanes], a))
    return tok, inv, q, k, v, maps, jnp.concatenate(mixed, axis=1)


def middle_back(packed, w_qkv, d_mixed):
    dh = w_qkv.shape[0]
    tok, inv, q, k, v, maps, _ = middle(packed, w_qkv)
    hm = tok.shape[1]
    pair = 2 * (hm // H)
    scale = 1.0 / float(dh) ** 0.5
    dq, dk, dv = [], [], []
    for g in range(H // 2):
        lanes = slice(g * pair, (g + 1) * pair)
        a, dm = maps[g], d_mixed[:, lanes]
        dv.append(nt(dm, a))
        da = tn(v[:, lanes], dm)
        ds = a * (da - jnp.sum(a * da, axis=0, keepdims=True)) * scale
        dk.append(nt(q[:, lanes], ds))
        dq.append(nn(k[:, lanes], ds))
    d_qkv = jnp.concatenate([jnp.concatenate(p, axis=1) for p in (dq, dk, dv)], axis=0)
    g_qkv = nt(tok, d_qkv)
    d_tok = nn(w_qkv, d_qkv)
    d_numer = d_tok * inv
    d_denom = -jnp.sum(d_tok * tok, axis=0, keepdims=True) * inv
    return g_qkv, d_numer, d_denom


def front_back(ds, d_numer, d_denom, s, proj, nf, logits, r, rs, w_in, w_temp, w_slice):
    width = proj.shape[1] // 2
    dh, m = w_slice.shape
    hm = H * m
    x, v = proj[:, :width], proj[:, width:]
    d_blk = split(expand(d_numer, m))
    ds = ds + nn(v, d_blk) + d_denom
    dv = nt(s, d_blk)
    sds = s * ds
    d_logits = sds - s * nn(sds, ones_block(hm, m, hm, m))
    d_t = -rs * nn(d_logits * logits, ones_block(hm, m, width, dh))
    du = split(d_logits * r)
    wt = tile_lanes(w_temp, H)
    dx = nt(du, expand(tile_lanes(w_slice, H), m)) + d_t * wt
    g_temp = jnp.sum(x * d_t, axis=0, keepdims=True)
    g_slice = fold(tn(x, du), m)
    g_slice = sum(g_slice[:, g * 2 * m : (g + 1) * 2 * m] for g in range(H // 2))
    g_slice = g_slice[:, :m] + g_slice[:, m:]
    d_proj = split(jnp.concatenate([dx, dv], axis=1))
    g_in = tn(nf, d_proj)
    return d_proj, g_in, g_temp, g_slice


def gelu_parts(pre):
    c = 0.7978845608028654
    sq = pre * pre
    t = jnp.tanh(c * pre * (1.0 + 0.044715 * sq))
    hid = 0.5 * pre * (1.0 + t)
    slope = 0.5 * (1.0 + t) + 0.5 * pre * (1.0 - t * t) * c * (1.0 + 3 * 0.044715 * sq)
    return hid, slope


def rear(field, s, mixed, w_out, w_up, w_down):
    m = mixed.shape[1] // H
    des = nt(s, expand(mixed, m))
    first = field + nn(des, w_out)
    n1, rstd1 = norm(first)
    pre = nn(n1, w_up)
    hid, _ = gelu_parts(pre)
    return first + nn(hid, w_down), des, n1, rstd1, pre


def rear_back(g, s, mixed, des, n1, rstd1, pre, w_out, w_up, w_down):
    m = mixed.shape[1] // H
    hid, slope = gelu_parts(pre)
    gs = split(g)
    g_down = tn(hid, gs)
    d_pre = split(nt(gs, w_down) * slope)
    g_up = tn(n1, d_pre)
    d_first = g + norm_back(nt(d_pre, w_up), n1, rstd1)
    dfs = split(d_first)
    g_out = tn(des, dfs)
    d_des = split(nt(dfs, w_out))
    ds = nn(d_des, expand(mixed, m))
    d_mixed = fold(tn(d_des, s), m)
    return d_first, ds, d_mixed, g_out, g_up, g_down


def store(refs, values):
    for ref, value in zip(refs, values, strict=True):
        ref[...] = value


def kernel_a(live, field, w_in, w_temp, w_slice, *out):
    store(out, front(field[...], w_in[...], w_temp[...], w_slice[...], live[0]))


def kernel_b(live, packed, field, s, w_qkv, w_out, w_up, w_down, w_in, w_temp, w_slice, *out):
    mixed = middle(packed[...], w_qkv[...])[-1]
    f1, des, n1, rstd1, pre = rear(field[...], s[...], mixed, w_out[...], w_up[...], w_down[...])
    store(out[:5], (mixed, des, n1, rstd1, pre))
    out[5][...] = f1
    store(out[6:], front(f1, w_in[...], w_temp[...], w_slice[...], live[0]))


def kernel_c(live, packed, field, s, w_qkv, w_out, w_up, w_down, w_head, cot, *out):
    pred, g_head, d_first, ds, d_mixed, g_out, g_up, g_down = out
    n = field.shape[0]
    mixed = middle(packed[...], w_qkv[...])[-1]
    s = s[...]
    f2, des, n1, rstd1, pre = rear(field[...], s, mixed, w_out[...], w_up[...], w_down[...])
    n2, rstd2 = norm(f2)
    wh = w_head[...]
    n2s = split(n2)
    pred[...] = nt(wh, n2s)[:2]
    lanes = lax.broadcasted_iota(jnp.int32, cot.shape, 1)
    dp = jnp.where(lanes < live[0], cot[...], 0.0)
    dp = jnp.concatenate([dp, jnp.zeros((6, n), F32)], axis=0)
    g_head[...] = nn(dp, n2s)
    g = norm_back(tn(dp, wh), n2, rstd2)
    store(
        (d_first, ds, d_mixed, g_out, g_up, g_down),
        rear_back(g, s, mixed, des, n1, rstd1, pre, w_out[...], w_up[...], w_down[...]),
    )


def kernel_d(
    packed, d_mixed, w_qkv, d_first, ds, s, proj, nf, rstd, logits, r, rs, w_in, w_temp, w_slice,
    s0, mixed0, des0, n10, rstd10, pre0, w_out0, w_up0, w_down0, *out,
):
    g_qkv, d_numer, d_denom = middle_back(packed[...], w_qkv[...], d_mixed[...])
    d_proj, g_in, g_temp, g_slice = front_back(
        ds[...], d_numer, d_denom, s[...], proj[...], nf[...], logits[...], r[...], rs[...],
        w_in[...], w_temp[...], w_slice[...],
    )
    store(out[:4], (g_qkv, g_in, g_temp, g_slice))
    g = d_first[...] + norm_back(nt(d_proj, w_in[...]), nf[...], rstd[...])
    _, ds0, d_mixed0, g_out, g_up, g_down = rear_back(
        g, s0[...], mixed0[...], des0[...], n10[...], rstd10[...], pre0[...],
        w_out0[...], w_up0[...], w_down0[...],
    )
    store(out[4:], (ds0, d_mixed0, g_out, g_up, g_down))


def kernel_e(packed, d_mixed, w_qkv, ds, s, proj, nf, logits, r, rs, w_in, w_temp, w_slice, *out):
    g_qkv, d_numer, d_denom = middle_back(packed[...], w_qkv[...], d_mixed[...])
    _, g_in, g_temp, g_slice = front_back(
        ds[...], d_numer, d_denom, s[...], proj[...], nf[...], logits[...], r[...], rs[...],
        w_in[...], w_temp[...], w_slice[...],
    )
    store(out, (g_qkv, g_in, g_temp, g_slice))


VM = pl.BlockSpec(memory_space=pltpu.VMEM)
SM = pl.BlockSpec(memory_space=pltpu.SMEM)


def call(body, shapes, *args, name):
    specs = [SM if a.dtype == jnp.int32 else VM for a in args]
    return pl.pallas_call(
        body,
        out_shape=[jax.ShapeDtypeStruct(s, F32) for s in shapes],
        in_specs=specs,
        out_specs=[VM] * len(shapes),
        compiler_params=pltpu.CompilerParams(vmem_limit_bytes=56 * 1024 * 1024),
        name=name,
    )(*args)


def swap(a, bit, count):
    return lax.ppermute(a, "cell", [(i, i ^ bit) for i in range(count)])


def sum_small(a, count):
    a = a + swap(a, 1, count)
    bit = 2
    while bit < count:
        if 2 * bit < count:
            one, two, both = (swap(a, b, count) for b in (bit, 2 * bit, 3 * bit))
            a = (a + one) + (two + both)
            bit *= 4
        else:
            a = a + swap(a, bit, count)
            bit *= 2
    return a


def shards(
    count,
    features,
    counts,
    cotangent,
    weight_in,
    weight_temp,
    weight_slice,
    weight_qkv,
    weight_out,
    expansion_matrix,
    weight_down,
    weight_head,
):
    n, width = features.shape
    dh, m = weight_slice.shape[1:]
    ff = expansion_matrix.shape[2]
    hm = H * m
    wi = [weight_in[l] for l in range(L)]
    wt = [weight_temp[l : l + 1] for l in range(L)]
    ws = [weight_slice[l] for l in range(L)]
    wq = [weight_qkv[l] for l in range(L)]
    wo = [weight_out[l] for l in range(L)]
    wu = [expansion_matrix[l] for l in range(L)]
    wd = [weight_down[l] for l in range(L)]
    wh = jnp.pad(weight_head.T, ((0, 6), (0, 0)))

    front_shapes = [
        (dh + 8, hm), (n, hm), (n, 2 * width), (n, width), (n, 1), (n, hm), (n, hm), (n, width),
    ]
    rear_shapes = [(dh, hm), (n, width), (n, width), (n, 1), (n, ff)]
    grad_rear = [(width, width), (width, ff), (ff, width)]
    grad_front = [(dh, 3 * dh), (width, 2 * width), (1, width), (dh, m)]

    p0, s0, proj0, nf0, _, lg0, r0, rs0 = call(
        kernel_a, front_shapes, counts, features, wi[0], wt[0], ws[0], name="front0"
    )
    p0 = sum_small(p0, count)
    mix0, des0, n10, rd10, pre0, f1, p1, s1, proj1, nf1, rstd1, lg1, r1, rs1 = call(
        kernel_b, rear_shapes + [(n, width)] + front_shapes,
        counts, p0, features, s0, wq[0], wo[0], wu[0], wd[0], wi[1], wt[1], ws[1], name="rear0_front1",
    )
    p1 = sum_small(p1, count)
    pred, g_head, d_first, ds1, dm1, go1, gu1, gd1 = call(
        kernel_c, [(2, n), (8, width), (n, width), (n, hm), (dh, hm)] + grad_rear,
        counts, p1, f1, s1, wq[1], wo[1], wu[1], wd[1], wh, cotangent, name="rear1_head_back1",
    )
    dm1 = sum_small(dm1, count)
    gq1, gi1, gt1, gs1, ds0, dm0, go0, gu0, gd0 = call(
        kernel_d, grad_front + [(n, hm), (dh, hm)] + grad_rear,
        p1, dm1, wq[1], d_first, ds1, s1, proj1, nf1, rstd1, lg1, r1, rs1, wi[1], wt[1], ws[1],
        s0, mix0, des0, n10, rd10, pre0, wo[0], wu[0], wd[0], name="back_front1_rear0",
    )
    dm0 = sum_small(dm0, count)
    gq0, gi0, gt0, gs0 = call(
        kernel_e, grad_front,
        p0, dm0, wq[0], ds0, s0, proj0, nf0, lg0, r0, rs0, wi[0], wt[0], ws[0], name="back_front0",
    )
    pair = lambda a, b: jnp.stack([a, b])
    big = lax.psum(
        (pair(gi0, gi1), pair(go0, go1), pair(gu0, gu1), pair(gd0, gd1)), "cell"
    )
    gt, gs, gh = (
        sum_small(a, count)
        for a in (jnp.concatenate([gt0, gt1], axis=0), pair(gs0, gs1), g_head)
    )
    gt = gt.reshape(L, H, dh).sum(1)
    return (
        pred, big[0], gt, gs, pair(gq0, gq1), big[1], big[2], big[3], gh[:2].T,
    )


def solution(mesh):
    cells = P(("grp", "cell"))
    return jax.shard_map(
        partial(shards, mesh.shape["cell"]),
        mesh=mesh,
        in_specs=(P(("grp", "cell"), None), cells, P(None, ("grp", "cell"))) + (P(),) * 8,
        out_specs=(
            P(None, ("grp", "cell")),
            P("grp", None, None),
            P("grp", None),
            P("grp", None, None),
            P("grp", None, None),
            P("grp", None, None),
            P("grp", None, None),
            P("grp", None, None),
            P("grp", None),
        ),
        check_vma=False,
    )
```

time: 629 us -> 277 us (0.44)
  waiting for transfers between devices: 379 us -> 147 us
  blocking collectives: 129 us -> 0 us
  matrix products: 72.4 us -> 0 us
  Pallas kernels: 0 us -> 42.8 us
  starting transfers between devices: 0.61 us -> 38.2 us
  local copies, waits for them, and re-layouts: 8.68 us -> 18.7 us
    psum x5 -> x1, waiting for transfers between devices: 379 us -> 103 us  [shards(): lax.psum((pair(gi0, gi1), pair(go0, go1), pair(gu0, gu1), pair(gd0, gd1))...]
    psum x3 -> x0, blocking collectives: 129 us -> none  [the longest x2 66.8 us: shards(): numer_all, denom_all = lax.psum((numerator, denom), 'cell')]
    dot_general x66 -> x0, matrix products: 72.4 us -> none  [the longest x26 37.7 us: matmul(): jnp.dot(left, right, precision=strict_reference_switch, preferred_element...]
    ppermute x0 -> x35, waiting for transfers between devices: none -> 44.1 us  [swap(): return lax.ppermute(a, 'cell', [(i, i ^ bit) for i in range(count)])]
    pallas_call x0 -> x5, Pallas kernels: none -> 42.8 us  [call(): pl.pallas_call(body, out_shape=[jax.ShapeDtypeStruct(s, F32) for s in sha...]
    ppermute x0 -> x35, starting transfers between devices: none -> 38.2 us  [swap(): return lax.ppermute(a, 'cell', [(i, i ^ bit) for i in range(count)])]
    squeeze x1 -> x6, local copies, waits for them, and re-layouts: 0.54 us -> 8.01 us  [the longest x1 2.25 us: shards(): wi = [weight_in[l] for l in range(L)]]
  transfers between devices with their start and end apart: 5 -> 36, of which waited for: 5 -> 28; matrix products, arithmetic and copies ran while one was open for 2% -> 5% of each run, Pallas kernels for 0% -> 0%
where the time goes in v1:
time: 277 us; the launch traced here: 276 us
  waiting for transfers between devices  147 us (53%)
  Pallas kernels  42.8 us (15%)
  starting transfers between devices  38.2 us (14%)
  local copies, waits for them, and re-layouts  18.7 us (7%)
  between operations  15.1 us (5%)
  other arithmetic  14.3 us (5%)
    psum x1, waiting for transfers between devices, shards(): lax.psum((pair(gi0, gi1), pair(go0, go1), pair(gu0, gu1), pair(gd0, gd1))...  103 us
    ppermute x35, waiting for transfers between devices, swap(): return lax.ppermute(a, 'cell', [(i, i ^ bit) for i in range(count)])  44.1 us
    pallas_call x5, Pallas kernels, call(): pl.pallas_call(body, out_shape=[jax.ShapeDtypeStruct(s, F32) for s in sha...  42.8 us
    ppermute x35, starting transfers between devices, swap(): return lax.ppermute(a, 'cell', [(i, i ^ bit) for i in range(count)])  38.2 us
    unnamed x48, local copies, waits for them, and re-layouts  8.66 us
    another operation x6, other arithmetic, shards(): pair = lambda a, b: jnp.stack([a, b])  7.98 us
  transfers between devices with their start and end apart: 36, of which 28 were waited for; matrix products, arithmetic and copies ran while one was open for 5% of the time, Pallas kernels for 0%

profile of v1, /device:TPU:0, one launch (start us, length us, event | category | flops | bytes accessed | tf_op | source)
XLA Modules:
  0.0 276.0 jit_solution(3914019377840004191)
XLA Ops:
  10.7 2.3 slice_bitcast_fusion.4
  13.0 4.2 %front0.1 = (f32[40,512]{1,0:T(8,128)}, f32[256,512]{1,0:T(8,128)}, f32[256,512]{1,0:T(8,128)}, f32[256,256]{1,0:T(8,128)}, f32[256,1]{1,0:T(8,128)}, /*index=5*...) custom-call(s32[1]{0:T(128)S(6)} %copy.24.live, f32[256,256]{1,0:T(8,128)} %field.3, ...), custom_call_target="tpu_custom_call" | custom-call | tf_op jit(solution)/shard_map/front0/pallas_call | solution.py:301
  20.6 4.4 %collective-permute-start.3 = (f32[40,512]{1,0:T(8,128)S(1)}, f32[40,512]{1,0:T(8,128)S(1)}, u32[]{:S(2)}, u32[]{:S(2)}) collective-permute-start(f32[40,512]{1,0:T(8,128)S(1)} %add.115), channel_id=1, source_target_pairs={{0,6},{1,7},{2,4},{3,5},{4,2},{5,3},{6,0},{7,1},{8,14},{9,15},{10,... | collective-permute-start | bytes 245768 | tf_op jit(solution)/shard_map/ppermute | solution.py:312
  28.0 1.7 collective-permute-done.2
  29.9 2.6 collective-permute-start.4
  33.2 2.1 collective-permute-done.4
  36.0 9.1 %rear0_front1.1 = (f32[32,512]{1,0:T(8,128)}, f32[256,256]{1,0:T(8,128)}, f32[256,256]{1,0:T(8,128)}, f32[256,1]{1,0:T(8,128)}, f32[256,1024]{1,0:T(8,128)}, /*i...) custom-call(s32[1]{0:T(128)S(6)} %copy.24.live, ...), custom_call_target="tpu_custom_call" | custom-call | tf_op jit(solution)/shard_map/rear0_front1/pallas_call | solution.py:301
  47.6 1.9 collective-permute-start.8
  51.1 2.5 collective-permute-done.8
  54.8 2.7 collective-permute-start.9
  58.1 3.8 %collective-permute-done.9 = f32[40,512]{1,0:T(8,128)S(1)} collective-permute-done((f32[40,512]{1,0:T(8,128)S(1)}, f32[40,512]{1,0:T(8,128)S(1)}, u32[]{:S(2)}, u32[]{:S(2)}) %collective-permute-start.9) | collective-permute-done | bytes 81952 | tf_op jit(solution)/shard_map/ppermute | solution.py:312
  62.6 10.6 %rear1_head_back1.1 = (f32[2,256]{1,0:T(2,128)}, f32[8,256]{1,0:T(8,128)}, f32[256,256]{1,0:T(8,128)}, f32[256,512]{1,0:T(8,128)}, f32[32,512]{1,0:T(8,128)}, /*...) custom-call(s32[1]{0:T(128)S(6)} %copy.24.live, f32[40,512]{1,0:T(8,128)} %add.124.packed, ...), custom_call_target="tpu_custom_call" | custom-call | tf_op jit(solution)/shard_map/rear1_head_back1/pallas_call | solution.py:301
  76.3 1.7 collective-permute-start.12
  79.1 2.3 collective-permute-done.13
  82.2 1.6 collective-permute-start.14
  83.9 4.3 %collective-permute-done.14 = f32[32,512]{1,0:T(8,128)S(1)} collective-permute-done((f32[32,512]{1,0:T(8,128)S(1)}, f32[32,512]{1,0:T(8,128)S(1)}, u32[]{:S(2)}, u32[]{:S(2)}) %collective-permute-start.14) | collective-permute-done | bytes 65568 | tf_op jit(solution)/shard_map/ppermute | solution.py:312
  88.8 12.2 %back_front1_rear0.1 = (f32[32,96]{1,0:T(8,128)}, f32[256,512]{1,0:T(8,128)}, f32[1,256]{1,0:T(1,128)}, f32[32,64]{1,0:T(8,128)}, f32[256,512]{1,0:T(8,128)}, /*...) custom-call(f32[40,512]{1,0:T(8,128)} %add.124.packed, ...), custom_call_target="tpu_custom_call" | custom-call | tf_op jit(solution)/shard_map/back_front1_rear0/pallas_call | solution.py:301
  101.2 2.9 %pad_maximum_fusion = f32[2,256,1024]{2,1,0:T(8,128)} fusion(f32[1,256,1024]{2,1,0:T(8,128)S(1)} %bitcast.40, f32[1,256,1024]{2,1,0:T(8,128)} %bitcast.42), kind=kLoop, calls=%fused_computation | loop fusion | flops 524288 | bytes 4194304 | tf_op jit(solution)/shard_map/stack | solution.py:387
  104.7 2.1 collective-permute-start.17
  112.9 3.7 %collective-permute-done.19 = f32[32,512]{1,0:T(8,128)S(1)} collective-permute-done((f32[32,512]{1,0:T(8,128)S(1)}, f32[32,512]{1,0:T(8,128)S(1)}, u32[]{:S(2)}, u32[]{:S(2)}) %collective-permute-start.19) | collective-permute-done | bytes 65568 | tf_op jit(solution)/shard_map/ppermute | solution.py:312
  117.3 6.7 %back_front0.1 = (f32[32,96]{1,0:T(8,128)}, f32[256,512]{1,0:T(8,128)}, f32[1,256]{1,0:T(1,128)}, f32[32,64]{1,0:T(8,128)}) custom-call(f32[40,512]{1,0:T(8,128)} %add.119.packed, f32[32,512]{1,0:T(8,128)} %add.134.d_mixed, f32[32,96]{1,0:T(8,128)} %get-tuple-element.106.w_qkv, f32[256,512]{1,0:T(8,128)} %get-tuple-element.72.ds, ...), custom_call_target="tpu_custom_call" | custom-call | tf_op jit(solution)/shard_map/back_front0/pallas_call | solution.py:301
  124.0 2.1 pad_maximum_fusion.2
  128.2 2.2 collective-permute-start.32
  132.5 1.6 collective-permute-done.31
  134.8 4.0 %collective-permute-done.34 = f32[8,256]{1,0:T(8,128)S(1)} collective-permute-done((f32[8,256]{1,0:T(8,128)S(1)}, f32[8,256]{1,0:T(8,128)S(1)}, u32[]{:S(2)}, u32[]{:S(2)}) %collective-permute-start.34) | collective-permute-done | bytes 8224 | tf_op jit(solution)/shard_map/ppermute | solution.py:312
  140.8 2.4 collective-permute-start.23
  144.3 2.4 collective-permute-start.28
  149.2 1.6 collective-permute-done.28
  154.0 3.7 %collective-permute-done.29 = f32[2,32,64]{2,1,0:T(8,128)S(1)} collective-permute-done((f32[2,32,64]{2,1,0:T(8,128)S(1)}, f32[2,32,64]{2,1,0:T(8,128)S(1)}, u32[]{:S(2)}, u32[]{:S(2)}) %collective-permute-start.29) | collective-permute-done | bytes 16416 | tf_op jit(solution)/shard_map/ppermute | solution.py:312
  158.3 102.9 %all-reduce.4.cloned.1.call-done = (f32[2,256,512]{2,1,0:T(8,128)}, f32[2,256,256]{2,1,0:T(8,128)}, f32[2,256,1024]{2,1,0:T(8,128)}, f32[2,1024,256]{2,1,0:T(8,128)}) async-done(((f32[2,256,512]{2,1,0:T(8,128)}, f32[2,256,256]{2,1,0:T(8,128)}, f32[2,256,1024]{2,1,0:T(8,128)}, f32[2,1024,256]{2,1,0:T(8,128)}), (f32[2,256,512]{2,1,0:T(8,128)}, f32[2,256,256]{2,1,0:T(8,128)}, f32[2,256,1024]{2,1,0:T(8,128)}, ...) | async-done | bytes 5767184 | tf_op jit(solution)/shard_map/psum | solution.py:388
  261.2 2.4 copy.25
  263.6 1.9 copy.26
  (132 shorter events, 48.3 us)
Async XLA Ops:
  7.2 254.0 %all-reduce.4.cloned.1.call-start = ((), (), s32[]{:S(2)}) async-start(), calls=%async_computation | async-start | bytes 11534336 | tf_op jit(solution)/shard_map/psum | solution.py:388
  17.1 3.5 %collective-permute-start = (f32[40,512]{1,0:T(8,128)}, f32[40,512]{1,0:T(8,128)S(1)}, u32[]{:S(2)}, u32[]{:S(2)}) collective-permute-start(f32[40,512]{1,0:T(8,128)} %get-tuple-element.51), channel_id=1, source_target_pairs={{0,1},{1,0},{2,3},{3,2},{4,5},{5,4},{6,7},{7,6},{8,9},{9,8},{10,11... | collective-permute-start | bytes 245768 | tf_op jit(solution)/shard_map/ppermute | solution.py:312
  20.6 7.4 %collective-permute-start.3 = (f32[40,512]{1,0:T(8,128)S(1)}, f32[40,512]{1,0:T(8,128)S(1)}, u32[]{:S(2)}, u32[]{:S(2)}) collective-permute-start(f32[40,512]{1,0:T(8,128)S(1)} %add.115), channel_id=1, source_target_pairs={{0,6},{1,7},{2,4},{3,5},{4,2},{5,3},{6,0},{7,1},{8,14},{9,15},{10,... | collective-permute-start | bytes 245768 | tf_op jit(solution)/shard_map/ppermute | solution.py:312
  25.0 4.6 %collective-permute-start.2 = (f32[40,512]{1,0:T(8,128)S(1)}, f32[40,512]{1,0:T(8,128)S(1)}, u32[]{:S(2)}, u32[]{:S(2)}) collective-permute-start(f32[40,512]{1,0:T(8,128)S(1)} %add.115), channel_id=1, source_target_pairs={{0,4},{1,5},{2,6},{3,7},{4,0},{5,1},{6,2},{7,3},{8,12},{9,13},{10,... | collective-permute-start | bytes 245768 | tf_op jit(solution)/shard_map/ppermute | solution.py:312
  25.5 4.4 %collective-permute-start.1 = (f32[40,512]{1,0:T(8,128)S(1)}, f32[40,512]{1,0:T(8,128)S(1)}, u32[]{:S(2)}, u32[]{:S(2)}) collective-permute-start(f32[40,512]{1,0:T(8,128)S(1)} %add.115), channel_id=1, source_target_pairs={{0,2},{1,3},{2,0},{3,1},{4,6},{5,7},{6,4},{7,5},{8,10},{9,11},{10,... | collective-permute-start | bytes 245768 | tf_op jit(solution)/shard_map/ppermute | solution.py:312
  29.9 5.4 %collective-permute-start.4 = (f32[40,512]{1,0:T(8,128)S(1)}, f32[40,512]{1,0:T(8,128)S(1)}, u32[]{:S(2)}, u32[]{:S(2)}) collective-permute-start(f32[40,512]{1,0:T(8,128)S(1)} %add_add_fusion.1), channel_id=1, source_target_pairs={{0,8},{1,9},{2,10},{3,11},{4,12},{5,13},{6,14},{7,15},{8,0},{9,1},... | collective-permute-start | bytes 245768 | tf_op jit(solution)/shard_map/ppermute | solution.py:312
  47.6 6.0 %collective-permute-start.8 = (f32[40,512]{1,0:T(8,128)S(1)}, f32[40,512]{1,0:T(8,128)S(1)}, u32[]{:S(2)}, u32[]{:S(2)}) collective-permute-start(f32[40,512]{1,0:T(8,128)S(1)} %add.120), channel_id=1, source_target_pairs={{0,6},{1,7},{2,4},{3,5},{4,2},{5,3},{6,0},{7,1},{8,14},{9,15},{10,... | collective-permute-start | bytes 245768 | tf_op jit(solution)/shard_map/ppermute | solution.py:312
  49.4 4.7 %collective-permute-start.7 = (f32[40,512]{1,0:T(8,128)S(1)}, f32[40,512]{1,0:T(8,128)S(1)}, u32[]{:S(2)}, u32[]{:S(2)}) collective-permute-start(f32[40,512]{1,0:T(8,128)S(1)} %add.120), channel_id=1, source_target_pairs={{0,4},{1,5},{2,6},{3,7},{4,0},{5,1},{6,2},{7,3},{8,12},{9,13},{10,... | collective-permute-start | bytes 245768 | tf_op jit(solution)/shard_map/ppermute | solution.py:312
  49.9 4.9 %collective-permute-start.6 = (f32[40,512]{1,0:T(8,128)S(1)}, f32[40,512]{1,0:T(8,128)S(1)}, u32[]{:S(2)}, u32[]{:S(2)}) collective-permute-start(f32[40,512]{1,0:T(8,128)S(1)} %add.120), channel_id=1, source_target_pairs={{0,2},{1,3},{2,0},{3,1},{4,6},{5,7},{6,4},{7,5},{8,10},{9,11},{10,... | collective-permute-start | bytes 245768 | tf_op jit(solution)/shard_map/ppermute | solution.py:312
  54.8 7.2 %collective-permute-start.9 = (f32[40,512]{1,0:T(8,128)S(1)}, f32[40,512]{1,0:T(8,128)S(1)}, u32[]{:S(2)}, u32[]{:S(2)}) collective-permute-start(f32[40,512]{1,0:T(8,128)S(1)} %add_add_fusion), channel_id=1, source_target_pairs={{0,8},{1,9},{2,10},{3,11},{4,12},{5,13},{6,14},{7,15},{8,0},{9,1},... | collective-permute-start | bytes 245768 | tf_op jit(solution)/shard_map/ppermute | solution.py:312
  75.6 5.8 %collective-permute-start.13 = (f32[32,512]{1,0:T(8,128)S(1)}, f32[32,512]{1,0:T(8,128)S(1)}, u32[]{:S(2)}, u32[]{:S(2)}) collective-permute-start(f32[32,512]{1,0:T(8,128)S(1)} %add.125), channel_id=1, source_target_pairs={{0,6},{1,7},{2,4},{3,5},{4,2},{5,3},{6,0},{7,1},{8,14},{9,15},{10,... | collective-permute-start | bytes 196616 | tf_op jit(solution)/shard_map/ppermute | solution.py:312
  76.3 5.2 %collective-permute-start.12 = (f32[32,512]{1,0:T(8,128)S(1)}, f32[32,512]{1,0:T(8,128)S(1)}, u32[]{:S(2)}, u32[]{:S(2)}) collective-permute-start(f32[32,512]{1,0:T(8,128)S(1)} %add.125), channel_id=1, source_target_pairs={{0,4},{1,5},{2,6},{3,7},{4,0},{5,1},{6,2},{7,3},{8,12},{9,13},{10,... | collective-permute-start | bytes 196616 | tf_op jit(solution)/shard_map/ppermute | solution.py:312
  77.9 4.3 %collective-permute-start.11 = (f32[32,512]{1,0:T(8,128)S(1)}, f32[32,512]{1,0:T(8,128)S(1)}, u32[]{:S(2)}, u32[]{:S(2)}) collective-permute-start(f32[32,512]{1,0:T(8,128)S(1)} %add.125), channel_id=1, source_target_pairs={{0,2},{1,3},{2,0},{3,1},{4,6},{5,7},{6,4},{7,5},{8,10},{9,11},{10,... | collective-permute-start | bytes 196616 | tf_op jit(solution)/shard_map/ppermute | solution.py:312
  82.2 5.9 %collective-permute-start.14 = (f32[32,512]{1,0:T(8,128)S(1)}, f32[32,512]{1,0:T(8,128)S(1)}, u32[]{:S(2)}, u32[]{:S(2)}) collective-permute-start(f32[32,512]{1,0:T(8,128)S(1)} %add_add_fusion.3), channel_id=1, source_target_pairs={{0,8},{1,9},{2,10},{3,11},{4,12},{5,13},{6,14},{7,15},{8,0},{9,1},... | collective-permute-start | bytes 196616 | tf_op jit(solution)/shard_map/ppermute | solution.py:312
  101.1 3.1 %collective-permute-start.15 = (f32[32,512]{1,0:T(8,128)}, f32[32,512]{1,0:T(8,128)S(1)}, u32[]{:S(2)}, u32[]{:S(2)}) collective-permute-start(f32[32,512]{1,0:T(8,128)} %get-tuple-element.71), channel_id=1, source_target_pairs={{0,1},{1,0},{2,3},{3,2},{4,5},{5,4},{6,7},{7,6},{8,9},{9,8},{10,11... | collective-permute-start | bytes 196616 | tf_op jit(solution)/shard_map/ppermute | solution.py:312
  104.1 5.9 %collective-permute-start.18 = (f32[32,512]{1,0:T(8,128)S(1)}, f32[32,512]{1,0:T(8,128)S(1)}, u32[]{:S(2)}, u32[]{:S(2)}) collective-permute-start(f32[32,512]{1,0:T(8,128)S(1)} %add.130), channel_id=1, source_target_pairs={{0,6},{1,7},{2,4},{3,5},{4,2},{5,3},{6,0},{7,1},{8,14},{9,15},{10,... | collective-permute-start | bytes 196616 | tf_op jit(solution)/shard_map/ppermute | solution.py:312
  104.7 5.9 %collective-permute-start.17 = (f32[32,512]{1,0:T(8,128)S(1)}, f32[32,512]{1,0:T(8,128)S(1)}, u32[]{:S(2)}, u32[]{:S(2)}) collective-permute-start(f32[32,512]{1,0:T(8,128)S(1)} %add.130), channel_id=1, source_target_pairs={{0,4},{1,5},{2,6},{3,7},{4,0},{5,1},{6,2},{7,3},{8,12},{9,13},{10,... | collective-permute-start | bytes 196616 | tf_op jit(solution)/shard_map/ppermute | solution.py:312
  106.8 4.3 %collective-permute-start.16 = (f32[32,512]{1,0:T(8,128)S(1)}, f32[32,512]{1,0:T(8,128)S(1)}, u32[]{:S(2)}, u32[]{:S(2)}) collective-permute-start(f32[32,512]{1,0:T(8,128)S(1)} %add.130), channel_id=1, source_target_pairs={{0,2},{1,3},{2,0},{3,1},{4,6},{5,7},{6,4},{7,5},{8,10},{9,11},{10,... | collective-permute-start | bytes 196616 | tf_op jit(solution)/shard_map/ppermute | solution.py:312
  111.1 5.5 %collective-permute-start.19 = (f32[32,512]{1,0:T(8,128)S(1)}, f32[32,512]{1,0:T(8,128)S(1)}, u32[]{:S(2)}, u32[]{:S(2)}) collective-permute-start(f32[32,512]{1,0:T(8,128)S(1)} %add_add_fusion.2), channel_id=1, source_target_pairs={{0,8},{1,9},{2,10},{3,11},{4,12},{5,13},{6,14},{7,15},{8,0},{9,1},... | collective-permute-start | bytes 196616 | tf_op jit(solution)/shard_map/ppermute | solution.py:312
  127.9 4.5 %collective-permute-start.33 = (f32[8,256]{1,0:T(8,128)S(1)}, f32[8,256]{1,0:T(8,128)S(1)}, u32[]{:S(2)}, u32[]{:S(2)}) collective-permute-start(f32[8,256]{1,0:T(8,128)S(1)} %add.145), channel_id=1, source_target_pairs={{0,6},{1,7},{2,4},{3,5},{4,2},{5,3},{6,0},{7,1},{8,14},{9,15},{10,... | collective-permute-start | bytes 24584 | tf_op jit(solution)/shard_map/ppermute | solution.py:312
  128.2 4.3 %collective-permute-start.32 = (f32[8,256]{1,0:T(8,128)S(1)}, f32[8,256]{1,0:T(8,128)S(1)}, u32[]{:S(2)}, u32[]{:S(2)}) collective-permute-start(f32[8,256]{1,0:T(8,128)S(1)} %add.145), channel_id=1, source_target_pairs={{0,4},{1,5},{2,6},{3,7},{4,0},{5,1},{6,2},{7,3},{8,12},{9,13},{10,... | collective-permute-start | bytes 24584 | tf_op jit(solution)/shard_map/ppermute | solution.py:312
  130.4 3.7 %collective-permute-start.31 = (f32[8,256]{1,0:T(8,128)S(1)}, f32[8,256]{1,0:T(8,128)S(1)}, u32[]{:S(2)}, u32[]{:S(2)}) collective-permute-start(f32[8,256]{1,0:T(8,128)S(1)} %add.145), channel_id=1, source_target_pairs={{0,2},{1,3},{2,0},{3,1},{4,6},{5,7},{6,4},{7,5},{8,10},{9,11},{10,... | collective-permute-start | bytes 24584 | tf_op jit(solution)/shard_map/ppermute | solution.py:312
  134.1 4.7 %collective-permute-start.34 = (f32[8,256]{1,0:T(8,128)S(1)}, f32[8,256]{1,0:T(8,128)S(1)}, u32[]{:S(2)}, u32[]{:S(2)}) collective-permute-start(f32[8,256]{1,0:T(8,128)S(1)} %add_add_fusion.5), channel_id=1, source_target_pairs={{0,8},{1,9},{2,10},{3,11},{4,12},{5,13},{6,14},{7,15},{8,0},{9,1},... | collective-permute-start | bytes 24584 | tf_op jit(solution)/shard_map/ppermute | solution.py:312
  139.5 4.7 %collective-permute-start.25 = (f32[2,32,64]{2,1,0:T(8,128)S(1)}, f32[2,32,64]{2,1,0:T(8,128)S(1)}, u32[]{:S(2)}, u32[]{:S(2)}) collective-permute-start(f32[2,32,64]{2,1,0:T(8,128)S(1)} %pad_maximum_fusion.4), channel_id=1, source_target_pairs={{0,1},{1,0},{2,3},{3,2},{4,5},{5,4},{6,7},{7,6},{8,9},{9,8},{10,11... | collective-permute-start | bytes 49160 | tf_op jit(solution)/shard_map/ppermute | solution.py:312
  140.6 6.2 %collective-permute-start.22 = (f32[2,256]{1,0:T(2,128)S(1)}, f32[2,256]{1,0:T(2,128)S(1)}, u32[]{:S(2)}, u32[]{:S(2)}) collective-permute-start(f32[2,256]{1,0:T(2,128)S(1)} %fusion.1), channel_id=1, source_target_pairs={{0,4},{1,5},{2,6},{3,7},{4,0},{5,1},{6,2},{7,3},{8,12},{9,13},{10,... | collective-permute-start | bytes 6152 | tf_op jit(solution)/shard_map/ppermute | solution.py:312
  140.8 7.0 %collective-permute-start.23 = (f32[2,256]{1,0:T(2,128)S(1)}, f32[2,256]{1,0:T(2,128)S(1)}, u32[]{:S(2)}, u32[]{:S(2)}) collective-permute-start(f32[2,256]{1,0:T(2,128)S(1)} %fusion.1), channel_id=1, source_target_pairs={{0,6},{1,7},{2,4},{3,5},{4,2},{5,3},{6,0},{7,1},{8,14},{9,15},{10,... | collective-permute-start | bytes 6152 | tf_op jit(solution)/shard_map/ppermute | solution.py:312
  143.2 4.6 %collective-permute-start.21 = (f32[2,256]{1,0:T(2,128)S(1)}, f32[2,256]{1,0:T(2,128)S(1)}, u32[]{:S(2)}, u32[]{:S(2)}) collective-permute-start(f32[2,256]{1,0:T(2,128)S(1)} %fusion.1), channel_id=1, source_target_pairs={{0,2},{1,3},{2,0},{3,1},{4,6},{5,7},{6,4},{7,5},{8,10},{9,11},{10,... | collective-permute-start | bytes 6152 | tf_op jit(solution)/shard_map/ppermute | solution.py:312
  144.2 5.0 %collective-permute-start.27 = (f32[2,32,64]{2,1,0:T(8,128)S(1)}, f32[2,32,64]{2,1,0:T(8,128)S(1)}, u32[]{:S(2)}, u32[]{:S(2)}) collective-permute-start(f32[2,32,64]{2,1,0:T(8,128)S(1)} %fusion.2), channel_id=1, source_target_pairs={{0,4},{1,5},{2,6},{3,7},{4,0},{5,1},{6,2},{7,3},{8,12},{9,13},{10,... | collective-permute-start | bytes 49160 | tf_op jit(solution)/shard_map/ppermute | solution.py:312
  144.3 6.4 %collective-permute-start.28 = (f32[2,32,64]{2,1,0:T(8,128)S(1)}, f32[2,32,64]{2,1,0:T(8,128)S(1)}, u32[]{:S(2)}, u32[]{:S(2)}) collective-permute-start(f32[2,32,64]{2,1,0:T(8,128)S(1)} %fusion.2), channel_id=1, source_target_pairs={{0,6},{1,7},{2,4},{3,5},{4,2},{5,3},{6,0},{7,1},{8,14},{9,15},{10,... | collective-permute-start | bytes 49160 | tf_op jit(solution)/shard_map/ppermute | solution.py:312
  146.8 4.8 %collective-permute-start.26 = (f32[2,32,64]{2,1,0:T(8,128)S(1)}, f32[2,32,64]{2,1,0:T(8,128)S(1)}, u32[]{:S(2)}, u32[]{:S(2)}) collective-permute-start(f32[2,32,64]{2,1,0:T(8,128)S(1)} %fusion.2), channel_id=1, source_target_pairs={{0,2},{1,3},{2,0},{3,1},{4,6},{5,7},{6,4},{7,5},{8,10},{9,11},{10,... | collective-permute-start | bytes 49160 | tf_op jit(solution)/shard_map/ppermute | solution.py:312
  147.8 5.6 %collective-permute-start.24 = (f32[2,256]{1,0:T(2,128)S(1)}, f32[2,256]{1,0:T(2,128)S(1)}, u32[]{:S(2)}, u32[]{:S(2)}) collective-permute-start(f32[2,256]{1,0:T(2,128)S(1)} %add_add_fusion.6), channel_id=1, source_target_pairs={{0,8},{1,9},{2,10},{3,11},{4,12},{5,13},{6,14},{7,15},{8,0},{9,1},... | collective-permute-start | bytes 6152 | tf_op jit(solution)/shard_map/ppermute | solution.py:312
  151.6 6.1 %collective-permute-start.29 = (f32[2,32,64]{2,1,0:T(8,128)S(1)}, f32[2,32,64]{2,1,0:T(8,128)S(1)}, u32[]{:S(2)}, u32[]{:S(2)}) collective-permute-start(f32[2,32,64]{2,1,0:T(8,128)S(1)} %add_add_fusion.4), channel_id=1, source_target_pairs={{0,8},{1,9},{2,10},{3,11},{4,12},{5,13},{6,14},{7,15},{8,0},{9,1},... | collective-permute-start | bytes 49160 | tf_op jit(solution)/shard_map/ppermute | solution.py:312
  (26 other events, 223.2 us)
Sparse Core Ops, SparseCore 0:
  126.2 134.9 all-reduce.3

commit v2 on v1

--- a/solution.py
+++ b/solution.py
@@ -12,6 +12,7 @@
 F32 = jnp.float32
 BF16 = jnp.bfloat16
 EPS = 1e-05
+MIB = 1024 * 1024
 
 
 def split(a):
@@ -227,31 +228,101 @@
     return d_first, ds, d_mixed, g_out, g_up, g_down
 
 
+def aligned(rows):
+    return -(-rows // 8) * 8
+
+
+def slabs(value):
+    return [value[:, i : i + 256] for i in range(0, value.shape[1], 256)]
+
+
+def scatter(count, pieces, keep, send):
+    me = lax.axis_index("cell")
+    core = lax.rem(me, 2)
+
+    def put(mine, other):
+        for c in range(count):
+            slot = (c ^ me) // 2
+            at = 0
+            for piece in pieces:
+                rows = sum(p.shape[0] for p in piece) // count
+                which, start = divmod(c * rows, piece[0].shape[0])
+                ref = mine if c % 2 == 0 else other
+                ref[slot, at : at + rows] = piece[which][start : start + rows]
+                at += aligned(rows)
+
+    pl.when(core == 0)(lambda: put(keep, send))
+    pl.when(core == 1)(lambda: put(send, keep))
+
+
+def gather(count, own, other, pieces):
+    me = lax.axis_index("cell")
+    core = lax.rem(me, 2)
+
+    def take(mine, theirs):
+        for c in range(count):
+            slot = (c ^ me) // 2
+            at = 0
+            for rows, targets in pieces:
+                each = rows // count
+                which, start = divmod(c * each, rows // len(targets))
+                src = mine if c % 2 == 0 else theirs
+                targets[which](start, src[slot, at : at + each])
+                at += aligned(each)
+
+    pl.when(core == 0)(lambda: take(own, other))
+    pl.when(core == 1)(lambda: take(other, own))
+
+
+def into(ref, layer, column, base=0):
+    def write(start, value):
+        start = base + start
+        ref[layer, start : start + value.shape[0], column : column + 256] = value
+
+    return write
+
+
+def rows_of(ref):
+    def write(start, value):
+        ref[start : start + value.shape[0]] = value
+
+    return write
+
+
 def store(refs, values):
     for ref, value in zip(refs, values, strict=True):
         ref[...] = value
 
 
+def pack_small(g_temp, g_slice, g_head, hm):
+    dh, m = g_slice.shape
+    width = g_temp.shape[1]
+    left = jnp.concatenate([g_temp, g_head, jnp.zeros((8 - 3, width), F32)], axis=0)
+    run = dh // 8
+    right = jnp.concatenate([g_slice[i * 8 : i * 8 + 8] for i in range(run)], axis=1)
+    return left, right
+
+
 def kernel_a(live, field, w_in, w_temp, w_slice, *out):
-    store(out, front(field[...], w_in[...], w_temp[...], w_slice[...], live[0]))
-
-
-def kernel_b(live, packed, field, s, w_qkv, w_out, w_up, w_down, w_in, w_temp, w_slice, *out):
-    mixed = middle(packed[...], w_qkv[...])[-1]
+    store(out, front(field[...], w_in[...], w_temp[0:1], w_slice[...], live[0]))
+
+
+def kernel_b(live, pa, pb, field, s, w_qkv, w_out, w_up, w_down, w_in, w_temp, w_slice, *out):
+    mixed = middle(pa[...] + pb[...], w_qkv[...])[-1]
     f1, des, n1, rstd1, pre = rear(field[...], s[...], mixed, w_out[...], w_up[...], w_down[...])
     store(out[:5], (mixed, des, n1, rstd1, pre))
     out[5][...] = f1
-    store(out[6:], front(f1, w_in[...], w_temp[...], w_slice[...], live[0]))
-
-
-def kernel_c(live, packed, field, s, w_qkv, w_out, w_up, w_down, w_head, cot, *out):
-    pred, g_head, d_first, ds, d_mixed, g_out, g_up, g_down = out
-    n = field.shape[0]
-    mixed = middle(packed[...], w_qkv[...])[-1]
+    store(out[6:], front(f1, w_in[...], w_temp[1:2], w_slice[...], live[0]))
+
+
+def kernel_c(count, live, pa, pb, field, s, w_qkv, w_out, w_up, w_down, w_head, cot, *out):
+    pred, g_head, d_first, ds, d_mixed, keep, send = out
+    n, width = field.shape
+    mixed = middle(pa[...] + pb[...], w_qkv[...])[-1]
     s = s[...]
     f2, des, n1, rstd1, pre = rear(field[...], s, mixed, w_out[...], w_up[...], w_down[...])
     n2, rstd2 = norm(f2)
-    wh = w_head[...]
+    wh = jnp.concatenate([w_head[...], jnp.zeros((6, width), F32)], axis=0)
     n2s = split(n2)
     pred[...] = nt(wh, n2s)[:2]
     lanes = lax.broadcasted_iota(jnp.int32, cot.shape, 1)
@@ -259,71 +330,409 @@
     dp = jnp.concatenate([dp, jnp.zeros((6, n), F32)], axis=0)
     g_head[...] = nn(dp, n2s)
     g = norm_back(tn(dp, wh), n2, rstd2)
-    store(
-        (d_first, ds, d_mixed, g_out, g_up, g_down),
-        rear_back(g, s, mixed, des, n1, rstd1, pre, w_out[...], w_up[...], w_down[...]),
-    )
+    d_first[...], ds[...], d_mixed[...], g_out, g_up, g_down = rear_back(
+        g, s, mixed, des, n1, rstd1, pre, w_out[...], w_up[...], w_down[...]
+    )
+    halves = [g_out[: width // 2], g_out[width // 2 :]]
+    scatter(count, [[g_down], [halves[0]], slabs(g_up), [halves[1]]], keep, send)
 
 
 def kernel_d(
-    packed, d_mixed, w_qkv, d_first, ds, s, proj, nf, rstd, logits, r, rs, w_in, w_temp, w_slice,
-    s0, mixed0, des0, n10, rstd10, pre0, w_out0, w_up0, w_down0, *out,
+    count, pa, pb, ma, mb, w_qkv, g_head, d_first, ds, s, proj, nf, rstd, logits, r, rs,
+    w_in, w_temp, w_slice, s0, mixed0, des0, n10, rstd10, pre0, w_out0, w_up0, w_down0,
+    g_qkv, ds0, d_mixed0, keep, send,
 ):
-    g_qkv, d_numer, d_denom = middle_back(packed[...], w_qkv[...], d_mixed[...])
+    width = nf.shape[1]
+    g_qkv[...], d_numer, d_denom = middle_back(pa[...] + pb[...], w_qkv[...], ma[...] + mb[...])
     d_proj, g_in, g_temp, g_slice = front_back(
         ds[...], d_numer, d_denom, s[...], proj[...], nf[...], logits[...], r[...], rs[...],
-        w_in[...], w_temp[...], w_slice[...],
-    )
-    store(out[:4], (g_qkv, g_in, g_temp, g_slice))
+        w_in[...], w_temp[1:2], w_slice[...],
+    )
     g = d_first[...] + norm_back(nt(d_proj, w_in[...]), nf[...], rstd[...])
-    _, ds0, d_mixed0, g_out, g_up, g_down = rear_back(
+    _, ds0[...], d_mixed, g_out, g_up, g_down = rear_back(
         g, s0[...], mixed0[...], des0[...], n10[...], rstd10[...], pre0[...],
         w_out0[...], w_up0[...], w_down0[...],
     )
-    store(out[4:], (ds0, d_mixed0, g_out, g_up, g_down))
-
-
-def kernel_e(packed, d_mixed, w_qkv, ds, s, proj, nf, logits, r, rs, w_in, w_temp, w_slice, *out):
-    g_qkv, d_numer, d_denom = middle_back(packed[...], w_qkv[...], d_mixed[...])
+    left, right = pack_small(g_temp, g_slice, g_head[:2], None)
+    d_mixed0[...] = jnp.concatenate([d_mixed, jnp.concatenate([left, right], axis=1)], axis=0)
+    halves = [g_out[: width // 2], g_out[width // 2 :]]
+    ins = slabs(g_in)
+    scatter(
+        count, [[g_down], [halves[0]], [ins[0]], slabs(g_up), [halves[1]], [ins[1]]], keep, send
+    )
+
+
+def kernel_e(
+    count, pa, pb, ma, mb, w_qkv, ds, s, proj, nf, logits, r, rs, w_in, w_temp, w_slice,
+    g_qkv, small, keep, send,
+):
+    dh = w_qkv.shape[0]
+    dm = ma[...] + mb[...]
+    small[...] = dm[dh:]
+    g_qkv[...], d_numer, d_denom = middle_back(pa[...] + pb[...], w_qkv[...], dm[:dh])
     _, g_in, g_temp, g_slice = front_back(
         ds[...], d_numer, d_denom, s[...], proj[...], nf[...], logits[...], r[...], rs[...],
-        w_in[...], w_temp[...], w_slice[...],
-    )
-    store(out, (g_qkv, g_in, g_temp, g_slice))
+        w_in[...], w_temp[0:1], w_slice[...],
+    )
+    left, right = pack_small(g_temp, g_slice, jnp.zeros((2, g_temp.shape[1]), F32), None)
+    rest = jnp.zeros((8 * count - 16, g_temp.shape[1]), F32)
+    ins = slabs(g_in)
+    scatter(
+        count, [[ins[0]], [jnp.concatenate([left, right, rest], axis=0)], [ins[1]]], keep, send
+    )
+
+
+def kernel_f(
+    count, own1, oth1, own2, oth2, own3, oth3, gq0, gq1, small1,
+    g_in, g_temp, g_slice, g_qkv, g_out, g_up, g_down, g_head, small0,
+):
+    width = g_out.shape[1]
+    dh, m = g_slice.shape[1:]
+    ff = g_up.shape[2]
+
+    def down(l):
+        return ff, [into(g_down, l, 0)]
+
+    def up(l):
+        return width * (ff // 256), [into(g_up, l, i) for i in range(0, ff, 256)]
+
+    def out(l, part):
+        return width // 2, [into(g_out, l, 0, part * (width // 2))]
+
+    def ins(l, part):
+        return width, [into(g_in, l, part * width)]
+
+    gather(count, own1, oth1, [down(1), out(1, 0), up(1), out(1, 1)])
+    gather(count, own2, oth2, [down(0), out(0, 0), ins(1, 0), up(0), out(0, 1), ins(1, 1)])
+    gather(count, own3, oth3, [ins(0, 0), (8 * count, [rows_of(small0)]), ins(0, 1)])
+    g_qkv[0] = gq0[...]
+    g_qkv[1] = gq1[...]
+    for l, (left, right) in enumerate(
+        ((small0[:8], small0[8:16]), (small1[:, :width], small1[:, width:]))
+    ):
+        g_temp[l : l + 1] = sum(left[:1, h * dh : (h + 1) * dh] for h in range(H))
+        for i in range(dh // 8):
+            g_slice[l, i * 8 : i * 8 + 8] = right[:, i * m : (i + 1) * m]
+    g_head[...] = small1[1:3, :width]
 
 
 VM = pl.BlockSpec(memory_space=pltpu.VMEM)
 SM = pl.BlockSpec(memory_space=pltpu.SMEM)
-
-
-def call(body, shapes, *args, name):
-    specs = [SM if a.dtype == jnp.int32 else VM for a in args]
+HBM = pl.BlockSpec(memory_space=pltpu.HBM)
+
+
+class Fetched:
+    def __init__(self, source, target, sem):
+        self.copy = pltpu.make_async_copy(source, target, sem)
+        self.copy.start()
+        self.target, self.waiting = target, True
+        self.shape = target.shape
+
+    def finish(self):
+        if self.waiting:
+            self.copy.wait()
+            self.waiting = False
+
+    def __getitem__(self, index):
+        self.finish()
+        return self.target[index]
+
+
+class Emitted:
+    def __init__(self, source, target, sem):
+        self.copy = pltpu.make_async_copy(source, target, sem)
+        self.source, self.started = source, False
+        self.shape = source.shape
+
+    def __setitem__(self, index, value):
+        self.source[index] = value
+        if index is Ellipsis:
+            self.start()
+
+    def start(self):
+        self.copy.start()
+        self.started = True
+
+    def finish(self):
+        if not self.started:
+            self.copy.start()
+        self.copy.wait()
+
+
+class Far:
+    def __init__(self, what, layer=None):
+        self.what, self.layer = what, layer
+
+
+def call(body, shapes, *args, name, scratch=(), flops=2e9, vmem=24, final=False):
+    specs, arrays, held, far_in, far_out, out_specs, out_shapes = [], [], [], [], [], [], []
+    for a in args:
+        if isinstance(a, Far):
+            far_in.append((len(arrays), a.layer))
+            held.append(pltpu.VMEM(a.what.shape if a.layer is None else a.what.shape[1:], F32))
+            specs.append(HBM)
+            a = pltpu.with_memory_space_constraint(a.what, pltpu.HBM)
+        else:
+            specs.append(SM if a.dtype == jnp.int32 else VM)
+            if a.dtype != jnp.int32:
+                a = pltpu.with_memory_space_constraint(a, pltpu.VMEM)
+        arrays.append(a)
+    for s in shapes:
+        if isinstance(s, Far):
+            far_out.append(len(arrays) + len(out_shapes))
+            held.append(pltpu.VMEM(s.what, F32))
+            s = s.what
+            out_specs.append(HBM)
+            out_shapes.append(pltpu.HBM(s, F32))
+        else:
+            out_specs.append(VM)
+            out_shapes.append(jax.ShapeDtypeStruct(s, F32) if final else pltpu.VMEM(s, F32))
+    count = len(arrays) + len(shapes)
+    copies = len(held)
+
+    def whole(*refs):
+        own, extra = list(refs[:count]), refs[count:]
+        moved = []
+        for at, layer in far_in:
+            i = len(moved)
+            source = own[at] if layer is None else own[at].at[layer]
+            own[at] = Fetched(source, extra[i], extra[copies].at[i])
+            moved.append(own[at])
+        for at in far_out:
+            i = len(moved)
+            own[at] = Emitted(extra[i], own[at], extra[copies].at[i])
+            moved.append(own[at])
+        body(*own, *extra[copies + bool(copies) :])
+        for m in moved:
+            m.finish()
+
+    if held:
+        held.append(pltpu.SemaphoreType.DMA((copies,)))
     return pl.pallas_call(
-        body,
-        out_shape=[jax.ShapeDtypeStruct(s, F32) for s in shapes],
+        whole,
+        out_shape=out_shapes,
         in_specs=specs,
-        out_specs=[VM] * len(shapes),
-        compiler_params=pltpu.CompilerParams(vmem_limit_bytes=56 * 1024 * 1024),
+        out_specs=out_specs,
+        scratch_shapes=held + list(scratch),
+        compiler_params=pltpu.CompilerParams(vmem_limit_bytes=vmem * MIB),
+        cost_estimate=pl.CostEstimate(
+            flops=int(flops), bytes_accessed=int(flops / 100), transcendentals=0
+        ),
         name=name,
-    )(*args)
+    )(*arrays)
 
 
 def swap(a, bit, count):
     return lax.ppermute(a, "cell", [(i, i ^ bit) for i in range(count)])
 
 
+def masks_of(group):
+    masks = [0]
+    for bit in group:
+        masks += [m | bit for m in masks]
+    return masks
+
+
+def pairs(count):
+    bits = [1 << i for i in range(1, count.bit_length() - 1)]
+    return [tuple(bits[i : i + 2]) for i in range(0, len(bits), 2)]
+
+
+class Small:
+    def __init__(self, a, count):
+        self.a, self.count = a, count
+        self.groups = [(1,)] + pairs(count)
+
+    def launch(self):
+        self.come = [swap(self.a, m, self.count) for m in masks_of(self.groups[0])[1:]]
+
+    def job(self):
+        def add(a, *come):
+            if len(come) == 1:
+                return [a + come[0]]
+            return [(a + come[0]) + (come[1] + come[2])]
+
+        return add, [self.a, *self.come]
+
+    def take(self, values):
+        (self.a,) = values
+        self.groups = self.groups[1:]
+
+    @property
+    def last(self):
+        return len(self.groups) == 1
+
+    def parts(self):
+        if len(self.come) == 1:
+            return self.a, self.come[0]
+        return self.a + self.come[0], self.come[1] + self.come[2]
+
+
+class Chunks:
+    def __init__(self, keep, send, a_rows, count):
+        self.count = count
+        rows = keep.shape[1]
+        groups = pairs(count)
+        bits = sorted((b for g in groups for b in g), reverse=True)
+        if a_rows is None:
+            self.sizes, plans = [rows], [groups]
+        else:
+            self.sizes = [a_rows, rows - a_rows]
+            plans = [[(b,) for g in groups for b in g], [(b,) for g in groups for b in g[::-1]]]
+        self.stages = list(zip(*plans))
+        self.at, self.phase = 0, "core"
+        self.have, self.sends = [keep], [[(send, 1)]]
+        self.left = [list(bits) for _ in self.sizes]
+        self.bits = bits
+
+    def launch(self):
+        self.come = [[swap(a, m, self.count) for a, m in sends] for sends in self.sends]
+
+    @property
+    def done(self):
+        return self.phase == "done"
+
+    def job(self):
+        sizes, left, phase, at, stages = self.sizes, self.left, self.phase, self.at, self.stages
+        shapes = [len(c) for c in self.come]
+        flat = [x for h, c in zip(self.have, self.come) for x in (h, *c)]
+
+        def unflatten(flat):
+            flat, out = list(flat), []
+            for k in shapes:
+                out.append((flat[0], flat[1 : k + 1]))
+                flat = flat[k + 1 :]
+            return out
+
+        def rows_split(parts):
+            if len(parts) == len(sizes):
+                return parts
+            a = sizes[0]
+            return [parts[0][..., :a, :], parts[0][..., a:, :]]
+
+        def cut(parts, stage):
+            out = []
+            same = len(parts) == 2 and stage[0] == stage[1]
+            if same:
+                parts = [jnp.concatenate(parts, axis=-2)]
+            for p, l, group in zip(parts, left, stage):
+                for mask in masks_of(group):
+                    piece, rest = p, list(l)
+                    for bit in group:
+                        axis = rest.index(bit)
+                        piece = lax.index_in_dim(piece, int(mask & bit > 0), axis, keepdims=False)
+                        rest.remove(bit)
+                    out.append(piece)
+            return out
+
+        def summed(flat):
+            out = []
+            for h, c in unflatten(flat):
+                for x in c:
+                    h = h + x
+                out.append(h)
+            return out
+
+        def reduce(*flat):
+            parts = summed(flat)
+            if phase == "core":
+                parts = [parts[0].reshape((2,) * len(left[0]) + parts[0].shape[1:])]
+                parts = rows_split(parts)
+            if at < len(stages):
+                return cut(parts, stages[at])
+            return parts
+
+        def gather_one(*flat):
+            out = []
+            stage = stages[at]
+            for (h, c), l, group in zip(unflatten(flat), left, stage):
+                done = list(l)
+                pieces = dict(zip(masks_of(group), (h, *c)))
+                for bit in reversed(group):
+                    done = sorted(done + [bit], reverse=True)
+                    axis = done.index(bit)
+                    pieces = {
+                        m: jnp.stack([v, pieces[m | bit]], axis=axis)
+                        for m, v in pieces.items()
+                        if not m & bit
+                    }
+                out.append(pieces[0])
+            if at == 0:
+                if len(out) == 2:
+                    out = [jnp.concatenate(out, axis=-2)]
+                return [out[0].reshape((-1,) + out[0].shape[-2:])]
+            before = stages[at - 1]
+            if len(out) == 1 and len(sizes) == 2 and before[0] != before[1]:
+                out = rows_split(out)
+            return out
+
+        return (gather_one if phase == "gather" else reduce), flat
+
+    def take(self, values):
+        values = list(values)
+        if self.phase in ("core", "reduce"):
+            if self.at < len(self.stages):
+                stage = self.stages[self.at]
+                self.have, self.sends = [], []
+                same = len(stage) == 2 and stage[0] == stage[1]
+                for group in stage[:1] if same else stage:
+                    masks = masks_of(group)
+                    self.have.append(values[0])
+                    self.sends.append(list(zip(values[1 : len(masks)], masks[1:])))
+                    values = values[len(masks) :]
+                self.left = [[b for b in l if b not in g] for l, g in zip(self.left, stage)]
+                self.at += 1
+                self.phase = "reduce"
+                return
+            self.phase = "gather"
+            self.at -= 1
+        else:
+            stage = self.stages[self.at]
+            self.left = [sorted(l + list(g), reverse=True) for l, g in zip(self.left, stage)]
+            self.at -= 1
+        self.have = values
+        if self.at < 0:
+            self.phase = "last"
+            self.sends = [[(values[0], 1)]]
+        else:
+            stage = self.stages[self.at]
+            self.sends = [
+                [(v, m) for m in masks_of(g)[1:]] for v, g in zip(values, stage)
+            ]
+
+    def result(self):
+        return self.have[0], self.come[0][0]
+
+
+def step(*works, name):
+    jobs = [w.job() for w in works]
+    outs = [jax.eval_shape(lambda *a, fn=fn: fn(*a), *arrays) for fn, arrays in jobs]
+
+    def body(*refs):
+        refs = list(refs)
+        ins, results = refs[: sum(len(a) for _, a in jobs)], refs[sum(len(a) for _, a in jobs) :]
+        for fn, arrays in jobs:
+            values = fn(*[r[...] for r in ins[: len(arrays)]])
+            ins = ins[len(arrays) :]
+            store(results[: len(values)], values)
+            results = results[len(values) :]
+
+    values = call(
+        body, [o.shape for out in outs for o in out], *[a for _, arrays in jobs for a in arrays],
+        name=name, flops=1e8, vmem=12,
+    )
+    for w, out in zip(works, outs):
+        w.take(values[: len(out)])
+        values = values[len(out) :]
+
+
 def sum_small(a, count):
-    a = a + swap(a, 1, count)
-    bit = 2
-    while bit < count:
-        if 2 * bit < count:
-            one, two, both = (swap(a, b, count) for b in (bit, 2 * bit, 3 * bit))
-            a = (a + one) + (two + both)
-            bit *= 4
-        else:
-            a = a + swap(a, bit, count)
-            bit *= 2
-    return a
+    small = Small(a, count)
+    small.launch()
+    while not small.last:
+        step(small, name="add")
+        small.launch()
+    return small.parts()
 
 
 def shards(
@@ -344,58 +753,90 @@
     dh, m = weight_slice.shape[1:]
     ff = expansion_matrix.shape[2]
     hm = H * m
-    wi = [weight_in[l] for l in range(L)]
-    wt = [weight_temp[l : l + 1] for l in range(L)]
-    ws = [weight_slice[l] for l in range(L)]
-    wq = [weight_qkv[l] for l in range(L)]
-    wo = [weight_out[l] for l in range(L)]
-    wu = [expansion_matrix[l] for l in range(L)]
-    wd = [weight_down[l] for l in range(L)]
-    wh = jnp.pad(weight_head.T, ((0, 6), (0, 0)))
-
-    front_shapes = [
-        (dh + 8, hm), (n, hm), (n, 2 * width), (n, width), (n, 1), (n, hm), (n, hm), (n, width),
-    ]
-    rear_shapes = [(dh, hm), (n, width), (n, width), (n, 1), (n, ff)]
-    grad_rear = [(width, width), (width, ff), (ff, width)]
-    grad_front = [(dh, 3 * dh), (width, 2 * width), (1, width), (dh, m)]
+    far = lambda *arrays: [Far(a) for a in arrays]
+    qkv = lambda l: Far(weight_qkv, l)
+    rear_w = lambda l: [Far(w, l) for w in (weight_out, expansion_matrix, weight_down)]
+    front_w = lambda l: [Far(weight_in, l), Far(weight_temp), Far(weight_slice, l)]
+
+    kept = [(n, hm), (n, 2 * width), (n, width), (n, 1), (n, hm), (n, hm), (n, width)]
+    front_shapes = [(dh + 8, hm)] + [Far(s) for s in kept]
+    rear_shapes = [Far(s) for s in [(dh, hm), (n, width), (n, width), (n, 1), (n, ff)]]
+    run = lambda *rows: sum(aligned(r // count) for r in rows)
+    a1 = run(ff, width // 2)
+    a2 = run(ff, width // 2, width)
+    a3 = run(width, 8 * count, width)
+    chunks = lambda rows: [(count // 2, rows, 256)] * 2
+    with_count = lambda body: partial(body, count)
 
     p0, s0, proj0, nf0, _, lg0, r0, rs0 = call(
-        kernel_a, front_shapes, counts, features, wi[0], wt[0], ws[0], name="front0"
+        kernel_a, front_shapes, counts, Far(features), *front_w(0), name="front0"
     )
     p0 = sum_small(p0, count)
     mix0, des0, n10, rd10, pre0, f1, p1, s1, proj1, nf1, rstd1, lg1, r1, rs1 = call(
-        kernel_b, rear_shapes + [(n, width)] + front_shapes,
-        counts, p0, features, s0, wq[0], wo[0], wu[0], wd[0], wi[1], wt[1], ws[1], name="rear0_front1",
+        kernel_b, rear_shapes + [Far((n, width))] + front_shapes,
+        counts, *p0, Far(features), Far(s0), qkv(0), *rear_w(0), *front_w(1), name="rear0_front1",
     )
     p1 = sum_small(p1, count)
-    pred, g_head, d_first, ds1, dm1, go1, gu1, gd1 = call(
-        kernel_c, [(2, n), (8, width), (n, width), (n, hm), (dh, hm)] + grad_rear,
-        counts, p1, f1, s1, wq[1], wo[1], wu[1], wd[1], wh, cotangent, name="rear1_head_back1",
-    )
-    dm1 = sum_small(dm1, count)
-    gq1, gi1, gt1, gs1, ds0, dm0, go0, gu0, gd0 = call(
-        kernel_d, grad_front + [(n, hm), (dh, hm)] + grad_rear,
-        p1, dm1, wq[1], d_first, ds1, s1, proj1, nf1, rstd1, lg1, r1, rs1, wi[1], wt[1], ws[1],
-        s0, mix0, des0, n10, rd10, pre0, wo[0], wu[0], wd[0], name="back_front1_rear0",
-    )
-    dm0 = sum_small(dm0, count)
-    gq0, gi0, gt0, gs0 = call(
-        kernel_e, grad_front,
-        p0, dm0, wq[0], ds0, s0, proj0, nf0, lg0, r0, rs0, wi[0], wt[0], ws[0], name="back_front0",
-    )
-    pair = lambda a, b: jnp.stack([a, b])
-    big = lax.psum(
-        (pair(gi0, gi1), pair(go0, go1), pair(gu0, gu1), pair(gd0, gd1)), "cell"
-    )
-    gt, gs, gh = (
-        sum_small(a, count)
-        for a in (jnp.concatenate([gt0, gt1], axis=0), pair(gs0, gs1), g_head)
-    )
-    gt = gt.reshape(L, H, dh).sum(1)
-    return (
-        pred, big[0], gt, gs, pair(gq0, gq1), big[1], big[2], big[3], gh[:2].T,
-    )
+    pred, g_head, d_first, ds1, dm, keep, send = call(
+        with_count(kernel_c),
+        [Far((2, n)), (8, width), (n, width), (n, hm), (dh, hm)] + chunks(2 * a1),
+        counts, *p1, Far(f1), Far(s1), qkv(1), *rear_w(1), Far(weight_head.T), Far(cotangent),
+        name="rear1_head_back1",
+    )
+
+    dm = Small(dm, count)
+    first = Chunks(keep, send, a1, count)
+    dm.launch()
+    first.launch()
+    step(dm, name="add")
+    while not dm.last:
+        dm.launch()
+        step(dm, first, name="add_chunks")
+        first.launch()
+    dm.launch()
+
+    gq1, ds0, dm0, keep, send = call(
+        with_count(kernel_d), [(dh, 3 * dh), (n, hm), (dh + 8, hm)] + chunks(2 * a2),
+        *p1, *dm.parts(), qkv(1), g_head, d_first, ds1, *far(s1, proj1, nf1, rstd1, lg1, r1, rs1),
+        *front_w(1), *far(s0, mix0, des0, n10, rd10, pre0), *rear_w(0), name="back_front1_rear0",
+    )
+
+    dm = Small(dm0, count)
+    second = Chunks(keep, send, a2, count)
+    dm.launch()
+    second.launch()
+    while not dm.last:
+        step(dm, first, second, name="add_chunks")
+        dm.launch()
+        first.launch()
+        second.launch()
+
+    gq0, small1, keep, send = call(
+        with_count(kernel_e), [(dh, 3 * dh), (8, hm)] + chunks(a3),
+        *p0, *dm.parts(), qkv(0), ds0, *far(s0, proj0, nf0, lg0, r0, rs0), *front_w(0),
+        name="back_front0",
+    )
+    third = Chunks(keep, send, None, count)
+    third.launch()
+    works = [first, second, third]
+    while True:
+        busy = [w for w in works if w.phase != "last"]
+        if not busy:
+            break
+        step(*busy, name="chunks")
+        for w in busy:
+            w.launch()
+
+    *grads, g_head = call(
+        with_count(kernel_f),
+        [
+            (L, width, 2 * width), (L, dh), (L, dh, m), (L, dh, 3 * dh), (L, width, width),
+            (L, width, ff), (L, ff, width), (2, width),
+        ],
+        *first.result(), *second.result(), *third.result(), gq0, gq1, small1,
+        name="place_gradients", scratch=[pltpu.VMEM((8 * count, 256), F32)], final=True,
+    )
+    return (pred, *grads, g_head.T)
 
 
 def solution(mesh):

time: 277 us -> 200 us (0.72)
  waiting for transfers between devices: 147 us -> 101 us
  local copies, waits for them, and re-layouts: 18.7 us -> 0 us
  starting transfers between devices: 38.2 us -> 55 us
  other arithmetic: 14.3 us -> 0 us
  between operations: 15.1 us -> 1.53 us
    psum x1 -> x0, waiting for transfers between devices: 103 us -> none  [shards(): lax.psum((pair(gi0, gi1), pair(go0, go1), pair(gu0, gu1), pair(gd0, gd1))...]
    ppermute x35 -> x54, waiting for transfers between devices: 44.1 us -> 101 us  [swap(): return lax.ppermute(a, 'cell', [(i, i ^ bit) for i in range(count)])]
    ppermute x35 -> x54, starting transfers between devices: 38.2 us -> 55 us  [swap(): return lax.ppermute(a, 'cell', [(i, i ^ bit) for i in range(count)])]
    unnamed x48 -> x0, local copies, waits for them, and re-layouts: 8.66 us -> none
    squeeze x6 -> x0, local copies, waits for them, and re-layouts: 8.01 us -> none  [the longest x1 2.25 us: shards(): wi = [weight_in[l] for l in range(L)]]
    another operation x6 -> x0, other arithmetic: 7.98 us -> none  [shards(): pair = lambda a, b: jnp.stack([a, b])]
    add x20 -> x0, other arithmetic: 5.11 us -> none  [the longest x6 3.19 us: sum_small(): a = a + swap(a, bit, count)]
    pallas_call x5 -> x19, Pallas kernels: 42.8 us -> 42.4 us  [call(): pl.pallas_call(whole, out_shape=out_shapes, in_specs=specs, out_specs=out...]
  transfers between devices with their start and end apart: 36 -> 54, of which waited for: 28 -> 31; matrix products, arithmetic and copies ran while one was open for 5% -> 0% of each run, Pallas kernels for 0% -> 0%
where the time goes in v2:
time: 200 us
  waiting for transfers between devices  101 us (50%)
  starting transfers between devices  55 us (28%)
  Pallas kernels  42.4 us (21%)
    ppermute x54, waiting for transfers between devices, swap(): return lax.ppermute(a, 'cell', [(i, i ^ bit) for i in range(count)])  101 us
    ppermute x54, starting transfers between devices, swap(): return lax.ppermute(a, 'cell', [(i, i ^ bit) for i in range(count)])  55 us
    pallas_call x19, Pallas kernels, call(): pl.pallas_call(whole, out_shape=out_shapes, in_specs=specs, out_specs=out...  42.4 us
  transfers between devices with their start and end apart: 54, of which 31 were waited for; matrix products, arithmetic and copies ran while one was open for 0% of the time, Pallas kernels for 0%

profile of v2, /device:TPU:0, one launch (start us, length us, event | category | flops | bytes accessed | tf_op | source)
XLA Modules:
  0.0 199.5 jit_solution(17108989152619751729)
XLA Ops:
  1.3 4.6 %front0.1 = (f32[40,512]{1,0:T(8,128)S(1)}, f32[256,512]{1,0:T(8,128)}, f32[256,512]{1,0:T(8,128)}, f32[256,256]{1,0:T(8,128)}, f32[256,1]{1,0:T(8,128)}, /*inde...) custom-call(s32[1]{0:T(128)S(6)} %copy.20.refs_0_, f32[256,256]{1,0:T(8,128)} %refs_3_.3, ...), custom_call_target="tpu_custom_call" | custom-call | flops 2000000000 | bytes 20000000 | tf_op jit(solution)/shard_map/front0/pallas_call | solution.py:511
  7.4 3.9 %collective-permute-start.3 = (f32[40,512]{1,0:T(8,128)S(1)}, f32[40,512]{1,0:T(8,128)S(1)}, u32[]{:S(2)}, u32[]{:S(2)}) collective-permute-start(f32[40,512]{1,0:T(8,128)S(1)} %add.5.refs_0_), channel_id=1, source_target_pairs={{0,6},{1,7},{2,4},{3,5},{4,2},{5,3},{6,0},{7,1},{8,14},{9,15},{10,... | collective-permute-start | bytes 245768 | tf_op jit(solution)/shard_map/ppermute | solution.py:526
  12.0 2.5 %collective-permute-done.3.refs_3_ = f32[40,512]{1,0:T(8,128)S(1)} collective-permute-done((f32[40,512]{1,0:T(8,128)S(1)}, f32[40,512]{1,0:T(8,128)S(1)}, u32[]{:S(2)}, u32[]{:S(2)}) %collective-permute-start.3) | collective-permute-done | bytes 81952 | tf_op jit(solution)/shard_map/ppermute | solution.py:526
  16.3 2.7 %collective-permute-start.4 = (f32[40,512]{1,0:T(8,128)S(1)}, f32[40,512]{1,0:T(8,128)S(1)}, u32[]{:S(2)}, u32[]{:S(2)}) collective-permute-start(f32[40,512]{1,0:T(8,128)S(1)} %add.6.refs_1_.refs_0_), channel_id=1, source_target_pairs={{0,8},{1,9},{2,10},{3,11},{4,12},{5,13},{6,14},{7,15},{8,0},{9,1},... | collective-permute-start | bytes 245768 | tf_op jit(solution)/shard_map/ppermute | solution.py:526
  18.9 2.9 %collective-permute-done.4.refs_2_.refs_1_ = f32[40,512]{1,0:T(8,128)S(1)} collective-permute-done((f32[40,512]{1,0:T(8,128)S(1)}, f32[40,512]{1,0:T(8,128)S(1)}, u32[]{:S(2)}, u32[]{:S(2)}) %collective-permute-start.4) | collective-permute-done | bytes 81952 | tf_op jit(solution)/shard_map/ppermute | solution.py:526
  21.8 8.8 %rear0_front1.1 = (f32[32,512]{1,0:T(8,128)}, f32[256,256]{1,0:T(8,128)}, f32[256,256]{1,0:T(8,128)}, f32[256,1]{1,0:T(8,128)}, f32[256,1024]{1,0:T(8,128)}, /*i...) custom-call(s32[1]{0:T(128)S(6)} %copy.20.refs_0_, ...), custom_call_target="tpu_custom_call" | custom-call | flops 2000000000 | bytes 20000000 | tf_op jit(solution)/shard_map/rear0_front1/pallas_call | solution.py:511
  32.0 2.6 %collective-permute-start.8 = (f32[40,512]{1,0:T(8,128)S(1)}, f32[40,512]{1,0:T(8,128)S(1)}, u32[]{:S(2)}, u32[]{:S(2)}) collective-permute-start(f32[40,512]{1,0:T(8,128)S(1)} %add.7.refs_0_), channel_id=1, source_target_pairs={{0,6},{1,7},{2,4},{3,5},{4,2},{5,3},{6,0},{7,1},{8,14},{9,15},{10,... | collective-permute-start | bytes 245768 | tf_op jit(solution)/shard_map/ppermute | solution.py:526
  38.0 2.4 %collective-permute-done.7.refs_2_ = f32[40,512]{1,0:T(8,128)S(1)} collective-permute-done((f32[40,512]{1,0:T(8,128)S(1)}, f32[40,512]{1,0:T(8,128)S(1)}, u32[]{:S(2)}, u32[]{:S(2)}) %collective-permute-start.7) | collective-permute-done | bytes 81952 | tf_op jit(solution)/shard_map/ppermute | solution.py:526
  42.7 4.2 %collective-permute-done.9.refs_2_.refs_1_ = f32[40,512]{1,0:T(8,128)S(1)} collective-permute-done((f32[40,512]{1,0:T(8,128)S(1)}, f32[40,512]{1,0:T(8,128)S(1)}, u32[]{:S(2)}, u32[]{:S(2)}) %collective-permute-start.9) | collective-permute-done | bytes 81952 | tf_op jit(solution)/shard_map/ppermute | solution.py:526
  47.0 9.9 %rear1_head_back1.1 = (f32[2,256]{1,0:T(2,128)}, f32[8,256]{1,0:T(8,128)S(1)}, f32[256,256]{1,0:T(8,128)S(1)}, f32[256,512]{1,0:T(8,128)S(1)}, f32[32,512]{1,0:T...) custom-call(s32[1]{0:T(128)S(6)} %copy.20.refs_0_, f32[40,512]{1,0:T(8,128)S(1)} %add.8.refs_1_.refs_0_, ...), custom_call_target="tpu_custom_call" | custom-call | flops 2000000000 | bytes 20000000 | tf_op jit(solution)/shard_map/rear1_head_back1/pallas_call | solution.py:511
  57.5 2.4 %collective-permute-done.10.refs_1_ = f32[32,512]{1,0:T(8,128)S(1)} collective-permute-done((f32[32,512]{1,0:T(8,128)S(1)}, f32[32,512]{1,0:T(8,128)S(1)}, u32[]{:S(2)}, u32[]{:S(2)}) %collective-permute-start.10) | collective-permute-done | bytes 65568 | tf_op jit(solution)/shard_map/ppermute | solution.py:526
  60.7 2.7 %collective-permute-start.12 = (f32[32,512]{1,0:T(8,128)S(1)}, f32[32,512]{1,0:T(8,128)S(1)}, u32[]{:S(2)}, u32[]{:S(2)}) collective-permute-start(f32[32,512]{1,0:T(8,128)S(1)} %add.9.refs_0_), channel_id=1, source_target_pairs={{0,4},{1,5},{2,6},{3,7},{4,0},{5,1},{6,2},{7,3},{8,12},{9,13},{10,... | collective-permute-start | bytes 196616 | tf_op jit(solution)/shard_map/ppermute | solution.py:526
  63.5 2.3 %collective-permute-done.13.refs_3_ = f32[32,512]{1,0:T(8,128)S(1)} collective-permute-done((f32[32,512]{1,0:T(8,128)S(1)}, f32[32,512]{1,0:T(8,128)S(1)}, u32[]{:S(2)}, u32[]{:S(2)}) %collective-permute-start.13) | collective-permute-done | bytes 65568 | tf_op jit(solution)/shard_map/ppermute | solution.py:526
  68.6 4.6 %collective-permute-done.15.refs_3_ = f32[32,512]{1,0:T(8,128)S(1)} collective-permute-done((f32[32,512]{1,0:T(8,128)S(1)}, f32[32,512]{1,0:T(8,128)S(1)}, u32[]{:S(2)}, u32[]{:S(2)}) %collective-permute-start.15) | collective-permute-done | bytes 65568 | tf_op jit(solution)/shard_map/ppermute | solution.py:526
  73.2 9.9 %back_front1_rear0.1 = (f32[32,96]{1,0:T(8,128)S(1)}, f32[256,512]{1,0:T(8,128)S(1)}, f32[40,512]{1,0:T(8,128)S(1)}, f32[8,176,256]{2,1,0:T(8,128)S(1)}, f32[8,176,256]{2,1,0:T(8,128)S(1)}) custom-call(f32[40,512]{1,0:T(8,128)S(1)} %add.8.refs_1_.refs_0_, f32[40,512]{1,0:T(8,128)S(1)} %collective-permute-done.9.refs_2_.refs_1_, ...), custom_call_target="tpu_custom_call" | custom-call | flops 2000000000 | bytes 20000000 | tf_op jit(solution)/shard_map/back_front1_rear0/pallas_call | solution.py:511
  84.3 2.2 %collective-permute-done.16.refs_1_ = f32[40,512]{1,0:T(8,128)S(1)} collective-permute-done((f32[40,512]{1,0:T(8,128)S(1)}, f32[40,512]{1,0:T(8,128)S(1)}, u32[]{:S(2)}, u32[]{:S(2)}) %collective-permute-start.16) | collective-permute-done | bytes 81952 | tf_op jit(solution)/shard_map/ppermute | solution.py:526
  86.5 6.1 %collective-permute-done.17.refs_3_ = f32[2,2,72,256]{3,2,1,0:T(8,128)S(1)} collective-permute-done((f32[2,2,72,256]{3,2,1,0:T(8,128)S(1)}, f32[2,2,72,256]{3,2,1,0:T(8,128)S(1)}, u32[]{:S(2)}, u32[]{:S(2)}) %collective-permute-start.17) | collective-permute-done | bytes 294944 | tf_op jit(solution)/shard_map/ppermute | solution.py:526
  99.1 9.1 %collective-permute-done.22.refs_3_ = f32[40,512]{1,0:T(8,128)S(1)} collective-permute-done((f32[40,512]{1,0:T(8,128)S(1)}, f32[40,512]{1,0:T(8,128)S(1)}, u32[]{:S(2)}, u32[]{:S(2)}) %collective-permute-start.22) | collective-permute-done | bytes 81952 | tf_op jit(solution)/shard_map/ppermute | solution.py:526
  110.1 4.0 %collective-permute-done.20.refs_1_ = f32[40,512]{1,0:T(8,128)S(1)} collective-permute-done((f32[40,512]{1,0:T(8,128)S(1)}, f32[40,512]{1,0:T(8,128)S(1)}, u32[]{:S(2)}, u32[]{:S(2)}) %collective-permute-start.20) | collective-permute-done | bytes 81952 | tf_op jit(solution)/shard_map/ppermute | solution.py:526
  115.5 4.8 %collective-permute-done.30.refs_3_ = f32[40,512]{1,0:T(8,128)S(1)} collective-permute-done((f32[40,512]{1,0:T(8,128)S(1)}, f32[40,512]{1,0:T(8,128)S(1)}, u32[]{:S(2)}, u32[]{:S(2)}) %collective-permute-start.30) | collective-permute-done | bytes 81952 | tf_op jit(solution)/shard_map/ppermute | solution.py:526
  120.3 5.0 %back_front0.1 = (f32[32,96]{1,0:T(8,128)S(1)}, f32[8,512]{1,0:T(8,128)S(1)}, f32[8,40,256]{2,1,0:T(8,128)S(1)}, f32[8,40,256]{2,1,0:T(8,128)S(1)}) custom-call(f32[40,512]{1,0:T(8,128)S(1)} %add.6.refs_1_.refs_0_, f32[40,512]{1,0:T(8,128)S(1)} %collective-permute-done.4.refs_2_.refs_1_, f32[40,512]{1,0:T(8,128)S(1)} %get-tuple-element.144.refs_2_, ...), custom_call_target="tpu_custom_call" | custom-call | flops 2000000000 | bytes 20000000 | tf_op jit(solution)/shard_map/back_front0/pallas_call | solution.py:511
  126.7 2.7 %collective-permute-start.27 = (f32[144,256]{1,0:T(8,128)S(1)}, f32[144,256]{1,0:T(8,128)S(1)}, u32[]{:S(2)}, u32[]{:S(2)}) collective-permute-start(f32[144,256]{1,0:T(8,128)S(1)} %get-tuple-element.139), channel_id=1, source_target_pairs={{0,8},{1,9},{2,10},{3,11},{4,12},{5,13},{6,14},{7,15},{8,0},{9,1},... | collective-permute-start | bytes 442376 | tf_op jit(solution)/shard_map/ppermute | solution.py:526
  129.4 7.3 %collective-permute-done.27.refs_1_ = f32[144,256]{1,0:T(8,128)S(1)} collective-permute-done((f32[144,256]{1,0:T(8,128)S(1)}, f32[144,256]{1,0:T(8,128)S(1)}, u32[]{:S(2)}, u32[]{:S(2)}) %collective-permute-start.27) | collective-permute-done | bytes 147488 | tf_op jit(solution)/shard_map/ppermute | solution.py:526
  136.9 2.8 %collective-permute-start.32 = (f32[144,256]{1,0:T(8,128)S(1)}, f32[144,256]{1,0:T(8,128)S(1)}, u32[]{:S(2)}, u32[]{:S(2)}) collective-permute-start(f32[144,256]{1,0:T(8,128)S(1)} %get-tuple-element.153.refs_0_), channel_id=1, source_target_pairs={{0,8},{1,9},{2,10},{3,11},{4,12},{5,13},{6,14},{7,15},{8,0},{9,1},... | collective-permute-start | bytes 442376 | tf_op jit(solution)/shard_map/ppermute | solution.py:526
  140.9 2.3 %collective-permute-start.36 = (f32[2,40,256]{2,1,0:T(8,128)S(1)}, f32[2,40,256]{2,1,0:T(8,128)S(1)}, u32[]{:S(2)}, u32[]{:S(2)}) collective-permute-start(f32[2,40,256]{2,1,0:T(8,128)S(1)} %get-tuple-element.159), channel_id=1, source_target_pairs={{0,6},{1,7},{2,4},{3,5},{4,2},{5,3},{6,0},{7,1},{8,14},{9,15},{10,... | collective-permute-start | bytes 245768 | tf_op jit(solution)/shard_map/ppermute | solution.py:526
  147.3 5.1 %collective-permute-done.32.refs_1_ = f32[144,256]{1,0:T(8,128)S(1)} collective-permute-done((f32[144,256]{1,0:T(8,128)S(1)}, f32[144,256]{1,0:T(8,128)S(1)}, u32[]{:S(2)}, u32[]{:S(2)}) %collective-permute-start.32) | collective-permute-done | bytes 147488 | tf_op jit(solution)/shard_map/ppermute | solution.py:526
  152.5 3.3 %collective-permute-start.37 = (f32[2,72,256]{2,1,0:T(8,128)S(1)}, f32[2,72,256]{2,1,0:T(8,128)S(1)}, u32[]{:S(2)}, u32[]{:S(2)}) collective-permute-start(f32[2,72,256]{2,1,0:T(8,128)S(1)} %get-tuple-element.160.refs_0_), channel_id=1, source_target_pairs={{0,4},{1,5},{2,6},{3,7},{4,0},{5,1},{6,2},{7,3},{8,12},{9,13},{10,... | collective-permute-start | bytes 442376 | tf_op jit(solution)/shard_map/ppermute | solution.py:526
  157.1 7.0 %collective-permute-done.40.refs_7_ = f32[40,256]{1,0:T(8,128)S(1)} collective-permute-done((f32[40,256]{1,0:T(8,128)S(1)}, f32[40,256]{1,0:T(8,128)S(1)}, u32[]{:S(2)}, u32[]{:S(2)}) %collective-permute-start.40) | collective-permute-done | bytes 40992 | tf_op jit(solution)/shard_map/ppermute | solution.py:526
  168.5 7.6 %collective-permute-done.45.refs_9_ = f32[40,256]{1,0:T(8,128)S(1)} collective-permute-done((f32[40,256]{1,0:T(8,128)S(1)}, f32[40,256]{1,0:T(8,128)S(1)}, u32[]{:S(2)}, u32[]{:S(2)}) %collective-permute-start.45) | collective-permute-done | bytes 40992 | tf_op jit(solution)/shard_map/ppermute | solution.py:526
  183.6 7.4 %collective-permute-done.51.refs_7_ = f32[2,40,256]{2,1,0:T(8,128)S(1)} collective-permute-done((f32[2,40,256]{2,1,0:T(8,128)S(1)}, f32[2,40,256]{2,1,0:T(8,128)S(1)}, u32[]{:S(2)}, u32[]{:S(2)}) %collective-permute-start.51) | collective-permute-done | bytes 81952 | tf_op jit(solution)/shard_map/ppermute | solution.py:526
  191.8 4.8 %collective-permute-done.53.refs_5_ = f32[8,40,256]{2,1,0:T(8,128)S(1)} collective-permute-done((f32[8,40,256]{2,1,0:T(8,128)S(1)}, f32[8,40,256]{2,1,0:T(8,128)S(1)}, u32[]{:S(2)}, u32[]{:S(2)}) %collective-permute-start.53) | collective-permute-done | bytes 327712 | tf_op jit(solution)/shard_map/ppermute | solution.py:526
  196.5 3.0 %place_gradients.1 = (f32[2,256,512]{2,1,0:T(8,128)}, f32[2,32]{1,0:T(2,128)}, f32[2,32,64]{2,1,0:T(8,128)}, f32[2,32,96]{2,1,0:T(8,128)}, f32[2,256,256]{2,1,0:...) custom-call(f32[8,144,256]{2,1,0:T(8,128)S(1)} %get-tuple-element.170.refs_0_, ...), custom_call_target="tpu_custom_call" | custom-call | flops 2000000000 | bytes 20000000 | tf_op jit(solution)/shard_map/place_gradients/pallas_call | solution.py:511
  (95 shorter events, 47.1 us)
Async XLA Ops:
  7.4 7.1 %collective-permute-start.3 = (f32[40,512]{1,0:T(8,128)S(1)}, f32[40,512]{1,0:T(8,128)S(1)}, u32[]{:S(2)}, u32[]{:S(2)}) collective-permute-start(f32[40,512]{1,0:T(8,128)S(1)} %add.5.refs_0_), channel_id=1, source_target_pairs={{0,6},{1,7},{2,4},{3,5},{4,2},{5,3},{6,0},{7,1},{8,14},{9,15},{10,... | collective-permute-start | bytes 245768 | tf_op jit(solution)/shard_map/ppermute | solution.py:526
  40.7 6.3 %collective-permute-start.9 = (f32[40,512]{1,0:T(8,128)S(1)}, f32[40,512]{1,0:T(8,128)S(1)}, u32[]{:S(2)}, u32[]{:S(2)}) collective-permute-start(f32[40,512]{1,0:T(8,128)S(1)} %add.8.refs_1_.refs_0_), channel_id=1, source_target_pairs={{0,8},{1,9},{2,10},{3,11},{4,12},{5,13},{6,14},{7,15},{8,0},{9,1},... | collective-permute-start | bytes 245768 | tf_op jit(solution)/shard_map/ppermute | solution.py:526
  56.9 10.8 %collective-permute-start.14 = (f32[8,144,256]{2,1,0:T(8,128)S(1)}, f32[8,144,256]{2,1,0:T(8,128)S(1)}, u32[]{:S(2)}, u32[]{:S(2)}) collective-permute-start(f32[8,144,256]{2,1,0:T(8,128)S(1)} %get-tuple-element.106), channel_id=1, source_target_pairs={{0,1},{1,0},{2,3},{3,2},{4,5},{5,4},{6,7},{7,6},{8,9},{9,8},{10,11... | collective-permute-start | bytes 3538952 | tf_op jit(solution)/shard_map/ppermute | solution.py:526
  83.1 10.1 %collective-permute-start.19 = (f32[8,176,256]{2,1,0:T(8,128)S(1)}, f32[8,176,256]{2,1,0:T(8,128)S(1)}, u32[]{:S(2)}, u32[]{:S(2)}) collective-permute-start(f32[8,176,256]{2,1,0:T(8,128)S(1)} %get-tuple-element.128), channel_id=1, source_target_pairs={{0,1},{1,0},{2,3},{3,2},{4,5},{5,4},{6,7},{7,6},{8,9},{9,8},{10,11... | collective-permute-start | bytes 4325384 | tf_op jit(solution)/shard_map/ppermute | solution.py:526
  83.2 9.4 %collective-permute-start.17 = (f32[2,2,72,256]{3,2,1,0:T(8,128)S(1)}, f32[2,2,72,256]{3,2,1,0:T(8,128)S(1)}, u32[]{:S(2)}, u32[]{:S(2)}) collective-permute-start(f32[2,2,72,256]{3,2,1,0:T(8,128)S(1)} %get-tuple-element.124), channel_id=1, source_target_pairs={{0,2},{1,3},{2,0},{3,1},{4,6},{5,7},{6,4},{7,5},{8,10},{9,11},{10,... | collective-permute-start | bytes 884744 | tf_op jit(solution)/shard_map/ppermute | solution.py:526
  84.1 9.1 %collective-permute-start.18 = (f32[2,2,72,256]{3,2,1,0:T(8,128)S(1)}, f32[2,2,72,256]{3,2,1,0:T(8,128)S(1)}, u32[]{:S(2)}, u32[]{:S(2)}) collective-permute-start(f32[2,2,72,256]{3,2,1,0:T(8,128)S(1)} %get-tuple-element.126), channel_id=1, source_target_pairs={{0,4},{1,5},{2,6},{3,7},{4,0},{5,1},{6,2},{7,3},{8,12},{9,13},{10,... | collective-permute-start | bytes 884744 | tf_op jit(solution)/shard_map/ppermute | solution.py:526
  93.5 20.7 %collective-permute-start.25 = (f32[2,2,88,256]{3,2,1,0:T(8,128)S(1)}, f32[2,2,88,256]{3,2,1,0:T(8,128)S(1)}, u32[]{:S(2)}, u32[]{:S(2)}) collective-permute-start(f32[2,2,88,256]{3,2,1,0:T(8,128)S(1)} %get-tuple-element.135), channel_id=1, source_target_pairs={{0,2},{1,3},{2,0},{3,1},{4,6},{5,7},{6,4},{7,5},{8,10},{9,11},{10,... | collective-permute-start | bytes 1081352 | tf_op jit(solution)/shard_map/ppermute | solution.py:526
  94.7 19.4 %collective-permute-start.26 = (f32[2,2,88,256]{3,2,1,0:T(8,128)S(1)}, f32[2,2,88,256]{3,2,1,0:T(8,128)S(1)}, u32[]{:S(2)}, u32[]{:S(2)}) collective-permute-start(f32[2,2,88,256]{3,2,1,0:T(8,128)S(1)} %get-tuple-element.137), channel_id=1, source_target_pairs={{0,4},{1,5},{2,6},{3,7},{4,0},{5,1},{6,2},{7,3},{8,12},{9,13},{10,... | collective-permute-start | bytes 1081352 | tf_op jit(solution)/shard_map/ppermute | solution.py:526
  95.0 13.1 %collective-permute-start.22 = (f32[40,512]{1,0:T(8,128)S(1)}, f32[40,512]{1,0:T(8,128)S(1)}, u32[]{:S(2)}, u32[]{:S(2)}) collective-permute-start(f32[40,512]{1,0:T(8,128)S(1)} %get-tuple-element.129.refs_0_), channel_id=1, source_target_pairs={{0,6},{1,7},{2,4},{3,5},{4,2},{5,3},{6,0},{7,1},{8,14},{9,15},{10,... | collective-permute-start | bytes 245768 | tf_op jit(solution)/shard_map/ppermute | solution.py:526
  97.0 12.3 %collective-permute-start.21 = (f32[40,512]{1,0:T(8,128)S(1)}, f32[40,512]{1,0:T(8,128)S(1)}, u32[]{:S(2)}, u32[]{:S(2)}) collective-permute-start(f32[40,512]{1,0:T(8,128)S(1)} %get-tuple-element.129.refs_0_), channel_id=1, source_target_pairs={{0,4},{1,5},{2,6},{3,7},{4,0},{5,1},{6,2},{7,3},{8,12},{9,13},{10,... | collective-permute-start | bytes 245768 | tf_op jit(solution)/shard_map/ppermute | solution.py:526
  97.3 16.8 %collective-permute-start.23 = (f32[2,72,256]{2,1,0:T(8,128)S(1)}, f32[2,72,256]{2,1,0:T(8,128)S(1)}, u32[]{:S(2)}, u32[]{:S(2)}) collective-permute-start(f32[2,72,256]{2,1,0:T(8,128)S(1)} %get-tuple-element.131), channel_id=1, source_target_pairs={{0,4},{1,5},{2,6},{3,7},{4,0},{5,1},{6,2},{7,3},{8,12},{9,13},{10,... | collective-permute-start | bytes 442376 | tf_op jit(solution)/shard_map/ppermute | solution.py:526
  125.3 11.3 %collective-permute-start.31 = (f32[8,40,256]{2,1,0:T(8,128)S(1)}, f32[8,40,256]{2,1,0:T(8,128)S(1)}, u32[]{:S(2)}, u32[]{:S(2)}) collective-permute-start(f32[8,40,256]{2,1,0:T(8,128)S(1)} %get-tuple-element.152), channel_id=1, source_target_pairs={{0,1},{1,0},{2,3},{3,2},{4,5},{5,4},{6,7},{7,6},{8,9},{9,8},{10,11... | collective-permute-start | bytes 983048 | tf_op jit(solution)/shard_map/ppermute | solution.py:526
  125.4 11.2 %collective-permute-start.28 = (f32[2,88,256]{2,1,0:T(8,128)S(1)}, f32[2,88,256]{2,1,0:T(8,128)S(1)}, u32[]{:S(2)}, u32[]{:S(2)}) collective-permute-start(f32[2,88,256]{2,1,0:T(8,128)S(1)} %get-tuple-element.141), channel_id=1, source_target_pairs={{0,4},{1,5},{2,6},{3,7},{4,0},{5,1},{6,2},{7,3},{8,12},{9,13},{10,... | collective-permute-start | bytes 540680 | tf_op jit(solution)/shard_map/ppermute | solution.py:526
  125.4 11.2 %collective-permute-start.29 = (f32[2,88,256]{2,1,0:T(8,128)S(1)}, f32[2,88,256]{2,1,0:T(8,128)S(1)}, u32[]{:S(2)}, u32[]{:S(2)}) collective-permute-start(f32[2,88,256]{2,1,0:T(8,128)S(1)} %get-tuple-element.143), channel_id=1, source_target_pairs={{0,2},{1,3},{2,0},{3,1},{4,6},{5,7},{6,4},{7,5},{8,10},{9,11},{10,... | collective-permute-start | bytes 540680 | tf_op jit(solution)/shard_map/ppermute | solution.py:526
  126.7 9.9 %collective-permute-start.27 = (f32[144,256]{1,0:T(8,128)S(1)}, f32[144,256]{1,0:T(8,128)S(1)}, u32[]{:S(2)}, u32[]{:S(2)}) collective-permute-start(f32[144,256]{1,0:T(8,128)S(1)} %get-tuple-element.139), channel_id=1, source_target_pairs={{0,8},{1,9},{2,10},{3,11},{4,12},{5,13},{6,14},{7,15},{8,0},{9,1},... | collective-permute-start | bytes 442376 | tf_op jit(solution)/shard_map/ppermute | solution.py:526
  136.7 15.6 %collective-permute-start.33 = (f32[176,256]{1,0:T(8,128)S(1)}, f32[176,256]{1,0:T(8,128)S(1)}, u32[]{:S(2)}, u32[]{:S(2)}) collective-permute-start(f32[176,256]{1,0:T(8,128)S(1)} %get-tuple-element.155), channel_id=1, source_target_pairs={{0,8},{1,9},{2,10},{3,11},{4,12},{5,13},{6,14},{7,15},{8,0},{9,1},... | collective-permute-start | bytes 540680 | tf_op jit(solution)/shard_map/ppermute | solution.py:526
  136.9 15.4 %collective-permute-start.32 = (f32[144,256]{1,0:T(8,128)S(1)}, f32[144,256]{1,0:T(8,128)S(1)}, u32[]{:S(2)}, u32[]{:S(2)}) collective-permute-start(f32[144,256]{1,0:T(8,128)S(1)} %get-tuple-element.153.refs_0_), channel_id=1, source_target_pairs={{0,8},{1,9},{2,10},{3,11},{4,12},{5,13},{6,14},{7,15},{8,0},{9,1},... | collective-permute-start | bytes 442376 | tf_op jit(solution)/shard_map/ppermute | solution.py:526
  140.9 6.4 %collective-permute-start.36 = (f32[2,40,256]{2,1,0:T(8,128)S(1)}, f32[2,40,256]{2,1,0:T(8,128)S(1)}, u32[]{:S(2)}, u32[]{:S(2)}) collective-permute-start(f32[2,40,256]{2,1,0:T(8,128)S(1)} %get-tuple-element.159), channel_id=1, source_target_pairs={{0,6},{1,7},{2,4},{3,5},{4,2},{5,3},{6,0},{7,1},{8,14},{9,15},{10,... | collective-permute-start | bytes 245768 | tf_op jit(solution)/shard_map/ppermute | solution.py:526
  152.4 11.7 %collective-permute-start.39 = (f32[176,256]{1,0:T(8,128)S(1)}, f32[176,256]{1,0:T(8,128)S(1)}, u32[]{:S(2)}, u32[]{:S(2)}) collective-permute-start(f32[176,256]{1,0:T(8,128)S(1)} %get-tuple-element.162.refs_4_), channel_id=1, source_target_pairs={{0,8},{1,9},{2,10},{3,11},{4,12},{5,13},{6,14},{7,15},{8,0},{9,1},... | collective-permute-start | bytes 540680 | tf_op jit(solution)/shard_map/ppermute | solution.py:526
  152.5 11.6 %collective-permute-start.37 = (f32[2,72,256]{2,1,0:T(8,128)S(1)}, f32[2,72,256]{2,1,0:T(8,128)S(1)}, u32[]{:S(2)}, u32[]{:S(2)}) collective-permute-start(f32[2,72,256]{2,1,0:T(8,128)S(1)} %get-tuple-element.160.refs_0_), channel_id=1, source_target_pairs={{0,4},{1,5},{2,6},{3,7},{4,0},{5,1},{6,2},{7,3},{8,12},{9,13},{10,... | collective-permute-start | bytes 442376 | tf_op jit(solution)/shard_map/ppermute | solution.py:526
  155.8 8.4 %collective-permute-start.38 = (f32[2,72,256]{2,1,0:T(8,128)S(1)}, f32[2,72,256]{2,1,0:T(8,128)S(1)}, u32[]{:S(2)}, u32[]{:S(2)}) collective-permute-start(f32[2,72,256]{2,1,0:T(8,128)S(1)} %get-tuple-element.161.refs_2_), channel_id=1, source_target_pairs={{0,2},{1,3},{2,0},{3,1},{4,6},{5,7},{6,4},{7,5},{8,10},{9,11},{10,... | collective-permute-start | bytes 442376 | tf_op jit(solution)/shard_map/ppermute | solution.py:526
  157.0 7.1 %collective-permute-start.40 = (f32[40,256]{1,0:T(8,128)S(1)}, f32[40,256]{1,0:T(8,128)S(1)}, u32[]{:S(2)}, u32[]{:S(2)}) collective-permute-start(f32[40,256]{1,0:T(8,128)S(1)} %get-tuple-element.164), channel_id=1, source_target_pairs={{0,8},{1,9},{2,10},{3,11},{4,12},{5,13},{6,14},{7,15},{8,0},{9,1},... | collective-permute-start | bytes 122888 | tf_op jit(solution)/shard_map/ppermute | solution.py:526
  164.2 13.3 %collective-permute-start.41 = (f32[2,2,72,256]{3,2,1,0:T(8,128)S(1)}, f32[2,2,72,256]{3,2,1,0:T(8,128)S(1)}, u32[]{:S(2)}, u32[]{:S(2)}) collective-permute-start(f32[2,2,72,256]{3,2,1,0:T(8,128)S(1)} %get-tuple-element.165.refs_0_), channel_id=1, source_target_pairs={{0,2},{1,3},{2,0},{3,1},{4,6},{5,7},{6,4},{7,5},{8,10},{9,11},{10,... | collective-permute-start | bytes 884744 | tf_op jit(solution)/shard_map/ppermute | solution.py:526
  166.0 11.5 %collective-permute-start.42 = (f32[2,2,72,256]{3,2,1,0:T(8,128)S(1)}, f32[2,2,72,256]{3,2,1,0:T(8,128)S(1)}, u32[]{:S(2)}, u32[]{:S(2)}) collective-permute-start(f32[2,2,72,256]{3,2,1,0:T(8,128)S(1)} %get-tuple-element.166.refs_2_), channel_id=1, source_target_pairs={{0,4},{1,5},{2,6},{3,7},{4,0},{5,1},{6,2},{7,3},{8,12},{9,13},{10,... | collective-permute-start | bytes 884744 | tf_op jit(solution)/shard_map/ppermute | solution.py:526
  166.1 11.4 %collective-permute-start.43 = (f32[2,88,256]{2,1,0:T(8,128)S(1)}, f32[2,88,256]{2,1,0:T(8,128)S(1)}, u32[]{:S(2)}, u32[]{:S(2)}) collective-permute-start(f32[2,88,256]{2,1,0:T(8,128)S(1)} %get-tuple-element.167.refs_4_), channel_id=1, source_target_pairs={{0,4},{1,5},{2,6},{3,7},{4,0},{5,1},{6,2},{7,3},{8,12},{9,13},{10,... | collective-permute-start | bytes 540680 | tf_op jit(solution)/shard_map/ppermute | solution.py:526
  168.0 9.5 %collective-permute-start.44 = (f32[2,88,256]{2,1,0:T(8,128)S(1)}, f32[2,88,256]{2,1,0:T(8,128)S(1)}, u32[]{:S(2)}, u32[]{:S(2)}) collective-permute-start(f32[2,88,256]{2,1,0:T(8,128)S(1)} %get-tuple-element.168.refs_6_), channel_id=1, source_target_pairs={{0,2},{1,3},{2,0},{3,1},{4,6},{5,7},{6,4},{7,5},{8,10},{9,11},{10,... | collective-permute-start | bytes 540680 | tf_op jit(solution)/shard_map/ppermute | solution.py:526
  168.3 7.7 %collective-permute-start.45 = (f32[40,256]{1,0:T(8,128)S(1)}, f32[40,256]{1,0:T(8,128)S(1)}, u32[]{:S(2)}, u32[]{:S(2)}) collective-permute-start(f32[40,256]{1,0:T(8,128)S(1)} %get-tuple-element.169.refs_8_), channel_id=1, source_target_pairs={{0,8},{1,9},{2,10},{3,11},{4,12},{5,13},{6,14},{7,15},{8,0},{9,1},... | collective-permute-start | bytes 122888 | tf_op jit(solution)/shard_map/ppermute | solution.py:526
  177.7 13.3 %collective-permute-start.47 = (f32[2,2,88,256]{3,2,1,0:T(8,128)S(1)}, f32[2,2,88,256]{3,2,1,0:T(8,128)S(1)}, u32[]{:S(2)}, u32[]{:S(2)}) collective-permute-start(f32[2,2,88,256]{3,2,1,0:T(8,128)S(1)} %get-tuple-element.171.refs_0_), channel_id=1, source_target_pairs={{0,2},{1,3},{2,0},{3,1},{4,6},{5,7},{6,4},{7,5},{8,10},{9,11},{10,... | collective-permute-start | bytes 1081352 | tf_op jit(solution)/shard_map/ppermute | solution.py:526
  178.1 12.9 %collective-permute-start.48 = (f32[2,2,88,256]{3,2,1,0:T(8,128)S(1)}, f32[2,2,88,256]{3,2,1,0:T(8,128)S(1)}, u32[]{:S(2)}, u32[]{:S(2)}) collective-permute-start(f32[2,2,88,256]{3,2,1,0:T(8,128)S(1)} %get-tuple-element.172.refs_2_), channel_id=1, source_target_pairs={{0,4},{1,5},{2,6},{3,7},{4,0},{5,1},{6,2},{7,3},{8,12},{9,13},{10,... | collective-permute-start | bytes 1081352 | tf_op jit(solution)/shard_map/ppermute | solution.py:526
  180.1 10.9 %collective-permute-start.51 = (f32[2,40,256]{2,1,0:T(8,128)S(1)}, f32[2,40,256]{2,1,0:T(8,128)S(1)}, u32[]{:S(2)}, u32[]{:S(2)}) collective-permute-start(f32[2,40,256]{2,1,0:T(8,128)S(1)} %get-tuple-element.173.refs_4_), channel_id=1, source_target_pairs={{0,6},{1,7},{2,4},{3,5},{4,2},{5,3},{6,0},{7,1},{8,14},{9,15},{10,... | collective-permute-start | bytes 245768 | tf_op jit(solution)/shard_map/ppermute | solution.py:526
  181.2 9.7 %collective-permute-start.50 = (f32[2,40,256]{2,1,0:T(8,128)S(1)}, f32[2,40,256]{2,1,0:T(8,128)S(1)}, u32[]{:S(2)}, u32[]{:S(2)}) collective-permute-start(f32[2,40,256]{2,1,0:T(8,128)S(1)} %get-tuple-element.173.refs_4_), channel_id=1, source_target_pairs={{0,4},{1,5},{2,6},{3,7},{4,0},{5,1},{6,2},{7,3},{8,12},{9,13},{10,... | collective-permute-start | bytes 245768 | tf_op jit(solution)/shard_map/ppermute | solution.py:526
  183.2 7.8 %collective-permute-start.49 = (f32[2,40,256]{2,1,0:T(8,128)S(1)}, f32[2,40,256]{2,1,0:T(8,128)S(1)}, u32[]{:S(2)}, u32[]{:S(2)}) collective-permute-start(f32[2,40,256]{2,1,0:T(8,128)S(1)} %get-tuple-element.173.refs_4_), channel_id=1, source_target_pairs={{0,2},{1,3},{2,0},{3,1},{4,6},{5,7},{6,4},{7,5},{8,10},{9,11},{10,... | collective-permute-start | bytes 245768 | tf_op jit(solution)/shard_map/ppermute | solution.py:526
  (22 other events, 104.3 us)

commit v3 on v2

--- a/solution.py
+++ b/solution.py
@@ -464,8 +464,25 @@
         self.what, self.layer = what, layer
 
 
-def call(body, shapes, *args, name, scratch=(), flops=2e9, vmem=24, final=False):
+class Order:
+    def __init__(self):
+        self.token = None
+
+
+def call(body, shapes, *args, name, order=None, scratch=(), flops=1.5e10, vmem=24, final=False):
     specs, arrays, held, far_in, far_out, out_specs, out_shapes = [], [], [], [], [], [], []
+    if order is not None:
+        inner, tokens = body, int(order.token is not None)
+        args = args + (order.token,) * tokens
+        used = len(args) - tokens
+        shapes = list(shapes) + [(8, 128)]
+        results = len(shapes) - 1
+
+        def body(*refs):
+            outs = refs[used + tokens :]
+            outs[results][...] = jnp.zeros((8, 128), F32)
+            inner(*refs[:used], *outs[:results], *outs[results + 1 :])
+
     for a in args:
         if isinstance(a, Far):
             far_in.append((len(arrays), a.layer))
@@ -508,7 +525,7 @@
 
     if held:
         held.append(pltpu.SemaphoreType.DMA((copies,)))
-    return pl.pallas_call(
+    values = pl.pallas_call(
         whole,
         out_shape=out_shapes,
         in_specs=specs,
@@ -520,6 +537,10 @@
         ),
         name=name,
     )(*arrays)
+    if order is not None:
+        order.token = values[-1]
+        values = values[:-1]
+    return values
 
 
 def swap(a, bit, count):
@@ -704,7 +725,7 @@
         return self.have[0], self.come[0][0]
 
 
-def step(*works, name):
+def step(*works, name, order=None):
     jobs = [w.job() for w in works]
     outs = [jax.eval_shape(lambda *a, fn=fn: fn(*a), *arrays) for fn, arrays in jobs]
 
@@ -719,7 +740,7 @@
 
     values = call(
         body, [o.shape for out in outs for o in out], *[a for _, arrays in jobs for a in arrays],
-        name=name, flops=1e8, vmem=12,
+        name=name, order=order, flops=1.5e10, vmem=12,
     )
     for w, out in zip(works, outs):
         w.take(values[: len(out)])
@@ -784,48 +805,49 @@
         name="rear1_head_back1",
     )
 
+    order = Order()
+
+    def advance(*works):
+        for w in works:
+            if isinstance(w, Small):
+                step(w, name="add", order=order)
+                w.launch()
+            elif w.phase != "last":
+                step(w, name="chunks", order=order)
+                w.launch()
+
     dm = Small(dm, count)
     first = Chunks(keep, send, a1, count)
     dm.launch()
     first.launch()
-    step(dm, name="add")
+    advance(dm)
     while not dm.last:
-        dm.launch()
-        step(dm, first, name="add_chunks")
-        first.launch()
-    dm.launch()
+        advance(first, dm)
 
     gq1, ds0, dm0, keep, send = call(
         with_count(kernel_d), [(dh, 3 * dh), (n, hm), (dh + 8, hm)] + chunks(2 * a2),
         *p1, *dm.parts(), qkv(1), g_head, d_first, ds1, *far(s1, proj1, nf1, rstd1, lg1, r1, rs1),
         *front_w(1), *far(s0, mix0, des0, n10, rd10, pre0), *rear_w(0), name="back_front1_rear0",
+        order=order,
     )
 
     dm = Small(dm0, count)
     second = Chunks(keep, send, a2, count)
     dm.launch()
     second.launch()
+    advance(first, dm)
     while not dm.last:
-        step(dm, first, second, name="add_chunks")
-        dm.launch()
-        first.launch()
-        second.launch()
+        advance(second, dm, first)
 
     gq0, small1, keep, send = call(
         with_count(kernel_e), [(dh, 3 * dh), (8, hm)] + chunks(a3),
         *p0, *dm.parts(), qkv(0), ds0, *far(s0, proj0, nf0, lg0, r0, rs0), *front_w(0),
-        name="back_front0",
-    )
-    third = Chunks(keep, send, None, count)
+        name="back_front0", order=order,
+    )
+    third = Chunks(keep, send, aligned(width // count) + 8, count)
     third.launch()
-    works = [first, second, third]
-    while True:
-        busy = [w for w in works if w.phase != "last"]
-        if not busy:
-            break
-        step(*busy, name="chunks")
-        for w in busy:
-            w.launch()
+    while any(w.phase != "last" for w in (first, second, third)):
+        advance(second, first, third)
 
     *grads, g_head = call(
         with_count(kernel_f),

time: 200 us -> 169 us (0.84)
  waiting for transfers between devices: 101 us -> 70.1 us
    ppermute x54 -> x56, waiting for transfers between devices: 101 us -> 70.1 us  [swap(): return lax.ppermute(a, 'cell', [(i, i ^ bit) for i in range(count)])]
    ppermute x54 -> x56, starting transfers between devices: 55 us -> 53.4 us  [swap(): return lax.ppermute(a, 'cell', [(i, i ^ bit) for i in range(count)])]
    pallas_call x19 -> x35, Pallas kernels: 42.4 us -> 43 us  [call(): pl.pallas_call(whole, out_shape=out_shapes, in_specs=specs, out_specs=out...]
  transfers between devices with their start and end apart: 54 -> 56, of which waited for: 31 -> 34; matrix products, arithmetic and copies ran while one was open for 0% -> 0% of each run, Pallas kernels for 0% -> 10%
where the time goes in v3:
time: 169 us; the launch traced here: 168 us
  waiting for transfers between devices  70.1 us (41%)
  starting transfers between devices  53.4 us (32%)
  Pallas kernels  43 us (25%)
    ppermute x56, waiting for transfers between devices, swap(): return lax.ppermute(a, 'cell', [(i, i ^ bit) for i in range(count)])  70.1 us
    ppermute x56, starting transfers between devices, swap(): return lax.ppermute(a, 'cell', [(i, i ^ bit) for i in range(count)])  53.4 us
    pallas_call x35, Pallas kernels, call(): pl.pallas_call(whole, out_shape=out_shapes, in_specs=specs, out_specs=out...  43 us
  transfers between devices with their start and end apart: 56, of which 34 were waited for; matrix products, arithmetic and copies ran while one was open for 0% of the time, Pallas kernels for 10%

profile of v3, /device:TPU:0, one launch (start us, length us, event | category | flops | bytes accessed | tf_op | source)
XLA Modules:
  0.0 168.2 jit_solution(4935124878336746765)
XLA Ops:
  1.3 4.6 %front0.1 = (f32[40,512]{1,0:T(8,128)S(1)}, f32[256,512]{1,0:T(8,128)}, f32[256,512]{1,0:T(8,128)}, f32[256,256]{1,0:T(8,128)}, f32[256,1]{1,0:T(8,128)}, /*inde...) custom-call(s32[1]{0:T(128)S(6)} %copy.20.refs_0_, f32[256,256]{1,0:T(8,128)} %refs_3_.3, ...), custom_call_target="tpu_custom_call" | custom-call | flops 15000000512 | bytes 150000000 | tf_op jit(solution)/shard_map/front0/pallas_call | solution.py:528
  7.4 4.0 %collective-permute-start.3 = (f32[40,512]{1,0:T(8,128)S(1)}, f32[40,512]{1,0:T(8,128)S(1)}, u32[]{:S(2)}, u32[]{:S(2)}) collective-permute-start(f32[40,512]{1,0:T(8,128)S(1)} %add.8.refs_0_), channel_id=1, source_target_pairs={{0,6},{1,7},{2,4},{3,5},{4,2},{5,3},{6,0},{7,1},{8,14},{9,15},{10,... | collective-permute-start | bytes 245768 | tf_op jit(solution)/shard_map/ppermute | solution.py:547
  12.0 2.5 %collective-permute-done.3.refs_3_ = f32[40,512]{1,0:T(8,128)S(1)} collective-permute-done((f32[40,512]{1,0:T(8,128)S(1)}, f32[40,512]{1,0:T(8,128)S(1)}, u32[]{:S(2)}, u32[]{:S(2)}) %collective-permute-start.3) | collective-permute-done | bytes 81952 | tf_op jit(solution)/shard_map/ppermute | solution.py:547
  16.3 2.7 %collective-permute-start.4 = (f32[40,512]{1,0:T(8,128)S(1)}, f32[40,512]{1,0:T(8,128)S(1)}, u32[]{:S(2)}, u32[]{:S(2)}) collective-permute-start(f32[40,512]{1,0:T(8,128)S(1)} %add.9.refs_1_.refs_0_), channel_id=1, source_target_pairs={{0,8},{1,9},{2,10},{3,11},{4,12},{5,13},{6,14},{7,15},{8,0},{9,1},... | collective-permute-start | bytes 245768 | tf_op jit(solution)/shard_map/ppermute | solution.py:547
  18.9 2.9 %collective-permute-done.4.refs_2_.refs_1_ = f32[40,512]{1,0:T(8,128)S(1)} collective-permute-done((f32[40,512]{1,0:T(8,128)S(1)}, f32[40,512]{1,0:T(8,128)S(1)}, u32[]{:S(2)}, u32[]{:S(2)}) %collective-permute-start.4) | collective-permute-done | bytes 81952 | tf_op jit(solution)/shard_map/ppermute | solution.py:547
  21.8 8.8 %rear0_front1.1 = (f32[32,512]{1,0:T(8,128)}, f32[256,256]{1,0:T(8,128)}, f32[256,256]{1,0:T(8,128)}, f32[256,1]{1,0:T(8,128)}, f32[256,1024]{1,0:T(8,128)}, /*i...) custom-call(s32[1]{0:T(128)S(6)} %copy.20.refs_0_, ...), custom_call_target="tpu_custom_call" | custom-call | flops 15000000512 | bytes 150000000 | tf_op jit(solution)/shard_map/rear0_front1/pallas_call | solution.py:528
  32.1 2.6 %collective-permute-start.8 = (f32[40,512]{1,0:T(8,128)S(1)}, f32[40,512]{1,0:T(8,128)S(1)}, u32[]{:S(2)}, u32[]{:S(2)}) collective-permute-start(f32[40,512]{1,0:T(8,128)S(1)} %add.10.refs_0_), channel_id=1, source_target_pairs={{0,6},{1,7},{2,4},{3,5},{4,2},{5,3},{6,0},{7,1},{8,14},{9,15},{10,... | collective-permute-start | bytes 245768 | tf_op jit(solution)/shard_map/ppermute | solution.py:547
  36.3 1.8 %collective-permute-done.8.refs_3_ = f32[40,512]{1,0:T(8,128)S(1)} collective-permute-done((f32[40,512]{1,0:T(8,128)S(1)}, f32[40,512]{1,0:T(8,128)S(1)}, u32[]{:S(2)}, u32[]{:S(2)}) %collective-permute-start.8) | collective-permute-done | bytes 81952 | tf_op jit(solution)/shard_map/ppermute | solution.py:547
  38.1 2.4 %collective-permute-done.7.refs_2_ = f32[40,512]{1,0:T(8,128)S(1)} collective-permute-done((f32[40,512]{1,0:T(8,128)S(1)}, f32[40,512]{1,0:T(8,128)S(1)}, u32[]{:S(2)}, u32[]{:S(2)}) %collective-permute-start.7) | collective-permute-done | bytes 81952 | tf_op jit(solution)/shard_map/ppermute | solution.py:547
  40.7 2.0 %collective-permute-start.9 = (f32[40,512]{1,0:T(8,128)S(1)}, f32[40,512]{1,0:T(8,128)S(1)}, u32[]{:S(2)}, u32[]{:S(2)}) collective-permute-start(f32[40,512]{1,0:T(8,128)S(1)} %add.11.refs_1_.refs_0_), channel_id=1, source_target_pairs={{0,8},{1,9},{2,10},{3,11},{4,12},{5,13},{6,14},{7,15},{8,0},{9,1},... | collective-permute-start | bytes 245768 | tf_op jit(solution)/shard_map/ppermute | solution.py:547
  42.8 4.2 %collective-permute-done.9.refs_2_.refs_1_ = f32[40,512]{1,0:T(8,128)S(1)} collective-permute-done((f32[40,512]{1,0:T(8,128)S(1)}, f32[40,512]{1,0:T(8,128)S(1)}, u32[]{:S(2)}, u32[]{:S(2)}) %collective-permute-start.9) | collective-permute-done | bytes 81952 | tf_op jit(solution)/shard_map/ppermute | solution.py:547
  47.0 9.9 %rear1_head_back1.1 = (f32[2,256]{1,0:T(2,128)}, f32[8,256]{1,0:T(8,128)S(1)}, f32[256,256]{1,0:T(8,128)S(1)}, f32[256,512]{1,0:T(8,128)S(1)}, f32[32,512]{1,0:T...) custom-call(s32[1]{0:T(128)S(6)} %copy.20.refs_0_, f32[40,512]{1,0:T(8,128)S(1)} %add.11.refs_1_.refs_0_, ...), custom_call_target="tpu_custom_call" | custom-call | flops 15000000512 | bytes 150000000 | tf_op jit(solution)/shard_map/rear1_head_back1/pallas_call | solution.py:528
  59.1 2.7 %collective-permute-start.15 = (f32[32,512]{1,0:T(8,128)S(1)}, f32[32,512]{1,0:T(8,128)S(1)}, u32[]{:S(2)}, u32[]{:S(2)}) collective-permute-start(f32[32,512]{1,0:T(8,128)S(1)} %get-tuple-element.146.refs_0_), channel_id=1, source_target_pairs={{0,4},{1,5},{2,6},{3,7},{4,0},{5,1},{6,2},{7,3},{8,12},{9,13},{10,... | collective-permute-start | bytes 196616 | tf_op jit(solution)/shard_map/ppermute | solution.py:547
  61.9 2.2 %collective-permute-done.16.refs_3_ = f32[32,512]{1,0:T(8,128)S(1)} collective-permute-done((f32[32,512]{1,0:T(8,128)S(1)}, f32[32,512]{1,0:T(8,128)S(1)}, u32[]{:S(2)}, u32[]{:S(2)}) %collective-permute-start.16) | collective-permute-done | bytes 65568 | tf_op jit(solution)/shard_map/ppermute | solution.py:547
  67.7 2.0 %collective-permute-start.13 = (f32[2,2,72,256]{3,2,1,0:T(8,128)S(1)}, f32[2,2,72,256]{3,2,1,0:T(8,128)S(1)}, u32[]{:S(2)}, u32[]{:S(2)}) collective-permute-start(f32[2,2,72,256]{3,2,1,0:T(8,128)S(1)} %get-tuple-element.145), channel_id=1, source_target_pairs={{0,4},{1,5},{2,6},{3,7},{4,0},{5,1},{6,2},{7,3},{8,12},{9,13},{10,... | collective-permute-start | bytes 884744 | tf_op jit(solution)/shard_map/ppermute | solution.py:547
  71.5 9.9 %back_front1_rear0.1 = (f32[32,96]{1,0:T(8,128)S(1)}, f32[256,512]{1,0:T(8,128)S(1)}, f32[40,512]{1,0:T(8,128)S(1)}, f32[8,176,256]{2,1,0:T(8,128)S(1)}, f32[8,1...) custom-call(f32[40,512]{1,0:T(8,128)S(1)} %add.11.refs_1_.refs_0_, f32[40,512]{1,0:T(8,128)S(1)} %collective-permute-done.9.refs_2_.refs_1_, ...), custom_call_target="tpu_custom_call" | custom-call | flops 15000000512 | bytes 150000000 | tf_op jit(solution)/shard_map/back_front1_rear0/pallas_call | solution.py:528
  82.9 2.2 %collective-permute-start.22 = (f32[40,512]{1,0:T(8,128)S(1)}, f32[40,512]{1,0:T(8,128)S(1)}, u32[]{:S(2)}, u32[]{:S(2)}) collective-permute-start(f32[40,512]{1,0:T(8,128)S(1)} %get-tuple-element.171.refs_0_), channel_id=1, source_target_pairs={{0,4},{1,5},{2,6},{3,7},{4,0},{5,1},{6,2},{7,3},{8,12},{9,13},{10,... | collective-permute-start | bytes 245768 | tf_op jit(solution)/shard_map/ppermute | solution.py:547
  95.3 1.7 %collective-permute-start.27 = (f32[2,2,88,256]{3,2,1,0:T(8,128)S(1)}, f32[2,2,88,256]{3,2,1,0:T(8,128)S(1)}, u32[]{:S(2)}, u32[]{:S(2)}) collective-permute-start(f32[2,2,88,256]{3,2,1,0:T(8,128)S(1)} %get-tuple-element.182), channel_id=1, source_target_pairs={{0,4},{1,5},{2,6},{3,7},{4,0},{5,1},{6,2},{7,3},{8,12},{9,13},{10,... | collective-permute-start | bytes 1081352 | tf_op jit(solution)/shard_map/ppermute | solution.py:547
  97.0 2.7 %collective-permute-done.28.refs_3_ = f32[40,512]{1,0:T(8,128)S(1)} collective-permute-done((f32[40,512]{1,0:T(8,128)S(1)}, f32[40,512]{1,0:T(8,128)S(1)}, u32[]{:S(2)}, u32[]{:S(2)}) %collective-permute-start.28) | collective-permute-done | bytes 81952 | tf_op jit(solution)/shard_map/ppermute | solution.py:547
  99.7 5.0 %back_front0.1 = (f32[32,96]{1,0:T(8,128)S(1)}, f32[8,512]{1,0:T(8,128)S(1)}, f32[8,40,256]{2,1,0:T(8,128)S(1)}, f32[8,40,256]{2,1,0:T(8,128)S(1)}, f32[8,128]{1,0:T(8,128)S(1)}) custom-call(f32[40,512]{1,0:T(8,128)S(1)} %copy-done.1, f32[40,512]{1,0:T(8,128)S(1)} %copy-done.3, f32[40,512]{1,0:T(8,128)S(1)} %get-tuple-element.183.refs_2_, ...), custom_call_target="tpu_custom_call" | custom-call | flops 15000000512 | bytes 150000000 | tf_op jit(solution)/shard_map/back_front0/pallas_call | solution.py:528
  104.8 3.4 %collective-permute-done.27.refs_3_ = f32[2,2,88,256]{3,2,1,0:T(8,128)S(1)} collective-permute-done((f32[2,2,88,256]{3,2,1,0:T(8,128)S(1)}, f32[2,2,88,256]{3,2,1,0:T(8,128)S(1)}, u32[]{:S(2)}, u32[]{:S(2)}) %collective-permute-start.27) | collective-permute-done | bytes 360480 | tf_op jit(solution)/shard_map/ppermute | solution.py:547
  108.4 2.3 %collective-permute-start.30 = (f32[2,88,256]{2,1,0:T(8,128)S(1)}, f32[2,88,256]{2,1,0:T(8,128)S(1)}, u32[]{:S(2)}, u32[]{:S(2)}) collective-permute-start(f32[2,88,256]{2,1,0:T(8,128)S(1)} %get-tuple-element.195), channel_id=1, source_target_pairs={{0,4},{1,5},{2,6},{3,7},{4,0},{5,1},{6,2},{7,3},{8,12},{9,13},{10,... | collective-permute-start | bytes 540680 | tf_op jit(solution)/shard_map/ppermute | solution.py:547
  112.9 5.7 %collective-permute-done.30.refs_1_ = f32[2,88,256]{2,1,0:T(8,128)S(1)} collective-permute-done((f32[2,88,256]{2,1,0:T(8,128)S(1)}, f32[2,88,256]{2,1,0:T(8,128)S(1)}, u32[]{:S(2)}, u32[]{:S(2)}) %collective-permute-start.30) | collective-permute-done | bytes 180256 | tf_op jit(solution)/shard_map/ppermute | solution.py:547
  120.7 2.1 %collective-permute-start.41 = (f32[2,24,256]{2,1,0:T(8,128)S(1)}, f32[2,24,256]{2,1,0:T(8,128)S(1)}, u32[]{:S(2)}, u32[]{:S(2)}) collective-permute-start(f32[2,24,256]{2,1,0:T(8,128)S(1)} %get-tuple-element.218), channel_id=1, source_target_pairs={{0,4},{1,5},{2,6},{3,7},{4,0},{5,1},{6,2},{7,3},{8,12},{9,13},{10,... | collective-permute-start | bytes 147464 | tf_op jit(solution)/shard_map/ppermute | solution.py:547
  124.0 6.5 %collective-permute-done.35.refs_1_ = f32[176,256]{1,0:T(8,128)S(1)} collective-permute-done((f32[176,256]{1,0:T(8,128)S(1)}, f32[176,256]{1,0:T(8,128)S(1)}, u32[]{:S(2)}, u32[]{:S(2)}) %collective-permute-start.35) | collective-permute-done | bytes 180256 | tf_op jit(solution)/shard_map/ppermute | solution.py:547
  130.7 3.0 %collective-permute-start.46 = (f32[40,256]{1,0:T(8,128)S(1)}, f32[40,256]{1,0:T(8,128)S(1)}, u32[]{:S(2)}, u32[]{:S(2)}) collective-permute-start(f32[40,256]{1,0:T(8,128)S(1)} %get-tuple-element.228), channel_id=1, source_target_pairs={{0,8},{1,9},{2,10},{3,11},{4,12},{5,13},{6,14},{7,15},{8,0},{9,1},... | collective-permute-start | bytes 122888 | tf_op jit(solution)/shard_map/ppermute | solution.py:547
  135.3 4.9 %collective-permute-done.40.refs_1_ = f32[176,256]{1,0:T(8,128)S(1)} collective-permute-done((f32[176,256]{1,0:T(8,128)S(1)}, f32[176,256]{1,0:T(8,128)S(1)}, u32[]{:S(2)}, u32[]{:S(2)}) %collective-permute-start.40) | collective-permute-done | bytes 180256 | tf_op jit(solution)/shard_map/ppermute | solution.py:547
  140.8 2.7 %collective-permute-done.39.refs_3_ = f32[2,2,72,256]{3,2,1,0:T(8,128)S(1)} collective-permute-done((f32[2,2,72,256]{3,2,1,0:T(8,128)S(1)}, f32[2,2,72,256]{3,2,1,0:T(8,128)S(1)}, u32[]{:S(2)}, u32[]{:S(2)}) %collective-permute-start.39) | collective-permute-done | bytes 294944 | tf_op jit(solution)/shard_map/ppermute | solution.py:547
  145.2 2.6 %collective-permute-done.44.refs_1_ = f32[2,88,256]{2,1,0:T(8,128)S(1)} collective-permute-done((f32[2,88,256]{2,1,0:T(8,128)S(1)}, f32[2,88,256]{2,1,0:T(8,128)S(1)}, u32[]{:S(2)}, u32[]{:S(2)}) %collective-permute-start.44) | collective-permute-done | bytes 180256 | tf_op jit(solution)/shard_map/ppermute | solution.py:547
  152.1 4.3 %collective-permute-done.47.refs_1_ = f32[2,2,88,256]{3,2,1,0:T(8,128)S(1)} collective-permute-done((f32[2,2,88,256]{3,2,1,0:T(8,128)S(1)}, f32[2,2,88,256]{3,2,1,0:T(8,128)S(1)}, u32[]{:S(2)}, u32[]{:S(2)}) %collective-permute-start.47) | collective-permute-done | bytes 360480 | tf_op jit(solution)/shard_map/ppermute | solution.py:547
  159.2 3.7 %collective-permute-done.54.refs_3_ = f32[2,2,16,256]{3,2,1,0:T(8,128)S(1)} collective-permute-done((f32[2,2,16,256]{3,2,1,0:T(8,128)S(1)}, f32[2,2,16,256]{3,2,1,0:T(8,128)S(1)}, u32[]{:S(2)}, u32[]{:S(2)}) %collective-permute-start.54) | collective-permute-done | bytes 65568 | tf_op jit(solution)/shard_map/ppermute | solution.py:547
  165.2 3.0 %place_gradients.1 = (f32[2,256,512]{2,1,0:T(8,128)}, f32[2,32]{1,0:T(2,128)}, f32[2,32,64]{2,1,0:T(8,128)}, f32[2,32,96]{2,1,0:T(8,128)}, f32[2,256,256]{2,1,0:...) custom-call(f32[8,144,256]{2,1,0:T(8,128)S(1)} %get-tuple-element.224.refs_0_, ...), custom_call_target="tpu_custom_call" | custom-call | flops 15000000512 | bytes 150000000 | tf_op jit(solution)/shard_map/place_gradients/pallas_call | solution.py:528
  (123 shorter events, 45.2 us)
Async XLA Ops:
  7.4 7.1 %collective-permute-start.3 = (f32[40,512]{1,0:T(8,128)S(1)}, f32[40,512]{1,0:T(8,128)S(1)}, u32[]{:S(2)}, u32[]{:S(2)}) collective-permute-start(f32[40,512]{1,0:T(8,128)S(1)} %add.8.refs_0_), channel_id=1, source_target_pairs={{0,6},{1,7},{2,4},{3,5},{4,2},{5,3},{6,0},{7,1},{8,14},{9,15},{10,... | collective-permute-start | bytes 245768 | tf_op jit(solution)/shard_map/ppermute | solution.py:547
  66.8 15.2 %collective-permute-start.12 = (f32[2,2,72,256]{3,2,1,0:T(8,128)S(1)}, f32[2,2,72,256]{3,2,1,0:T(8,128)S(1)}, u32[]{:S(2)}, u32[]{:S(2)}) collective-permute-start(f32[2,2,72,256]{3,2,1,0:T(8,128)S(1)} %get-tuple-element.143), channel_id=1, source_target_pairs={{0,2},{1,3},{2,0},{3,1},{4,6},{5,7},{6,4},{7,5},{8,10},{9,11},{10,... | collective-permute-start | bytes 884744 | tf_op jit(solution)/shard_map/ppermute | solution.py:547
  67.7 14.3 %collective-permute-start.13 = (f32[2,2,72,256]{3,2,1,0:T(8,128)S(1)}, f32[2,2,72,256]{3,2,1,0:T(8,128)S(1)}, u32[]{:S(2)}, u32[]{:S(2)}) collective-permute-start(f32[2,2,72,256]{3,2,1,0:T(8,128)S(1)} %get-tuple-element.145), channel_id=1, source_target_pairs={{0,4},{1,5},{2,6},{3,7},{4,0},{5,1},{6,2},{7,3},{8,12},{9,13},{10,... | collective-permute-start | bytes 884744 | tf_op jit(solution)/shard_map/ppermute | solution.py:547
  82.9 7.2 %collective-permute-start.22 = (f32[40,512]{1,0:T(8,128)S(1)}, f32[40,512]{1,0:T(8,128)S(1)}, u32[]{:S(2)}, u32[]{:S(2)}) collective-permute-start(f32[40,512]{1,0:T(8,128)S(1)} %get-tuple-element.171.refs_0_), channel_id=1, source_target_pairs={{0,4},{1,5},{2,6},{3,7},{4,0},{5,1},{6,2},{7,3},{8,12},{9,13},{10,... | collective-permute-start | bytes 245768 | tf_op jit(solution)/shard_map/ppermute | solution.py:547
  86.4 6.8 %collective-permute-start.19 = (f32[2,72,256]{2,1,0:T(8,128)S(1)}, f32[2,72,256]{2,1,0:T(8,128)S(1)}, u32[]{:S(2)}, u32[]{:S(2)}) collective-permute-start(f32[2,72,256]{2,1,0:T(8,128)S(1)} %get-tuple-element.168), channel_id=1, source_target_pairs={{0,2},{1,3},{2,0},{3,1},{4,6},{5,7},{6,4},{7,5},{8,10},{9,11},{10,... | collective-permute-start | bytes 442376 | tf_op jit(solution)/shard_map/ppermute | solution.py:547
  90.7 9.0 %collective-permute-start.28 = (f32[40,512]{1,0:T(8,128)S(1)}, f32[40,512]{1,0:T(8,128)S(1)}, u32[]{:S(2)}, u32[]{:S(2)}) collective-permute-start(f32[40,512]{1,0:T(8,128)S(1)} %get-tuple-element.183.refs_2_), channel_id=1, source_target_pairs={{0,8},{1,9},{2,10},{3,11},{4,12},{5,13},{6,14},{7,15},{8,0},{9,1},... | collective-permute-start | bytes 245768 | tf_op jit(solution)/shard_map/ppermute | solution.py:547
  93.2 15.1 %collective-permute-start.25 = (f32[144,256]{1,0:T(8,128)S(1)}, f32[144,256]{1,0:T(8,128)S(1)}, u32[]{:S(2)}, u32[]{:S(2)}) collective-permute-start(f32[144,256]{1,0:T(8,128)S(1)} %get-tuple-element.178), channel_id=1, source_target_pairs={{0,8},{1,9},{2,10},{3,11},{4,12},{5,13},{6,14},{7,15},{8,0},{9,1},... | collective-permute-start | bytes 442376 | tf_op jit(solution)/shard_map/ppermute | solution.py:547
  94.3 10.5 %collective-permute-start.26 = (f32[2,2,88,256]{3,2,1,0:T(8,128)S(1)}, f32[2,2,88,256]{3,2,1,0:T(8,128)S(1)}, u32[]{:S(2)}, u32[]{:S(2)}) collective-permute-start(f32[2,2,88,256]{3,2,1,0:T(8,128)S(1)} %get-tuple-element.180), channel_id=1, source_target_pairs={{0,2},{1,3},{2,0},{3,1},{4,6},{5,7},{6,4},{7,5},{8,10},{9,11},{10,... | collective-permute-start | bytes 1081352 | tf_op jit(solution)/shard_map/ppermute | solution.py:547
  95.3 12.9 %collective-permute-start.27 = (f32[2,2,88,256]{3,2,1,0:T(8,128)S(1)}, f32[2,2,88,256]{3,2,1,0:T(8,128)S(1)}, u32[]{:S(2)}, u32[]{:S(2)}) collective-permute-start(f32[2,2,88,256]{3,2,1,0:T(8,128)S(1)} %get-tuple-element.182), channel_id=1, source_target_pairs={{0,4},{1,5},{2,6},{3,7},{4,0},{5,1},{6,2},{7,3},{8,12},{9,13},{10,... | collective-permute-start | bytes 1081352 | tf_op jit(solution)/shard_map/ppermute | solution.py:547
  104.7 7.1 %collective-permute-start.32 = (f32[8,40,256]{2,1,0:T(8,128)S(1)}, f32[8,40,256]{2,1,0:T(8,128)S(1)}, u32[]{:S(2)}, u32[]{:S(2)}) collective-permute-start(f32[8,40,256]{2,1,0:T(8,128)S(1)} %get-tuple-element.199), channel_id=1, source_target_pairs={{0,1},{1,0},{2,3},{3,2},{4,5},{5,4},{6,7},{7,6},{8,9},{9,8},{10,11... | collective-permute-start | bytes 983048 | tf_op jit(solution)/shard_map/ppermute | solution.py:547
  108.3 11.0 %collective-permute-start.29 = (f32[144,256]{1,0:T(8,128)S(1)}, f32[144,256]{1,0:T(8,128)S(1)}, u32[]{:S(2)}, u32[]{:S(2)}) collective-permute-start(f32[144,256]{1,0:T(8,128)S(1)} %get-tuple-element.193.refs_0_), channel_id=1, source_target_pairs={{0,8},{1,9},{2,10},{3,11},{4,12},{5,13},{6,14},{7,15},{8,0},{9,1},... | collective-permute-start | bytes 442376 | tf_op jit(solution)/shard_map/ppermute | solution.py:547
  108.4 10.3 %collective-permute-start.30 = (f32[2,88,256]{2,1,0:T(8,128)S(1)}, f32[2,88,256]{2,1,0:T(8,128)S(1)}, u32[]{:S(2)}, u32[]{:S(2)}) collective-permute-start(f32[2,88,256]{2,1,0:T(8,128)S(1)} %get-tuple-element.195), channel_id=1, source_target_pairs={{0,4},{1,5},{2,6},{3,7},{4,0},{5,1},{6,2},{7,3},{8,12},{9,13},{10,... | collective-permute-start | bytes 540680 | tf_op jit(solution)/shard_map/ppermute | solution.py:547
  110.7 7.9 %collective-permute-start.31 = (f32[2,88,256]{2,1,0:T(8,128)S(1)}, f32[2,88,256]{2,1,0:T(8,128)S(1)}, u32[]{:S(2)}, u32[]{:S(2)}) collective-permute-start(f32[2,88,256]{2,1,0:T(8,128)S(1)} %get-tuple-element.197), channel_id=1, source_target_pairs={{0,2},{1,3},{2,0},{3,1},{4,6},{5,7},{6,4},{7,5},{8,10},{9,11},{10,... | collective-permute-start | bytes 540680 | tf_op jit(solution)/shard_map/ppermute | solution.py:547
  111.9 7.6 %collective-permute-start.37 = (f32[2,2,16,256]{3,2,1,0:T(8,128)S(1)}, f32[2,2,16,256]{3,2,1,0:T(8,128)S(1)}, u32[]{:S(2)}, u32[]{:S(2)}) collective-permute-start(f32[2,2,16,256]{3,2,1,0:T(8,128)S(1)} %get-tuple-element.210), channel_id=1, source_target_pairs={{0,4},{1,5},{2,6},{3,7},{4,0},{5,1},{6,2},{7,3},{8,12},{9,13},{10,... | collective-permute-start | bytes 196616 | tf_op jit(solution)/shard_map/ppermute | solution.py:547
  112.0 7.6 %collective-permute-start.36 = (f32[2,2,24,256]{3,2,1,0:T(8,128)S(1)}, f32[2,2,24,256]{3,2,1,0:T(8,128)S(1)}, u32[]{:S(2)}, u32[]{:S(2)}) collective-permute-start(f32[2,2,24,256]{3,2,1,0:T(8,128)S(1)} %get-tuple-element.208), channel_id=1, source_target_pairs={{0,2},{1,3},{2,0},{3,1},{4,6},{5,7},{6,4},{7,5},{8,10},{9,11},{10,... | collective-permute-start | bytes 294920 | tf_op jit(solution)/shard_map/ppermute | solution.py:547
  118.7 11.8 %collective-permute-start.35 = (f32[176,256]{1,0:T(8,128)S(1)}, f32[176,256]{1,0:T(8,128)S(1)}, u32[]{:S(2)}, u32[]{:S(2)}) collective-permute-start(f32[176,256]{1,0:T(8,128)S(1)} %get-tuple-element.206), channel_id=1, source_target_pairs={{0,8},{1,9},{2,10},{3,11},{4,12},{5,13},{6,14},{7,15},{8,0},{9,1},... | collective-permute-start | bytes 540680 | tf_op jit(solution)/shard_map/ppermute | solution.py:547
  119.6 11.1 %collective-permute-start.42 = (f32[2,16,256]{2,1,0:T(8,128)S(1)}, f32[2,16,256]{2,1,0:T(8,128)S(1)}, u32[]{:S(2)}, u32[]{:S(2)}) collective-permute-start(f32[2,16,256]{2,1,0:T(8,128)S(1)} %get-tuple-element.220), channel_id=1, source_target_pairs={{0,2},{1,3},{2,0},{3,1},{4,6},{5,7},{6,4},{7,5},{8,10},{9,11},{10,... | collective-permute-start | bytes 98312 | tf_op jit(solution)/shard_map/ppermute | solution.py:547
  120.7 10.0 %collective-permute-start.41 = (f32[2,24,256]{2,1,0:T(8,128)S(1)}, f32[2,24,256]{2,1,0:T(8,128)S(1)}, u32[]{:S(2)}, u32[]{:S(2)}) collective-permute-start(f32[2,24,256]{2,1,0:T(8,128)S(1)} %get-tuple-element.218), channel_id=1, source_target_pairs={{0,4},{1,5},{2,6},{3,7},{4,0},{5,1},{6,2},{7,3},{8,12},{9,13},{10,... | collective-permute-start | bytes 147464 | tf_op jit(solution)/shard_map/ppermute | solution.py:547
  122.8 7.8 %collective-permute-start.33 = (f32[2,72,256]{2,1,0:T(8,128)S(1)}, f32[2,72,256]{2,1,0:T(8,128)S(1)}, u32[]{:S(2)}, u32[]{:S(2)}) collective-permute-start(f32[2,72,256]{2,1,0:T(8,128)S(1)} %get-tuple-element.203.refs_0_), channel_id=1, source_target_pairs={{0,4},{1,5},{2,6},{3,7},{4,0},{5,1},{6,2},{7,3},{8,12},{9,13},{10,... | collective-permute-start | bytes 442376 | tf_op jit(solution)/shard_map/ppermute | solution.py:547
  122.8 7.8 %collective-permute-start.34 = (f32[2,72,256]{2,1,0:T(8,128)S(1)}, f32[2,72,256]{2,1,0:T(8,128)S(1)}, u32[]{:S(2)}, u32[]{:S(2)}) collective-permute-start(f32[2,72,256]{2,1,0:T(8,128)S(1)} %get-tuple-element.204.refs_2_), channel_id=1, source_target_pairs={{0,2},{1,3},{2,0},{3,1},{4,6},{5,7},{6,4},{7,5},{8,10},{9,11},{10,... | collective-permute-start | bytes 442376 | tf_op jit(solution)/shard_map/ppermute | solution.py:547
  130.5 9.7 %collective-permute-start.40 = (f32[176,256]{1,0:T(8,128)S(1)}, f32[176,256]{1,0:T(8,128)S(1)}, u32[]{:S(2)}, u32[]{:S(2)}) collective-permute-start(f32[176,256]{1,0:T(8,128)S(1)} %get-tuple-element.216.refs_0_), channel_id=1, source_target_pairs={{0,8},{1,9},{2,10},{3,11},{4,12},{5,13},{6,14},{7,15},{8,0},{9,1},... | collective-permute-start | bytes 540680 | tf_op jit(solution)/shard_map/ppermute | solution.py:547
  130.7 12.9 %collective-permute-start.46 = (f32[40,256]{1,0:T(8,128)S(1)}, f32[40,256]{1,0:T(8,128)S(1)}, u32[]{:S(2)}, u32[]{:S(2)}) collective-permute-start(f32[40,256]{1,0:T(8,128)S(1)} %get-tuple-element.228), channel_id=1, source_target_pairs={{0,8},{1,9},{2,10},{3,11},{4,12},{5,13},{6,14},{7,15},{8,0},{9,1},... | collective-permute-start | bytes 122888 | tf_op jit(solution)/shard_map/ppermute | solution.py:547
  133.7 7.1 %collective-permute-start.38 = (f32[2,2,72,256]{3,2,1,0:T(8,128)S(1)}, f32[2,2,72,256]{3,2,1,0:T(8,128)S(1)}, u32[]{:S(2)}, u32[]{:S(2)}) collective-permute-start(f32[2,2,72,256]{3,2,1,0:T(8,128)S(1)} %get-tuple-element.214.refs_0_), channel_id=1, source_target_pairs={{0,2},{1,3},{2,0},{3,1},{4,6},{5,7},{6,4},{7,5},{8,10},{9,11},{10,... | collective-permute-start | bytes 884744 | tf_op jit(solution)/shard_map/ppermute | solution.py:547
  134.3 9.2 %collective-permute-start.39 = (f32[2,2,72,256]{3,2,1,0:T(8,128)S(1)}, f32[2,2,72,256]{3,2,1,0:T(8,128)S(1)}, u32[]{:S(2)}, u32[]{:S(2)}) collective-permute-start(f32[2,2,72,256]{3,2,1,0:T(8,128)S(1)} %get-tuple-element.215.refs_2_), channel_id=1, source_target_pairs={{0,4},{1,5},{2,6},{3,7},{4,0},{5,1},{6,2},{7,3},{8,12},{9,13},{10,... | collective-permute-start | bytes 884744 | tf_op jit(solution)/shard_map/ppermute | solution.py:547
  140.3 7.6 %collective-permute-start.44 = (f32[2,88,256]{2,1,0:T(8,128)S(1)}, f32[2,88,256]{2,1,0:T(8,128)S(1)}, u32[]{:S(2)}, u32[]{:S(2)}) collective-permute-start(f32[2,88,256]{2,1,0:T(8,128)S(1)} %get-tuple-element.225.refs_0_), channel_id=1, source_target_pairs={{0,4},{1,5},{2,6},{3,7},{4,0},{5,1},{6,2},{7,3},{8,12},{9,13},{10,... | collective-permute-start | bytes 540680 | tf_op jit(solution)/shard_map/ppermute | solution.py:547
  140.3 7.5 %collective-permute-start.45 = (f32[2,88,256]{2,1,0:T(8,128)S(1)}, f32[2,88,256]{2,1,0:T(8,128)S(1)}, u32[]{:S(2)}, u32[]{:S(2)}) collective-permute-start(f32[2,88,256]{2,1,0:T(8,128)S(1)} %get-tuple-element.226.refs_2_), channel_id=1, source_target_pairs={{0,2},{1,3},{2,0},{3,1},{4,6},{5,7},{6,4},{7,5},{8,10},{9,11},{10,... | collective-permute-start | bytes 540680 | tf_op jit(solution)/shard_map/ppermute | solution.py:547
  147.9 8.5 %collective-permute-start.47 = (f32[2,2,88,256]{3,2,1,0:T(8,128)S(1)}, f32[2,2,88,256]{3,2,1,0:T(8,128)S(1)}, u32[]{:S(2)}, u32[]{:S(2)}) collective-permute-start(f32[2,2,88,256]{3,2,1,0:T(8,128)S(1)} %get-tuple-element.231.refs_0_), channel_id=1, source_target_pairs={{0,2},{1,3},{2,0},{3,1},{4,6},{5,7},{6,4},{7,5},{8,10},{9,11},{10,... | collective-permute-start | bytes 1081352 | tf_op jit(solution)/shard_map/ppermute | solution.py:547
  149.2 8.1 %collective-permute-start.48 = (f32[2,2,88,256]{3,2,1,0:T(8,128)S(1)}, f32[2,2,88,256]{3,2,1,0:T(8,128)S(1)}, u32[]{:S(2)}, u32[]{:S(2)}) collective-permute-start(f32[2,2,88,256]{3,2,1,0:T(8,128)S(1)} %get-tuple-element.232.refs_2_), channel_id=1, source_target_pairs={{0,4},{1,5},{2,6},{3,7},{4,0},{5,1},{6,2},{7,3},{8,12},{9,13},{10,... | collective-permute-start | bytes 1081352 | tf_op jit(solution)/shard_map/ppermute | solution.py:547
  149.2 8.2 %collective-permute-start.52 = (f32[2,16,256]{2,1,0:T(8,128)S(1)}, f32[2,16,256]{2,1,0:T(8,128)S(1)}, u32[]{:S(2)}, u32[]{:S(2)}) collective-permute-start(f32[2,16,256]{2,1,0:T(8,128)S(1)} %get-tuple-element.238.refs_2_), channel_id=1, source_target_pairs={{0,2},{1,3},{2,0},{3,1},{4,6},{5,7},{6,4},{7,5},{8,10},{9,11},{10,... | collective-permute-start | bytes 98312 | tf_op jit(solution)/shard_map/ppermute | solution.py:547
  150.7 7.0 %collective-permute-start.51 = (f32[2,24,256]{2,1,0:T(8,128)S(1)}, f32[2,24,256]{2,1,0:T(8,128)S(1)}, u32[]{:S(2)}, u32[]{:S(2)}) collective-permute-start(f32[2,24,256]{2,1,0:T(8,128)S(1)} %get-tuple-element.237.refs_0_), channel_id=1, source_target_pairs={{0,4},{1,5},{2,6},{3,7},{4,0},{5,1},{6,2},{7,3},{8,12},{9,13},{10,... | collective-permute-start | bytes 147464 | tf_op jit(solution)/shard_map/ppermute | solution.py:547
  158.7 6.5 %collective-permute-start.43 = (f32[8,144,256]{2,1,0:T(8,128)S(1)}, f32[8,144,256]{2,1,0:T(8,128)S(1)}, u32[]{:S(2)}, u32[]{:S(2)}) collective-permute-start(f32[8,144,256]{2,1,0:T(8,128)S(1)} %get-tuple-element.224.refs_0_), channel_id=1, source_target_pairs={{0,1},{1,0},{2,3},{3,2},{4,5},{5,4},{6,7},{7,6},{8,9},{9,8},{10,11... | collective-permute-start | bytes 3538952 | tf_op jit(solution)/shard_map/ppermute | solution.py:547
  158.7 6.5 %collective-permute-start.50 = (f32[8,176,256]{2,1,0:T(8,128)S(1)}, f32[8,176,256]{2,1,0:T(8,128)S(1)}, u32[]{:S(2)}, u32[]{:S(2)}) collective-permute-start(f32[8,176,256]{2,1,0:T(8,128)S(1)} %get-tuple-element.236.refs_2_), channel_id=1, source_target_pairs={{0,1},{1,0},{2,3},{3,2},{4,5},{5,4},{6,7},{7,6},{8,9},{9,8},{10,11... | collective-permute-start | bytes 4325384 | tf_op jit(solution)/shard_map/ppermute | solution.py:547
  (28 other events, 145.2 us)

commit v4 on v3

--- a/solution.py
+++ b/solution.py
@@ -340,11 +340,11 @@
 def kernel_d(
     count, pa, pb, ma, mb, w_qkv, g_head, d_first, ds, s, proj, nf, rstd, logits, r, rs,
     w_in, w_temp, w_slice, s0, mixed0, des0, n10, rstd10, pre0, w_out0, w_up0, w_down0,
-    g_qkv, ds0, d_mixed0, keep, send,
+    g_qkv, ds0, d_mixed0, g_in1, keep, send,
 ):
     width = nf.shape[1]
     g_qkv[...], d_numer, d_denom = middle_back(pa[...] + pb[...], w_qkv[...], ma[...] + mb[...])
-    d_proj, g_in, g_temp, g_slice = front_back(
+    d_proj, g_in1[...], g_temp, g_slice = front_back(
         ds[...], d_numer, d_denom, s[...], proj[...], nf[...], logits[...], r[...], rs[...],
         w_in[...], w_temp[1:2], w_slice[...],
     )
@@ -356,14 +356,11 @@
     left, right = pack_small(g_temp, g_slice, g_head[:2], None)
     d_mixed0[...] = jnp.concatenate([d_mixed, jnp.concatenate([left, right], axis=1)], axis=0)
     halves = [g_out[: width // 2], g_out[width // 2 :]]
-    ins = slabs(g_in)
-    scatter(
-        count, [[g_down], [halves[0]], [ins[0]], slabs(g_up), [halves[1]], [ins[1]]], keep, send
-    )
+    scatter(count, [[g_down], [halves[0]], slabs(g_up), [halves[1]]], keep, send)
 
 
 def kernel_e(
-    count, pa, pb, ma, mb, w_qkv, ds, s, proj, nf, logits, r, rs, w_in, w_temp, w_slice,
+    count, pa, pb, ma, mb, g_in1, w_qkv, ds, s, proj, nf, logits, r, rs, w_in, w_temp, w_slice,
     g_qkv, small, keep, send,
 ):
     dh = w_qkv.shape[0]
@@ -376,10 +373,9 @@
     )
     left, right = pack_small(g_temp, g_slice, jnp.zeros((2, g_temp.shape[1]), F32), None)
     rest = jnp.zeros((8 * count - 16, g_temp.shape[1]), F32)
-    ins = slabs(g_in)
-    scatter(
-        count, [[ins[0]], [jnp.concatenate([left, right, rest], axis=0)], [ins[1]]], keep, send
-    )
+    ins, ins1 = slabs(g_in), slabs(g_in1[...])
+    small = jnp.concatenate([left, right, rest], axis=0)
+    scatter(count, [[ins[0]], [small], [ins1[0]], [ins[1]], [ins1[1]]], keep, send)
 
 
 def kernel_f(
@@ -403,8 +399,9 @@
         return width, [into(g_in, l, part * width)]
 
     gather(count, own1, oth1, [down(1), out(1, 0), up(1), out(1, 1)])
-    gather(count, own2, oth2, [down(0), out(0, 0), ins(1, 0), up(0), out(0, 1), ins(1, 1)])
-    gather(count, own3, oth3, [ins(0, 0), (8 * count, [rows_of(small0)]), ins(0, 1)])
+    gather(count, own2, oth2, [down(0), out(0, 0), up(0), out(0, 1)])
+    small = (8 * count, [rows_of(small0)])
+    gather(count, own3, oth3, [ins(0, 0), small, ins(1, 0), ins(0, 1), ins(1, 1)])
     g_qkv[0] = gq0[...]
     g_qkv[1] = gq1[...]
     for l, (left, right) in enumerate(
@@ -784,8 +781,9 @@
     rear_shapes = [Far(s) for s in [(dh, hm), (n, width), (n, width), (n, 1), (n, ff)]]
     run = lambda *rows: sum(aligned(r // count) for r in rows)
     a1 = run(ff, width // 2)
-    a2 = run(ff, width // 2, width)
+    a2 = run(ff, width // 2)
     a3 = run(width, 8 * count, width)
+    b3 = run(width, width)
     chunks = lambda rows: [(count // 2, rows, 256)] * 2
     with_count = lambda body: partial(body, count)
 
@@ -824,8 +822,9 @@
     while not dm.last:
         advance(first, dm)
 
-    gq1, ds0, dm0, keep, send = call(
-        with_count(kernel_d), [(dh, 3 * dh), (n, hm), (dh + 8, hm)] + chunks(2 * a2),
+    gq1, ds0, dm0, g_in1, keep, send = call(
+        with_count(kernel_d),
+        [(dh, 3 * dh), (n, hm), (dh + 8, hm), (width, 2 * width)] + chunks(2 * a2),
         *p1, *dm.parts(), qkv(1), g_head, d_first, ds1, *far(s1, proj1, nf1, rstd1, lg1, r1, rs1),
         *front_w(1), *far(s0, mix0, des0, n10, rd10, pre0), *rear_w(0), name="back_front1_rear0",
         order=order,
@@ -840,11 +839,11 @@
         advance(second, dm, first)
 
     gq0, small1, keep, send = call(
-        with_count(kernel_e), [(dh, 3 * dh), (8, hm)] + chunks(a3),
-        *p0, *dm.parts(), qkv(0), ds0, *far(s0, proj0, nf0, lg0, r0, rs0), *front_w(0),
+        with_count(kernel_e), [(dh, 3 * dh), (8, hm)] + chunks(a3 + b3),
+        *p0, *dm.parts(), g_in1, qkv(0), ds0, *far(s0, proj0, nf0, lg0, r0, rs0), *front_w(0),
         name="back_front0", order=order,
     )
-    third = Chunks(keep, send, aligned(width // count) + 8, count)
+    third = Chunks(keep, send, a3, count)
     third.launch()
     while any(w.phase != "last" for w in (first, second, third)):
         advance(second, first, third)

time: 169 us -> 164 us (0.970)
  waiting for transfers between devices: 70.1 us -> 63.2 us
  starting transfers between devices: 53.4 us -> 55.4 us
    ppermute x56, waiting for transfers between devices: 70.1 us -> 63.2 us  [swap(): return lax.ppermute(a, 'cell', [(i, i ^ bit) for i in range(count)])]
    ppermute x56, starting transfers between devices: 53.4 us -> 55.4 us  [swap(): return lax.ppermute(a, 'cell', [(i, i ^ bit) for i in range(count)])]
  transfers between devices with their start and end apart: 56 -> 56, of which waited for: 34 -> 33; matrix products, arithmetic and copies ran while one was open for 0% -> 0% of each run, Pallas kernels for 10% -> 10%
where the time goes in v4:
time: 164 us; the launch traced here: 163 us
  waiting for transfers between devices  63.2 us (39%)
  starting transfers between devices  55.4 us (34%)
  Pallas kernels  43 us (26%)
    ppermute x56, waiting for transfers between devices, swap(): return lax.ppermute(a, 'cell', [(i, i ^ bit) for i in range(count)])  63.2 us
    ppermute x56, starting transfers between devices, swap(): return lax.ppermute(a, 'cell', [(i, i ^ bit) for i in range(count)])  55.4 us
    pallas_call x35, Pallas kernels, call(): pl.pallas_call(whole, out_shape=out_shapes, in_specs=specs, out_specs=out...  43 us
  transfers between devices with their start and end apart: 56, of which 33 were waited for; matrix products, arithmetic and copies ran while one was open for 0% of the time, Pallas kernels for 10%

profile of v4, /device:TPU:0, one launch (start us, length us, event | category | flops | bytes accessed | tf_op | source)
XLA Modules:
  0.0 163.3 jit_solution(5645227337693708896)
XLA Ops:
  1.3 4.6 %front0.1 = (f32[40,512]{1,0:T(8,128)S(1)}, f32[256,512]{1,0:T(8,128)}, f32[256,512]{1,0:T(8,128)}, f32[256,256]{1,0:T(8,128)}, f32[256,1]{1,0:T(8,128)}, /*inde...) custom-call(s32[1]{0:T(128)S(6)} %copy.20.refs_0_, f32[256,256]{1,0:T(8,128)} %refs_3_.3, ...), custom_call_target="tpu_custom_call" | custom-call | flops 15000000512 | bytes 150000000 | tf_op jit(solution)/shard_map/front0/pallas_call | solution.py:525
  7.4 4.0 %collective-permute-start.3 = (f32[40,512]{1,0:T(8,128)S(1)}, f32[40,512]{1,0:T(8,128)S(1)}, u32[]{:S(2)}, u32[]{:S(2)}) collective-permute-start(f32[40,512]{1,0:T(8,128)S(1)} %add.8.refs_0_), channel_id=1, source_target_pairs={{0,6},{1,7},{2,4},{3,5},{4,2},{5,3},{6,0},{7,1},{8,14},{9,15},{10,... | collective-permute-start | bytes 245768 | tf_op jit(solution)/shard_map/ppermute | solution.py:544
  12.0 2.5 %collective-permute-done.3.refs_3_ = f32[40,512]{1,0:T(8,128)S(1)} collective-permute-done((f32[40,512]{1,0:T(8,128)S(1)}, f32[40,512]{1,0:T(8,128)S(1)}, u32[]{:S(2)}, u32[]{:S(2)}) %collective-permute-start.3) | collective-permute-done | bytes 81952 | tf_op jit(solution)/shard_map/ppermute | solution.py:544
  16.3 2.7 %collective-permute-start.4 = (f32[40,512]{1,0:T(8,128)S(1)}, f32[40,512]{1,0:T(8,128)S(1)}, u32[]{:S(2)}, u32[]{:S(2)}) collective-permute-start(f32[40,512]{1,0:T(8,128)S(1)} %add.9.refs_1_.refs_0_), channel_id=1, source_target_pairs={{0,8},{1,9},{2,10},{3,11},{4,12},{5,13},{6,14},{7,15},{8,0},{9,1},... | collective-permute-start | bytes 245768 | tf_op jit(solution)/shard_map/ppermute | solution.py:544
  18.9 2.9 %collective-permute-done.4.refs_2_.refs_1_ = f32[40,512]{1,0:T(8,128)S(1)} collective-permute-done((f32[40,512]{1,0:T(8,128)S(1)}, f32[40,512]{1,0:T(8,128)S(1)}, u32[]{:S(2)}, u32[]{:S(2)}) %collective-permute-start.4) | collective-permute-done | bytes 81952 | tf_op jit(solution)/shard_map/ppermute | solution.py:544
  21.8 8.8 %rear0_front1.1 = (f32[32,512]{1,0:T(8,128)}, f32[256,256]{1,0:T(8,128)}, f32[256,256]{1,0:T(8,128)}, f32[256,1]{1,0:T(8,128)}, f32[256,1024]{1,0:T(8,128)}, /*i...) custom-call(s32[1]{0:T(128)S(6)} %copy.20.refs_0_, ...), custom_call_target="tpu_custom_call" | custom-call | flops 15000000512 | bytes 150000000 | tf_op jit(solution)/shard_map/rear0_front1/pallas_call | solution.py:525
  32.1 2.6 %collective-permute-start.8 = (f32[40,512]{1,0:T(8,128)S(1)}, f32[40,512]{1,0:T(8,128)S(1)}, u32[]{:S(2)}, u32[]{:S(2)}) collective-permute-start(f32[40,512]{1,0:T(8,128)S(1)} %add.10.refs_0_), channel_id=1, source_target_pairs={{0,6},{1,7},{2,4},{3,5},{4,2},{5,3},{6,0},{7,1},{8,14},{9,15},{10,... | collective-permute-start | bytes 245768 | tf_op jit(solution)/shard_map/ppermute | solution.py:544
  36.3 1.8 %collective-permute-done.8.refs_3_ = f32[40,512]{1,0:T(8,128)S(1)} collective-permute-done((f32[40,512]{1,0:T(8,128)S(1)}, f32[40,512]{1,0:T(8,128)S(1)}, u32[]{:S(2)}, u32[]{:S(2)}) %collective-permute-start.8) | collective-permute-done | bytes 81952 | tf_op jit(solution)/shard_map/ppermute | solution.py:544
  38.1 2.4 %collective-permute-done.7.refs_2_ = f32[40,512]{1,0:T(8,128)S(1)} collective-permute-done((f32[40,512]{1,0:T(8,128)S(1)}, f32[40,512]{1,0:T(8,128)S(1)}, u32[]{:S(2)}, u32[]{:S(2)}) %collective-permute-start.7) | collective-permute-done | bytes 81952 | tf_op jit(solution)/shard_map/ppermute | solution.py:544
  40.7 2.0 %collective-permute-start.9 = (f32[40,512]{1,0:T(8,128)S(1)}, f32[40,512]{1,0:T(8,128)S(1)}, u32[]{:S(2)}, u32[]{:S(2)}) collective-permute-start(f32[40,512]{1,0:T(8,128)S(1)} %add.11.refs_1_.refs_0_), channel_id=1, source_target_pairs={{0,8},{1,9},{2,10},{3,11},{4,12},{5,13},{6,14},{7,15},{8,0},{9,1},... | collective-permute-start | bytes 245768 | tf_op jit(solution)/shard_map/ppermute | solution.py:544
  42.8 4.2 %collective-permute-done.9.refs_2_.refs_1_ = f32[40,512]{1,0:T(8,128)S(1)} collective-permute-done((f32[40,512]{1,0:T(8,128)S(1)}, f32[40,512]{1,0:T(8,128)S(1)}, u32[]{:S(2)}, u32[]{:S(2)}) %collective-permute-start.9) | collective-permute-done | bytes 81952 | tf_op jit(solution)/shard_map/ppermute | solution.py:544
  47.0 9.9 %rear1_head_back1.1 = (f32[2,256]{1,0:T(2,128)}, f32[8,256]{1,0:T(8,128)S(1)}, f32[256,256]{1,0:T(8,128)S(1)}, f32[256,512]{1,0:T(8,128)S(1)}, f32[32,512]{1,0:T...) custom-call(s32[1]{0:T(128)S(6)} %copy.20.refs_0_, f32[40,512]{1,0:T(8,128)S(1)} %add.11.refs_1_.refs_0_, ...), custom_call_target="tpu_custom_call" | custom-call | flops 15000000512 | bytes 150000000 | tf_op jit(solution)/shard_map/rear1_head_back1/pallas_call | solution.py:525
  59.1 2.7 %collective-permute-start.15 = (f32[32,512]{1,0:T(8,128)S(1)}, f32[32,512]{1,0:T(8,128)S(1)}, u32[]{:S(2)}, u32[]{:S(2)}) collective-permute-start(f32[32,512]{1,0:T(8,128)S(1)} %get-tuple-element.147.refs_0_), channel_id=1, source_target_pairs={{0,4},{1,5},{2,6},{3,7},{4,0},{5,1},{6,2},{7,3},{8,12},{9,13},{10,... | collective-permute-start | bytes 196616 | tf_op jit(solution)/shard_map/ppermute | solution.py:544
  61.9 2.2 %collective-permute-done.16.refs_3_ = f32[32,512]{1,0:T(8,128)S(1)} collective-permute-done((f32[32,512]{1,0:T(8,128)S(1)}, f32[32,512]{1,0:T(8,128)S(1)}, u32[]{:S(2)}, u32[]{:S(2)}) %collective-permute-start.16) | collective-permute-done | bytes 65568 | tf_op jit(solution)/shard_map/ppermute | solution.py:544
  67.7 2.0 %collective-permute-start.13 = (f32[2,2,72,256]{3,2,1,0:T(8,128)S(1)}, f32[2,2,72,256]{3,2,1,0:T(8,128)S(1)}, u32[]{:S(2)}, u32[]{:S(2)}) collective-permute-start(f32[2,2,72,256]{3,2,1,0:T(8,128)S(1)} %get-tuple-element.146), channel_id=1, source_target_pairs={{0,4},{1,5},{2,6},{3,7},{4,0},{5,1},{6,2},{7,3},{8,12},{9,13},{10,... | collective-permute-start | bytes 884744 | tf_op jit(solution)/shard_map/ppermute | solution.py:544
  69.8 1.7 %collective-permute-done.17.refs_3_ = f32[32,512]{1,0:T(8,128)S(1)} collective-permute-done((f32[32,512]{1,0:T(8,128)S(1)}, f32[32,512]{1,0:T(8,128)S(1)}, u32[]{:S(2)}, u32[]{:S(2)}) %collective-permute-start.17) | collective-permute-done | bytes 65568 | tf_op jit(solution)/shard_map/ppermute | solution.py:544
  71.5 9.9 %back_front1_rear0.1 = (f32[32,96]{1,0:T(8,128)S(1)}, f32[256,512]{1,0:T(8,128)S(1)}, f32[40,512]{1,0:T(8,128)S(1)}, f32[256,512]{1,0:T(8,128)S(1)}, f32[8,144,2...) custom-call(f32[40,512]{1,0:T(8,128)S(1)} %add.11.refs_1_.refs_0_, ...), custom_call_target="tpu_custom_call" | custom-call | flops 15000000512 | bytes 150000000 | tf_op jit(solution)/shard_map/back_front1_rear0/pallas_call | solution.py:525
  82.9 2.2 %collective-permute-start.22 = (f32[40,512]{1,0:T(8,128)S(1)}, f32[40,512]{1,0:T(8,128)S(1)}, u32[]{:S(2)}, u32[]{:S(2)}) collective-permute-start(f32[40,512]{1,0:T(8,128)S(1)} %get-tuple-element.172.refs_0_), channel_id=1, source_target_pairs={{0,4},{1,5},{2,6},{3,7},{4,0},{5,1},{6,2},{7,3},{8,12},{9,13},{10,... | collective-permute-start | bytes 245768 | tf_op jit(solution)/shard_map/ppermute | solution.py:544
  95.3 1.7 %collective-permute-start.27 = (f32[2,2,72,256]{3,2,1,0:T(8,128)S(1)}, f32[2,2,72,256]{3,2,1,0:T(8,128)S(1)}, u32[]{:S(2)}, u32[]{:S(2)}) collective-permute-start(f32[2,2,72,256]{3,2,1,0:T(8,128)S(1)} %get-tuple-element.183), channel_id=1, source_target_pairs={{0,4},{1,5},{2,6},{3,7},{4,0},{5,1},{6,2},{7,3},{8,12},{9,13},{10,... | collective-permute-start | bytes 884744 | tf_op jit(solution)/shard_map/ppermute | solution.py:544
  97.0 2.7 %collective-permute-done.28.refs_3_ = f32[40,512]{1,0:T(8,128)S(1)} collective-permute-done((f32[40,512]{1,0:T(8,128)S(1)}, f32[40,512]{1,0:T(8,128)S(1)}, u32[]{:S(2)}, u32[]{:S(2)}) %collective-permute-start.28) | collective-permute-done | bytes 81952 | tf_op jit(solution)/shard_map/ppermute | solution.py:544
  99.7 5.0 %back_front0.1 = (f32[32,96]{1,0:T(8,128)S(1)}, f32[8,512]{1,0:T(8,128)S(1)}, f32[8,72,256]{2,1,0:T(8,128)S(1)}, f32[8,72,256]{2,1,0:T(8,128)S(1)}, f32[8,128]{1,0:T(8,128)S(1)}) custom-call(f32[40,512]{1,0:T(8,128)S(1)} %copy-done.1, f32[40,512]{1,0:T(8,128)S(1)} %copy-done.3, f32[40,512]{1,0:T(8,128)S(1)} %get-tuple-element.184.refs_2_, ...), custom_call_target="tpu_custom_call" | custom-call | flops 15000000512 | bytes 150000000 | tf_op jit(solution)/shard_map/back_front0/pallas_call | solution.py:525
  104.8 1.9 %collective-permute-done.27.refs_3_ = f32[2,2,72,256]{3,2,1,0:T(8,128)S(1)} collective-permute-done((f32[2,2,72,256]{3,2,1,0:T(8,128)S(1)}, f32[2,2,72,256]{3,2,1,0:T(8,128)S(1)}, u32[]{:S(2)}, u32[]{:S(2)}) %collective-permute-start.27) | collective-permute-done | bytes 294944 | tf_op jit(solution)/shard_map/ppermute | solution.py:544
  107.0 2.3 %collective-permute-start.30 = (f32[2,72,256]{2,1,0:T(8,128)S(1)}, f32[2,72,256]{2,1,0:T(8,128)S(1)}, u32[]{:S(2)}, u32[]{:S(2)}) collective-permute-start(f32[2,72,256]{2,1,0:T(8,128)S(1)} %get-tuple-element.197), channel_id=1, source_target_pairs={{0,4},{1,5},{2,6},{3,7},{4,0},{5,1},{6,2},{7,3},{8,12},{9,13},{10,... | collective-permute-start | bytes 442376 | tf_op jit(solution)/shard_map/ppermute | solution.py:544
  111.5 5.3 %collective-permute-done.30.refs_1_ = f32[2,72,256]{2,1,0:T(8,128)S(1)} collective-permute-done((f32[2,72,256]{2,1,0:T(8,128)S(1)}, f32[2,72,256]{2,1,0:T(8,128)S(1)}, u32[]{:S(2)}, u32[]{:S(2)}) %collective-permute-start.30) | collective-permute-done | bytes 147488 | tf_op jit(solution)/shard_map/ppermute | solution.py:544
  118.3 2.4 %collective-permute-start.35 = (f32[144,256]{1,0:T(8,128)S(1)}, f32[144,256]{1,0:T(8,128)S(1)}, u32[]{:S(2)}, u32[]{:S(2)}) collective-permute-start(f32[144,256]{1,0:T(8,128)S(1)} %get-tuple-element.208), channel_id=1, source_target_pairs={{0,8},{1,9},{2,10},{3,11},{4,12},{5,13},{6,14},{7,15},{8,0},{9,1},... | collective-permute-start | bytes 442376 | tf_op jit(solution)/shard_map/ppermute | solution.py:544
  121.7 5.1 %collective-permute-done.35.refs_1_ = f32[144,256]{1,0:T(8,128)S(1)} collective-permute-done((f32[144,256]{1,0:T(8,128)S(1)}, f32[144,256]{1,0:T(8,128)S(1)}, u32[]{:S(2)}, u32[]{:S(2)}) %collective-permute-start.35) | collective-permute-done | bytes 147488 | tf_op jit(solution)/shard_map/ppermute | solution.py:544
  131.1 4.0 %collective-permute-done.40.refs_1_ = f32[144,256]{1,0:T(8,128)S(1)} collective-permute-done((f32[144,256]{1,0:T(8,128)S(1)}, f32[144,256]{1,0:T(8,128)S(1)}, u32[]{:S(2)}, u32[]{:S(2)}) %collective-permute-start.40) | collective-permute-done | bytes 147488 | tf_op jit(solution)/shard_map/ppermute | solution.py:544
  136.3 3.7 %collective-permute-done.39.refs_3_ = f32[2,2,72,256]{3,2,1,0:T(8,128)S(1)} collective-permute-done((f32[2,2,72,256]{3,2,1,0:T(8,128)S(1)}, f32[2,2,72,256]{3,2,1,0:T(8,128)S(1)}, u32[]{:S(2)}, u32[]{:S(2)}) %collective-permute-start.39) | collective-permute-done | bytes 294944 | tf_op jit(solution)/shard_map/ppermute | solution.py:544
  148.9 1.8 %collective-permute-done.48.refs_3_ = f32[2,2,72,256]{3,2,1,0:T(8,128)S(1)} collective-permute-done((f32[2,2,72,256]{3,2,1,0:T(8,128)S(1)}, f32[2,2,72,256]{3,2,1,0:T(8,128)S(1)}, u32[]{:S(2)}, u32[]{:S(2)}) %collective-permute-start.48) | collective-permute-done | bytes 294944 | tf_op jit(solution)/shard_map/ppermute | solution.py:544
  154.3 3.4 %collective-permute-done.54.refs_3_ = f32[2,2,32,256]{3,2,1,0:T(8,128)S(1)} collective-permute-done((f32[2,2,32,256]{3,2,1,0:T(8,128)S(1)}, f32[2,2,32,256]{3,2,1,0:T(8,128)S(1)}, u32[]{:S(2)}, u32[]{:S(2)}) %collective-permute-start.54) | collective-permute-done | bytes 131104 | tf_op jit(solution)/shard_map/ppermute | solution.py:544
  158.3 2.0 %collective-permute-done.55.refs_5_ = f32[8,72,256]{2,1,0:T(8,128)S(1)} collective-permute-done((f32[8,72,256]{2,1,0:T(8,128)S(1)}, f32[8,72,256]{2,1,0:T(8,128)S(1)}, u32[]{:S(2)}, u32[]{:S(2)}) %collective-permute-start.55) | collective-permute-done | bytes 589856 | tf_op jit(solution)/shard_map/ppermute | solution.py:544
  160.3 3.0 %place_gradients.1 = (f32[2,256,512]{2,1,0:T(8,128)}, f32[2,32]{1,0:T(2,128)}, f32[2,32,64]{2,1,0:T(8,128)}, f32[2,32,96]{2,1,0:T(8,128)}, f32[2,256,256]{2,1,0:...) custom-call(f32[8,144,256]{2,1,0:T(8,128)S(1)} %get-tuple-element.226.refs_0_, ...), custom_call_target="tpu_custom_call" | custom-call | flops 15000000512 | bytes 150000000 | tf_op jit(solution)/shard_map/place_gradients/pallas_call | solution.py:525
  (123 shorter events, 47.9 us)
Async XLA Ops:
  7.4 7.1 %collective-permute-start.3 = (f32[40,512]{1,0:T(8,128)S(1)}, f32[40,512]{1,0:T(8,128)S(1)}, u32[]{:S(2)}, u32[]{:S(2)}) collective-permute-start(f32[40,512]{1,0:T(8,128)S(1)} %add.8.refs_0_), channel_id=1, source_target_pairs={{0,6},{1,7},{2,4},{3,5},{4,2},{5,3},{6,0},{7,1},{8,14},{9,15},{10,... | collective-permute-start | bytes 245768 | tf_op jit(solution)/shard_map/ppermute | solution.py:544
  40.7 6.3 %collective-permute-start.9 = (f32[40,512]{1,0:T(8,128)S(1)}, f32[40,512]{1,0:T(8,128)S(1)}, u32[]{:S(2)}, u32[]{:S(2)}) collective-permute-start(f32[40,512]{1,0:T(8,128)S(1)} %add.11.refs_1_.refs_0_), channel_id=1, source_target_pairs={{0,8},{1,9},{2,10},{3,11},{4,12},{5,13},{6,14},{7,15},{8,0},{9,1},... | collective-permute-start | bytes 245768 | tf_op jit(solution)/shard_map/ppermute | solution.py:544
  66.8 15.2 %collective-permute-start.12 = (f32[2,2,72,256]{3,2,1,0:T(8,128)S(1)}, f32[2,2,72,256]{3,2,1,0:T(8,128)S(1)}, u32[]{:S(2)}, u32[]{:S(2)}) collective-permute-start(f32[2,2,72,256]{3,2,1,0:T(8,128)S(1)} %get-tuple-element.144), channel_id=1, source_target_pairs={{0,2},{1,3},{2,0},{3,1},{4,6},{5,7},{6,4},{7,5},{8,10},{9,11},{10,... | collective-permute-start | bytes 884744 | tf_op jit(solution)/shard_map/ppermute | solution.py:544
  67.7 14.2 %collective-permute-start.13 = (f32[2,2,72,256]{3,2,1,0:T(8,128)S(1)}, f32[2,2,72,256]{3,2,1,0:T(8,128)S(1)}, u32[]{:S(2)}, u32[]{:S(2)}) collective-permute-start(f32[2,2,72,256]{3,2,1,0:T(8,128)S(1)} %get-tuple-element.146), channel_id=1, source_target_pairs={{0,4},{1,5},{2,6},{3,7},{4,0},{5,1},{6,2},{7,3},{8,12},{9,13},{10,... | collective-permute-start | bytes 884744 | tf_op jit(solution)/shard_map/ppermute | solution.py:544
  82.8 6.3 %collective-permute-start.23 = (f32[40,512]{1,0:T(8,128)S(1)}, f32[40,512]{1,0:T(8,128)S(1)}, u32[]{:S(2)}, u32[]{:S(2)}) collective-permute-start(f32[40,512]{1,0:T(8,128)S(1)} %get-tuple-element.172.refs_0_), channel_id=1, source_target_pairs={{0,6},{1,7},{2,4},{3,5},{4,2},{5,3},{6,0},{7,1},{8,14},{9,15},{10,... | collective-permute-start | bytes 245768 | tf_op jit(solution)/shard_map/ppermute | solution.py:544
  82.9 7.2 %collective-permute-start.22 = (f32[40,512]{1,0:T(8,128)S(1)}, f32[40,512]{1,0:T(8,128)S(1)}, u32[]{:S(2)}, u32[]{:S(2)}) collective-permute-start(f32[40,512]{1,0:T(8,128)S(1)} %get-tuple-element.172.refs_0_), channel_id=1, source_target_pairs={{0,4},{1,5},{2,6},{3,7},{4,0},{5,1},{6,2},{7,3},{8,12},{9,13},{10,... | collective-permute-start | bytes 245768 | tf_op jit(solution)/shard_map/ppermute | solution.py:544
  86.3 6.2 %collective-permute-start.18 = (f32[2,72,256]{2,1,0:T(8,128)S(1)}, f32[2,72,256]{2,1,0:T(8,128)S(1)}, u32[]{:S(2)}, u32[]{:S(2)}) collective-permute-start(f32[2,72,256]{2,1,0:T(8,128)S(1)} %get-tuple-element.167), channel_id=1, source_target_pairs={{0,4},{1,5},{2,6},{3,7},{4,0},{5,1},{6,2},{7,3},{8,12},{9,13},{10,... | collective-permute-start | bytes 442376 | tf_op jit(solution)/shard_map/ppermute | solution.py:544
  86.3 6.8 %collective-permute-start.19 = (f32[2,72,256]{2,1,0:T(8,128)S(1)}, f32[2,72,256]{2,1,0:T(8,128)S(1)}, u32[]{:S(2)}, u32[]{:S(2)}) collective-permute-start(f32[2,72,256]{2,1,0:T(8,128)S(1)} %get-tuple-element.169), channel_id=1, source_target_pairs={{0,2},{1,3},{2,0},{3,1},{4,6},{5,7},{6,4},{7,5},{8,10},{9,11},{10,... | collective-permute-start | bytes 442376 | tf_op jit(solution)/shard_map/ppermute | solution.py:544
  90.7 9.0 %collective-permute-start.28 = (f32[40,512]{1,0:T(8,128)S(1)}, f32[40,512]{1,0:T(8,128)S(1)}, u32[]{:S(2)}, u32[]{:S(2)}) collective-permute-start(f32[40,512]{1,0:T(8,128)S(1)} %get-tuple-element.184.refs_2_), channel_id=1, source_target_pairs={{0,8},{1,9},{2,10},{3,11},{4,12},{5,13},{6,14},{7,15},{8,0},{9,1},... | collective-permute-start | bytes 245768 | tf_op jit(solution)/shard_map/ppermute | solution.py:544
  93.2 13.7 %collective-permute-start.25 = (f32[144,256]{1,0:T(8,128)S(1)}, f32[144,256]{1,0:T(8,128)S(1)}, u32[]{:S(2)}, u32[]{:S(2)}) collective-permute-start(f32[144,256]{1,0:T(8,128)S(1)} %get-tuple-element.179), channel_id=1, source_target_pairs={{0,8},{1,9},{2,10},{3,11},{4,12},{5,13},{6,14},{7,15},{8,0},{9,1},... | collective-permute-start | bytes 442376 | tf_op jit(solution)/shard_map/ppermute | solution.py:544
  94.3 10.5 %collective-permute-start.26 = (f32[2,2,72,256]{3,2,1,0:T(8,128)S(1)}, f32[2,2,72,256]{3,2,1,0:T(8,128)S(1)}, u32[]{:S(2)}, u32[]{:S(2)}) collective-permute-start(f32[2,2,72,256]{3,2,1,0:T(8,128)S(1)} %get-tuple-element.181), channel_id=1, source_target_pairs={{0,2},{1,3},{2,0},{3,1},{4,6},{5,7},{6,4},{7,5},{8,10},{9,11},{10,... | collective-permute-start | bytes 884744 | tf_op jit(solution)/shard_map/ppermute | solution.py:544
  95.3 11.5 %collective-permute-start.27 = (f32[2,2,72,256]{3,2,1,0:T(8,128)S(1)}, f32[2,2,72,256]{3,2,1,0:T(8,128)S(1)}, u32[]{:S(2)}, u32[]{:S(2)}) collective-permute-start(f32[2,2,72,256]{3,2,1,0:T(8,128)S(1)} %get-tuple-element.183), channel_id=1, source_target_pairs={{0,4},{1,5},{2,6},{3,7},{4,0},{5,1},{6,2},{7,3},{8,12},{9,13},{10,... | collective-permute-start | bytes 884744 | tf_op jit(solution)/shard_map/ppermute | solution.py:544
  106.9 10.0 %collective-permute-start.29 = (f32[144,256]{1,0:T(8,128)S(1)}, f32[144,256]{1,0:T(8,128)S(1)}, u32[]{:S(2)}, u32[]{:S(2)}) collective-permute-start(f32[144,256]{1,0:T(8,128)S(1)} %get-tuple-element.195.refs_0_), channel_id=1, source_target_pairs={{0,8},{1,9},{2,10},{3,11},{4,12},{5,13},{6,14},{7,15},{8,0},{9,1},... | collective-permute-start | bytes 442376 | tf_op jit(solution)/shard_map/ppermute | solution.py:544
  107.0 9.9 %collective-permute-start.30 = (f32[2,72,256]{2,1,0:T(8,128)S(1)}, f32[2,72,256]{2,1,0:T(8,128)S(1)}, u32[]{:S(2)}, u32[]{:S(2)}) collective-permute-start(f32[2,72,256]{2,1,0:T(8,128)S(1)} %get-tuple-element.197), channel_id=1, source_target_pairs={{0,4},{1,5},{2,6},{3,7},{4,0},{5,1},{6,2},{7,3},{8,12},{9,13},{10,... | collective-permute-start | bytes 442376 | tf_op jit(solution)/shard_map/ppermute | solution.py:544
  109.3 7.6 %collective-permute-start.31 = (f32[2,72,256]{2,1,0:T(8,128)S(1)}, f32[2,72,256]{2,1,0:T(8,128)S(1)}, u32[]{:S(2)}, u32[]{:S(2)}) collective-permute-start(f32[2,72,256]{2,1,0:T(8,128)S(1)} %get-tuple-element.199), channel_id=1, source_target_pairs={{0,2},{1,3},{2,0},{3,1},{4,6},{5,7},{6,4},{7,5},{8,10},{9,11},{10,... | collective-permute-start | bytes 442376 | tf_op jit(solution)/shard_map/ppermute | solution.py:544
  110.5 10.2 %collective-permute-start.37 = (f32[2,2,32,256]{3,2,1,0:T(8,128)S(1)}, f32[2,2,32,256]{3,2,1,0:T(8,128)S(1)}, u32[]{:S(2)}, u32[]{:S(2)}) collective-permute-start(f32[2,2,32,256]{3,2,1,0:T(8,128)S(1)} %get-tuple-element.212), channel_id=1, source_target_pairs={{0,4},{1,5},{2,6},{3,7},{4,0},{5,1},{6,2},{7,3},{8,12},{9,13},{10,... | collective-permute-start | bytes 393224 | tf_op jit(solution)/shard_map/ppermute | solution.py:544
  110.6 10.1 %collective-permute-start.36 = (f32[2,2,40,256]{3,2,1,0:T(8,128)S(1)}, f32[2,2,40,256]{3,2,1,0:T(8,128)S(1)}, u32[]{:S(2)}, u32[]{:S(2)}) collective-permute-start(f32[2,2,40,256]{3,2,1,0:T(8,128)S(1)} %get-tuple-element.210), channel_id=1, source_target_pairs={{0,2},{1,3},{2,0},{3,1},{4,6},{5,7},{6,4},{7,5},{8,10},{9,11},{10,... | collective-permute-start | bytes 491528 | tf_op jit(solution)/shard_map/ppermute | solution.py:544
  116.9 10.3 %collective-permute-start.33 = (f32[2,72,256]{2,1,0:T(8,128)S(1)}, f32[2,72,256]{2,1,0:T(8,128)S(1)}, u32[]{:S(2)}, u32[]{:S(2)}) collective-permute-start(f32[2,72,256]{2,1,0:T(8,128)S(1)} %get-tuple-element.205.refs_0_), channel_id=1, source_target_pairs={{0,4},{1,5},{2,6},{3,7},{4,0},{5,1},{6,2},{7,3},{8,12},{9,13},{10,... | collective-permute-start | bytes 442376 | tf_op jit(solution)/shard_map/ppermute | solution.py:544
  117.0 10.3 %collective-permute-start.34 = (f32[2,72,256]{2,1,0:T(8,128)S(1)}, f32[2,72,256]{2,1,0:T(8,128)S(1)}, u32[]{:S(2)}, u32[]{:S(2)}) collective-permute-start(f32[2,72,256]{2,1,0:T(8,128)S(1)} %get-tuple-element.206.refs_2_), channel_id=1, source_target_pairs={{0,2},{1,3},{2,0},{3,1},{4,6},{5,7},{6,4},{7,5},{8,10},{9,11},{10,... | collective-permute-start | bytes 442376 | tf_op jit(solution)/shard_map/ppermute | solution.py:544
  118.3 8.5 %collective-permute-start.35 = (f32[144,256]{1,0:T(8,128)S(1)}, f32[144,256]{1,0:T(8,128)S(1)}, u32[]{:S(2)}, u32[]{:S(2)}) collective-permute-start(f32[144,256]{1,0:T(8,128)S(1)} %get-tuple-element.208), channel_id=1, source_target_pairs={{0,8},{1,9},{2,10},{3,11},{4,12},{5,13},{6,14},{7,15},{8,0},{9,1},... | collective-permute-start | bytes 442376 | tf_op jit(solution)/shard_map/ppermute | solution.py:544
  120.8 8.8 %collective-permute-start.42 = (f32[2,32,256]{2,1,0:T(8,128)S(1)}, f32[2,32,256]{2,1,0:T(8,128)S(1)}, u32[]{:S(2)}, u32[]{:S(2)}) collective-permute-start(f32[2,32,256]{2,1,0:T(8,128)S(1)} %get-tuple-element.222), channel_id=1, source_target_pairs={{0,2},{1,3},{2,0},{3,1},{4,6},{5,7},{6,4},{7,5},{8,10},{9,11},{10,... | collective-permute-start | bytes 196616 | tf_op jit(solution)/shard_map/ppermute | solution.py:544
  121.5 8.1 %collective-permute-start.41 = (f32[2,40,256]{2,1,0:T(8,128)S(1)}, f32[2,40,256]{2,1,0:T(8,128)S(1)}, u32[]{:S(2)}, u32[]{:S(2)}) collective-permute-start(f32[2,40,256]{2,1,0:T(8,128)S(1)} %get-tuple-element.220), channel_id=1, source_target_pairs={{0,4},{1,5},{2,6},{3,7},{4,0},{5,1},{6,2},{7,3},{8,12},{9,13},{10,... | collective-permute-start | bytes 245768 | tf_op jit(solution)/shard_map/ppermute | solution.py:544
  126.8 8.3 %collective-permute-start.40 = (f32[144,256]{1,0:T(8,128)S(1)}, f32[144,256]{1,0:T(8,128)S(1)}, u32[]{:S(2)}, u32[]{:S(2)}) collective-permute-start(f32[144,256]{1,0:T(8,128)S(1)} %get-tuple-element.218.refs_0_), channel_id=1, source_target_pairs={{0,8},{1,9},{2,10},{3,11},{4,12},{5,13},{6,14},{7,15},{8,0},{9,1},... | collective-permute-start | bytes 442376 | tf_op jit(solution)/shard_map/ppermute | solution.py:544
  127.3 9.0 %collective-permute-start.38 = (f32[2,2,72,256]{3,2,1,0:T(8,128)S(1)}, f32[2,2,72,256]{3,2,1,0:T(8,128)S(1)}, u32[]{:S(2)}, u32[]{:S(2)}) collective-permute-start(f32[2,2,72,256]{3,2,1,0:T(8,128)S(1)} %get-tuple-element.216.refs_0_), channel_id=1, source_target_pairs={{0,2},{1,3},{2,0},{3,1},{4,6},{5,7},{6,4},{7,5},{8,10},{9,11},{10,... | collective-permute-start | bytes 884744 | tf_op jit(solution)/shard_map/ppermute | solution.py:544
  127.9 12.1 %collective-permute-start.39 = (f32[2,2,72,256]{3,2,1,0:T(8,128)S(1)}, f32[2,2,72,256]{3,2,1,0:T(8,128)S(1)}, u32[]{:S(2)}, u32[]{:S(2)}) collective-permute-start(f32[2,2,72,256]{3,2,1,0:T(8,128)S(1)} %get-tuple-element.217.refs_2_), channel_id=1, source_target_pairs={{0,4},{1,5},{2,6},{3,7},{4,0},{5,1},{6,2},{7,3},{8,12},{9,13},{10,... | collective-permute-start | bytes 884744 | tf_op jit(solution)/shard_map/ppermute | solution.py:544
  129.6 10.5 %collective-permute-start.46 = (f32[72,256]{1,0:T(8,128)S(1)}, f32[72,256]{1,0:T(8,128)S(1)}, u32[]{:S(2)}, u32[]{:S(2)}) collective-permute-start(f32[72,256]{1,0:T(8,128)S(1)} %get-tuple-element.230), channel_id=1, source_target_pairs={{0,8},{1,9},{2,10},{3,11},{4,12},{5,13},{6,14},{7,15},{8,0},{9,1},... | collective-permute-start | bytes 221192 | tf_op jit(solution)/shard_map/ppermute | solution.py:544
  135.2 6.5 %collective-permute-start.44 = (f32[2,72,256]{2,1,0:T(8,128)S(1)}, f32[2,72,256]{2,1,0:T(8,128)S(1)}, u32[]{:S(2)}, u32[]{:S(2)}) collective-permute-start(f32[2,72,256]{2,1,0:T(8,128)S(1)} %get-tuple-element.227.refs_0_), channel_id=1, source_target_pairs={{0,4},{1,5},{2,6},{3,7},{4,0},{5,1},{6,2},{7,3},{8,12},{9,13},{10,... | collective-permute-start | bytes 442376 | tf_op jit(solution)/shard_map/ppermute | solution.py:544
  135.2 6.4 %collective-permute-start.45 = (f32[2,72,256]{2,1,0:T(8,128)S(1)}, f32[2,72,256]{2,1,0:T(8,128)S(1)}, u32[]{:S(2)}, u32[]{:S(2)}) collective-permute-start(f32[2,72,256]{2,1,0:T(8,128)S(1)} %get-tuple-element.228.refs_2_), channel_id=1, source_target_pairs={{0,2},{1,3},{2,0},{3,1},{4,6},{5,7},{6,4},{7,5},{8,10},{9,11},{10,... | collective-permute-start | bytes 442376 | tf_op jit(solution)/shard_map/ppermute | solution.py:544
  141.7 7.2 %collective-permute-start.47 = (f32[2,2,72,256]{3,2,1,0:T(8,128)S(1)}, f32[2,2,72,256]{3,2,1,0:T(8,128)S(1)}, u32[]{:S(2)}, u32[]{:S(2)}) collective-permute-start(f32[2,2,72,256]{3,2,1,0:T(8,128)S(1)} %get-tuple-element.233.refs_0_), channel_id=1, source_target_pairs={{0,2},{1,3},{2,0},{3,1},{4,6},{5,7},{6,4},{7,5},{8,10},{9,11},{10,... | collective-permute-start | bytes 884744 | tf_op jit(solution)/shard_map/ppermute | solution.py:544
  142.8 7.8 %collective-permute-start.48 = (f32[2,2,72,256]{3,2,1,0:T(8,128)S(1)}, f32[2,2,72,256]{3,2,1,0:T(8,128)S(1)}, u32[]{:S(2)}, u32[]{:S(2)}) collective-permute-start(f32[2,2,72,256]{3,2,1,0:T(8,128)S(1)} %get-tuple-element.234.refs_2_), channel_id=1, source_target_pairs={{0,4},{1,5},{2,6},{3,7},{4,0},{5,1},{6,2},{7,3},{8,12},{9,13},{10,... | collective-permute-start | bytes 884744 | tf_op jit(solution)/shard_map/ppermute | solution.py:544
  153.8 6.6 %collective-permute-start.43 = (f32[8,144,256]{2,1,0:T(8,128)S(1)}, f32[8,144,256]{2,1,0:T(8,128)S(1)}, u32[]{:S(2)}, u32[]{:S(2)}) collective-permute-start(f32[8,144,256]{2,1,0:T(8,128)S(1)} %get-tuple-element.226.refs_0_), channel_id=1, source_target_pairs={{0,1},{1,0},{2,3},{3,2},{4,5},{5,4},{6,7},{7,6},{8,9},{9,8},{10,11... | collective-permute-start | bytes 3538952 | tf_op jit(solution)/shard_map/ppermute | solution.py:544
  153.8 6.6 %collective-permute-start.50 = (f32[8,144,256]{2,1,0:T(8,128)S(1)}, f32[8,144,256]{2,1,0:T(8,128)S(1)}, u32[]{:S(2)}, u32[]{:S(2)}) collective-permute-start(f32[8,144,256]{2,1,0:T(8,128)S(1)} %get-tuple-element.238.refs_2_), channel_id=1, source_target_pairs={{0,1},{1,0},{2,3},{3,2},{4,5},{5,4},{6,7},{7,6},{8,9},{9,8},{10,11... | collective-permute-start | bytes 3538952 | tf_op jit(solution)/shard_map/ppermute | solution.py:544
  (28 other events, 143.9 us)
